TPU v7x, 256 devices: a whole 4x4x8 slice. The times are simulated.
256 devices in a mesh: pair: 32 (over x, y, core), virt: 8 (over z).
Axes of the slice: x: 4, y: 4, z: 8, core: 2. Of those that a mesh axis runs over, the one named last changes fastest.
Arguments:
- amps: float32 [8, 2048, 2048], P(None, 'pair', 'virt'), may hold values from -6 to 6
- ints: float32 [8, 2048, 2048], P(None, 'pair', 'virt'), may hold values from -0.125 to 0.125
- panel_of: int32 [32], replicated, may hold values from 0 to 31, each once
- e_occ: float32 [8], replicated, may hold values from -2 to -0.5
- e_vir: float32 [2048], replicated, may hold values from 0.2 to 3
Outputs:
- cycle_update: float32 [8, 8, 2048, 2048], P('virt', None, 'pair')
Inputs may be any that keep to these rules, and one draw needn't show every extreme that they name: panel_of holds each of 0 to 31 once.
All inputs are finite; a program needn't handle non-finite values.
Results may differ from a plain program's by a relative error of at most 0.00007.
Values sent between devices are 32-bit elements; how exact they have to be, the bound alone decides.
No kernel may reach another device: no remote copies, remote signals or barrier semaphores. Data moves between devices by JAX's collectives and lax.ppermute only.
A program may use at most 192 MiB of HBM per device.

v0:
```python
import functools

import jax
import jax.numpy as jnp
from jax import lax
from jax.experimental import pallas as pl
from jax.experimental.pallas import tpu as pltpu
from jax.sharding import Mesh, PartitionSpec as P

SIDE = 4
CORES = 2
DEPTH = 8
HALVES = 2
BLOCK = 256
NT = (((1,), (1,)), ((), ()))
SMEM = pl.BlockSpec(memory_space=pltpu.SMEM)
ANY = pl.BlockSpec(memory_space=pl.ANY)
VMEM = pl.BlockSpec(memory_space=pltpu.VMEM)
LIMIT = pltpu.CompilerParams(vmem_limit_bytes=60 * 2**20)
COSTS = [pl.CostEstimate(flops=f * 10**9, transcendentals=0, bytes_accessed=20_000_000) for f in (40, 2, 40)]
ROUTES = [
    [((1, 0), (1, 0)), ((-1, 0), (-1, 0)), ((0, 1), (0, 1)), ((0, -1), (0, -1)), ((1, 1), (1, 0)), ((-1, -1), (-1, 0)), ((-1, 1), (0, 1))],
    [((1, -1), (0, -1)), ((2, 0), (1, 0)), ((0, 2), (0, 1)), ((2, 1), (-1, 0)), ((1, 2), (0, -1)), ((2, -1), (1, 0)), ((-1, 2), (0, -1)), ((2, 2), (0, 1))],
]
PIECES = [(0, (0,)), (0, (1,)), (1, (0, 1))]


def wrap(x, y):
    return x % SIDE, y % SIDE


def split(x):
    high = x.astype(jnp.bfloat16)
    return high, (x - high.astype(jnp.float32)).astype(jnp.bfloat16)


def product_kernel(dims, places, *refs):
    occ, part, panel, width, parts, chips = dims
    ints_hbm, amps_hbm = refs[:parts], refs[parts : parts + chips]
    own_all, other_all, whole = refs[parts + chips : parts + chips + 3]
    ints, amps, i_hi, i_lo, a_hi, a_lo, out, int_sem, amp_sem, out_sem = refs[parts + chips + 3 :]
    loads = [pltpu.make_async_copy(amps_hbm[g], amps.at[g], amp_sem.at[g]) for g in range(chips)]
    int_loads = [
        pltpu.make_async_copy(ints_hbm[h].at[s], ints.at[h, s], int_sem.at[h, s])
        for h in range(parts)
        for s in range(CORES * DEPTH)
    ]
    for copy in loads + int_loads:
        copy.start()
    for g in range(chips):
        loads[g].wait()
        rows = slice(g * panel, (g + 1) * panel)
        for s in range(DEPTH):
            cols = slice(s * width, (s + 1) * width)
            a_hi[rows, cols], a_lo[rows, cols] = split(amps[g, s])
    height = occ * part
    dot = functools.partial(lax.dot_general, dimension_numbers=NT, preferred_element_type=jnp.float32)
    for h in range(parts):
        for c in range(CORES):
            for s in range(DEPTH):
                int_loads[(h * CORES + c) * DEPTH + s].wait()
                cols = slice(s * width, (s + 1) * width)
                i_hi[:, cols], i_lo[:, cols] = split(ints[h, c * DEPTH + s].reshape(height, width))
            for m in range(0, height, BLOCK):
                at = slice(m, m + BLOCK)
                sums = dot(i_hi[at], a_lo[...]) + dot(i_lo[at], a_hi[...]) + dot(i_hi[at], a_hi[...])
                at = slice(c * occ + m // part, c * occ + (m + BLOCK) // part)
                out[at, h * part : (h + 1) * part, :] = sums.reshape(BLOCK // part, part, chips * panel)
    core = places[3]
    copies = [
        pltpu.make_async_copy(out, whole, out_sem.at[0]),
        pltpu.make_async_copy(out.at[pl.ds(core * occ, occ)], own_all, out_sem.at[1]),
        pltpu.make_async_copy(out.at[pl.ds((1 - core) * occ, occ)], other_all, out_sem.at[2]),
    ]
    for copy in copies:
        copy.start()
    for copy in copies:
        copy.wait()


def finish_kernel(dims, pieces, slots, places, panel_of, e_occ, e_b, e_vir, *refs):
    occ, panel, virtuals = dims
    out_hbm, slot_of, dir_v, mir_v, out_v, in_sem, out_sem = refs[3 * len(pieces) :]
    v, x, y, core = places[0], places[1], places[2], places[3]
    loads = []
    for j in range(occ):
        mine = []
        for n, (first, size, rows, height) in enumerate(pieces):
            own, other, mirror = refs[3 * n : 3 * n + 3]
            for e in range(CORES):
                at = (j, pl.ds(rows, height), pl.ds(e * virtuals // 2 + first, size))
                mine.append(((other if e else own).at[j], dir_v.at[at]))
                mine.append((mirror.at[lax.rem(core + e, CORES) * occ + j], mir_v.at[at]))
        loads.append([pltpu.make_async_copy(a, b, in_sem.at[j, n]) for n, (a, b) in enumerate(mine)])
        for copy in loads[j]:
            copy.start()
    for s, ((dx, dy), e) in enumerate(slots):
        chip = lax.rem(x + dx, SIDE) * SIDE + lax.rem(y + dy, SIDE)
        slot_of[panel_of[chip * CORES + lax.rem(core + e, CORES)]] = s
    lanes = 2 * panel
    lane = lax.broadcasted_iota(jnp.int32, (panel, lanes), 1)
    for j in range(occ):
        for copy in loads[j]:
            copy.wait()
        base = (e_occ[v] + e_occ[j]) - e_b[...]
        for t in range(virtuals // lanes):
            sides = []
            for h in range(2):
                s = slot_of[2 * t + h]
                cols = pl.ds(pl.multiple_of((s // 2) * lanes, lanes), lanes)
                diff = dir_v[j, :, cols] - mir_v[j, :, cols]
                sides.append(pltpu.roll(diff, lax.rem(s + h, 2) * panel, 1))
            cols = slice(t * lanes, (t + 1) * lanes)
            out_v[j, :, cols] = jnp.where(lane < panel, sides[0], sides[1]) / (base - e_vir[:, cols])
        pltpu.make_async_copy(out_v.at[j], out_hbm.at[j], out_sem.at[j]).start()
    for j in range(occ):
        pltpu.make_async_copy(out_v.at[j], out_hbm.at[j], out_sem.at[j]).wait()


def body(amps, ints, panel_of, e_occ, e_vir):
    occ, panel, width = amps.shape
    virtuals = e_vir.shape[0]
    f32, bf16 = jnp.float32, jnp.bfloat16
    index = [lax.axis_index(name).astype(jnp.int32) for name in ("virt", "x", "y", "core")]
    places = jnp.stack(index)
    part = panel // HALVES

    def move(data, dx, dy):
        name, step = ("x", dx) if dx else ("y", dy)
        return lax.ppermute(data, name, [(n, (n - step) % SIDE) for n in range(SIDE)])

    int_all = [lax.all_gather(ints[:, h * part : (h + 1) * part], ("core", "virt"), axis=0) for h in range(HALVES)]
    held = {(0, 0): lax.all_to_all(amps, "virt", split_axis=0, concat_axis=0, tiled=True)}
    sets, starts = [], []
    for k, routes in enumerate(ROUTES):
        chips = [(0, 0)] if k == 0 else []
        for to, (dx, dy) in routes:
            held[wrap(*to)] = move(held[wrap(to[0] - dx, to[1] - dy)], dx, dy)
            chips.append(wrap(*to))
        starts.append(sum(map(len, sets)) * panel)
        sets.append(chips)

    arrays, places_of, mirror = [], [], []
    for n, (k, halves) in enumerate(PIECES):
        chips, parts = sets[k], len(halves)
        size, tall = len(chips) * panel, parts * part
        every = jax.ShapeDtypeStruct((occ, tall, size), f32)
        both = jax.ShapeDtypeStruct((CORES * occ, tall, size), f32)
        own_all, other_all, whole = pl.pallas_call(
            functools.partial(product_kernel, (occ, part, panel, width, parts, len(chips))),
            out_shape=[every, every, both],
            in_specs=[SMEM] + [ANY] * (parts + len(chips)),
            out_specs=[ANY] * 3,
            scratch_shapes=[
                pltpu.VMEM((parts, CORES * DEPTH, occ, part, width), f32),
                pltpu.VMEM((len(chips), DEPTH, panel, width), f32),
                pltpu.VMEM((occ * part, DEPTH * width), bf16),
                pltpu.VMEM((occ * part, DEPTH * width), bf16),
                pltpu.VMEM((size, DEPTH * width), bf16),
                pltpu.VMEM((size, DEPTH * width), bf16),
                pltpu.VMEM(both.shape, f32),
                pltpu.SemaphoreType.DMA((parts, CORES * DEPTH)),
                pltpu.SemaphoreType.DMA((len(chips),)),
                pltpu.SemaphoreType.DMA((3,)),
            ],
            compiler_params=LIMIT,
            cost_estimate=COSTS[n],
            name=f"product_{n}",
        )(places, *[int_all[h] for h in halves], *[held[chip] for chip in chips])
        if mirror:
            whole, mirror[-1] = lax.optimization_barrier((whole, mirror[-1]))
        mirror.append(lax.all_to_all(whole, ("core", "virt"), split_axis=0, concat_axis=0, tiled=True))
        arrays.append([own_all, lax.ppermute(other_all, "core", [(0, 1), (1, 0)])])
        places_of.append((starts[k], size, halves[0] * part, tall))
        if n + 1 < len(PIECES):
            after = [own_all] + mirror[:-1]
            tied = lax.optimization_barrier(int_all + after)
            int_all = list(tied[:HALVES])
    for pair_of, back in zip(arrays, mirror):
        pair_of.append(back)

    slots = [(chip, e) for e in range(CORES) for chips in sets for chip in chips]
    pair = (index[1] * SIDE + index[2]) * CORES + index[3]
    e_b = lax.dynamic_slice(e_vir, (pair * panel,), (panel,)).reshape(panel, 1)
    out = pl.pallas_call(
        functools.partial(finish_kernel, (occ, panel, virtuals), places_of, slots),
        out_shape=jax.ShapeDtypeStruct((occ, panel, virtuals), f32),
        in_specs=[SMEM, SMEM, SMEM, VMEM, VMEM] + [ANY] * (3 * len(PIECES)),
        out_specs=ANY,
        scratch_shapes=[
            pltpu.SMEM((virtuals // panel,), jnp.int32),
            pltpu.VMEM((occ, panel, virtuals), f32),
            pltpu.VMEM((occ, panel, virtuals), f32),
            pltpu.VMEM((occ, panel, virtuals), f32),
            pltpu.SemaphoreType.DMA((occ, 2 * CORES * len(PIECES))),
            pltpu.SemaphoreType.DMA((occ,)),
        ],
        compiler_params=LIMIT,
        name="finish",
    )(places, panel_of, e_occ, e_b, e_vir.reshape(1, virtuals), *[a for group in arrays for a in group])
    return out[None]


def solution(mesh):
    fine = Mesh(mesh.devices.reshape(SIDE, SIDE, CORES, DEPTH), ("x", "y", "core", "virt"))
    rows = ("x", "y", "core")
    in_specs = (P(None, rows, "virt"), P(None, rows, "virt"), P(), P(), P())
    out_specs = P("virt", None, rows, None)
    return jax.shard_map(body, mesh=fine, in_specs=in_specs, out_specs=out_specs, check_vma=False)
```

profile of v0, /device:TPU:1, one launch (start us, length us, event | category | flops | bytes accessed | tf_op | source)
XLA Modules:
  0.0 234.1 jit_solution(17041442568066549596)
XLA Ops:
  6.5 1.9 fusion
  9.2 27.6 %all_to_all.20.refs_1_ = f32[8,64,256]{2,1,0:T(8,128)S(1)} all-to-all(f32[8,64,256]{2,1,0:T(8,128)} %param.5), channel_id=1, replica_groups=mesh['x'=4,'y'=4,'core'=2,'virt'=8] {'virt'}, dimensions={0} | all-to-all | bytes 1048576 | tf_op jit(solution)/shard_map/all_to_all | solution.py:133
  36.8 2.8 %collective-permute-start.2 = (f32[8,64,256]{2,1,0:T(8,128)S(1)}, f32[8,64,256]{2,1,0:T(8,128)S(1)}, u32[]{:S(2)}, u32[]{:S(2)}) collective-permute-start(f32[8,64,256]{2,1,0:T(8,128)S(1)} %all_to_all.20.refs_1_), channel_id=1, source_target_pairs={{0,48},{16,0},{32,16},{48,32},{1,49},{17,1},{33,17},{49,33},{2,50}... | collective-permute-start | bytes 1572872 | tf_op jit(solution)/shard_map/ppermute | solution.py:130
  40.8 1.5 collective-permute-start
  42.3 5.0 %collective-permute-done.2.refs_4_ = f32[8,64,256]{2,1,0:T(8,128)S(1)} collective-permute-done((f32[8,64,256]{2,1,0:T(8,128)S(1)}, f32[8,64,256]{2,1,0:T(8,128)S(1)}, u32[]{:S(2)}, u32[]{:S(2)}) %collective-permute-start.2) | collective-permute-done | bytes 524320 | tf_op jit(solution)/shard_map/ppermute | solution.py:130
  47.2 2.5 %collective-permute-start.4 = (f32[8,64,256]{2,1,0:T(8,128)S(1)}, f32[8,64,256]{2,1,0:T(8,128)}, u32[]{:S(2)}, u32[]{:S(2)}) collective-permute-start(f32[8,64,256]{2,1,0:T(8,128)S(1)} %collective-permute-done.2.refs_4_), channel_id=1, source_target_pairs={{0,192},{64,0},{128,64},{192,128},{1,193},{65,1},{129,65},{193,129... | collective-permute-start | bytes 1572872 | tf_op jit(solution)/shard_map/ppermute | solution.py:130
  51.7 1.7 collective-permute-start.6
  53.9 7.6 %collective-permute-done.4.refs_6_ = f32[8,64,256]{2,1,0:T(8,128)} collective-permute-done((f32[8,64,256]{2,1,0:T(8,128)S(1)}, f32[8,64,256]{2,1,0:T(8,128)}, u32[]{:S(2)}, u32[]{:S(2)}) %collective-permute-start.4) | collective-permute-done | bytes 524320 | tf_op jit(solution)/shard_map/ppermute | solution.py:130
  62.4 9.7 %product_0.1 = (f32[8,32,512]{2,1,0:T(8,128)}, f32[8,32,512]{2,1,0:T(8,128)}, f32[16,32,512]{2,1,0:T(8,128)}) custom-call(s32[4]{0:T(128)} %pad_add_fusion.places, f32[16,8,32,256]{3,2,1,0:T(8,128)} %bitcast.13, f32[8,64,256]{2,1,0:T(8,128)} %copy-done.3, f32[8,64,256]{2,1,0:T(8,128)} %copy-done.9, f32[8,64,256]{2,1,0:T(8,128)} %copy-done.8, ...), custom_call_target="tpu_custom_call" | custom-call | flops 40000000000 | bytes 20000000 | tf_op jit(solution)/shard_map/product_0/pallas_call | solution.py:149
  72.1 8.5 %all-to-all-start.1 = ((f32[16,32,512]{2,1,0:T(8,128)}), f32[16,32,512]{2,1,0:T(8,128)S(1)}, u32[]{:S(2)}, u32[]{:S(2)}) async-start(f32[16,32,512]{2,1,0:T(8,128)} %get-tuple-element.26), calls=%async_computation.1 | async-start | bytes 2097152 | tf_op jit(solution)/shard_map/all_to_all | solution.py:172
  80.6 2.6 %collective-permute-start.10 = (f32[8,64,256]{2,1,0:T(8,128)}, f32[8,64,256]{2,1,0:T(8,128)S(1)}, u32[]{:S(2)}, u32[]{:S(2)}) collective-permute-start(f32[8,64,256]{2,1,0:T(8,128)} %copy-done.9), channel_id=1, source_target_pairs={{0,192},{64,0},{128,64},{192,128},{1,193},{65,1},{129,65},{193,129... | collective-permute-start | bytes 1572872 | tf_op jit(solution)/shard_map/ppermute | solution.py:130
  83.3 2.7 %collective-permute-start.11 = (f32[8,64,256]{2,1,0:T(8,128)}, f32[8,64,256]{2,1,0:T(8,128)}, u32[]{:S(2)}, u32[]{:S(2)}) collective-permute-start(f32[8,64,256]{2,1,0:T(8,128)} %copy-done.5), channel_id=1, source_target_pairs={{0,48},{16,0},{32,16},{48,32},{1,49},{17,1},{33,17},{49,33},{2,50}... | collective-permute-start | bytes 1572872 | tf_op jit(solution)/shard_map/ppermute | solution.py:130
  85.9 9.9 %collective-permute-done.9.refs_2_ = f32[8,64,256]{2,1,0:T(8,128)S(1)} collective-permute-done((f32[8,64,256]{2,1,0:T(8,128)}, f32[8,64,256]{2,1,0:T(8,128)S(1)}, u32[]{:S(2)}, u32[]{:S(2)}) %collective-permute-start.9) | collective-permute-done | bytes 524320 | tf_op jit(solution)/shard_map/ppermute | solution.py:130
  95.8 2.2 collective-permute-start.14
  98.1 2.6 %collective-permute-start.16 = (f32[8,64,256]{2,1,0:T(8,128)}, f32[8,64,256]{2,1,0:T(8,128)}, u32[]{:S(2)}, u32[]{:S(2)}) collective-permute-start(f32[8,64,256]{2,1,0:T(8,128)} %collective-permute-done.12.refs_5_), channel_id=1, source_target_pairs={{0,48},{16,0},{32,16},{48,32},{1,49},{17,1},{33,17},{49,33},{2,50}... | collective-permute-start | bytes 1572872 | tf_op jit(solution)/shard_map/ppermute | solution.py:130
  100.8 22.2 %all-gather.7.cloned.1.call-done = f32[128,32,256]{2,1,0:T(8,128)} async-done(((f32[8,32,256]{2,1,0:T(8,128)}), f32[128,32,256]{2,1,0:T(8,128)}) %all-gather.7.cloned.1.call-update) | async-done | bytes 4194320 | tf_op jit(solution)/shard_map/all_gather | solution.py:132
  123.0 9.7 %product_1.1 = (f32[8,32,512]{2,1,0:T(8,128)}, f32[8,32,512]{2,1,0:T(8,128)}, f32[16,32,512]{2,1,0:T(8,128)}) custom-call(s32[4]{0:T(128)} %pad_add_fusion.places, f32[16,8,32,256]{3,2,1,0:T(8,128)} %bitcast.10, f32[8,64,256]{2,1,0:T(8,128)} %copy-done.3, f32[8,64,256]{2,1,0:T(8,128)} %copy-done.9, f32[8,64,256]{2,1,0:T(8,128)} %copy-done.8, ...), custom_call_target="tpu_custom_call" | custom-call | flops 2000000000 | bytes 20000000 | tf_op jit(solution)/shard_map/product_1/pallas_call | solution.py:149
  132.7 5.4 %all-to-all-start.2 = ((f32[16,32,512]{2,1,0:T(8,128)}), f32[16,32,512]{2,1,0:T(8,128)S(1)}, u32[]{:S(2)}, u32[]{:S(2)}) async-start(f32[16,32,512]{2,1,0:T(8,128)} %get-tuple-element.34), calls=%async_computation.2 | async-start | bytes 2097152 | tf_op jit(solution)/shard_map/all_to_all | solution.py:172
  138.2 15.8 %product_2.1 = (f32[8,64,512]{2,1,0:T(8,128)}, f32[8,64,512]{2,1,0:T(8,128)}, f32[16,64,512]{2,1,0:T(8,128)}) custom-call(s32[4]{0:T(128)} %pad_add_fusion.places, f32[16,8,32,256]{3,2,1,0:T(8,128)} %bitcast.14, f32[16,8,32,256]{3,2,1,0:T(8,128)} %bitcast.11, f32[8,64,256]{2,1,0:T(8,128)} %copy-done.10, f32[8,64,256]{2,1,0:T(8,128)} %copy-done.11, ...), custom_call_target="tpu_custom_call" | custom-call | flops 40000000000 | bytes 20000000 | tf_op jit(solution)/shard_map/product_2/pallas_call | solution.py:149
  154.1 10.7 %all-to-all-done.2.refs_5_ = f32[16,32,512]{2,1,0:T(8,128)S(1)} async-done(((f32[16,32,512]{2,1,0:T(8,128)}), f32[16,32,512]{2,1,0:T(8,128)S(1)}, u32[]{:S(2)}, u32[]{:S(2)}) %all-to-all-start.2) | async-done | bytes 1048608 | tf_op jit(solution)/shard_map/all_to_all | solution.py:172
  165.8 4.8 %all-to-all-start.3 = ((f32[16,64,512]{2,1,0:T(8,128)}), f32[16,64,512]{2,1,0:T(8,128)S(1)}, u32[]{:S(2)}, u32[]{:S(2)}) async-start(f32[16,64,512]{2,1,0:T(8,128)} %get-tuple-element.38), calls=%async_computation.3 | async-start | bytes 4194304 | tf_op jit(solution)/shard_map/all_to_all | solution.py:172
  172.7 1.6 collective-permute-done.8.refs_4_
  175.1 43.6 %all-to-all-done.3.refs_8_ = f32[16,64,512]{2,1,0:T(8,128)S(1)} async-done(((f32[16,64,512]{2,1,0:T(8,128)}), f32[16,64,512]{2,1,0:T(8,128)S(1)}, u32[]{:S(2)}, u32[]{:S(2)}) %all-to-all-start.3) | async-done | bytes 2097184 | tf_op jit(solution)/shard_map/all_to_all | solution.py:172
  220.0 7.3 %finish.1 = f32[8,64,2048]{2,1,0:T(8,128)} custom-call(s32[4]{0:T(128)} %pad_add_fusion.places, s32[32]{0:T(128)} %panel_of.1, f32[8]{0:T(128)} %e_occ.1, f32[64,1]{1,0:T(8,128)} %copy.7.e_b, f32[1,2048]{1,0:T(1,128)} %bitcast.12, f32[8,32,512]{2,1,0:T(8,128)} %get-tuple-element.22.refs_0_, f32[8,32,512]{2,1,0:T(8,128)} %collective-permute-done.7.refs_1_, ...), custom_call_target="tpu_custom_call" | custom-call | tf_op jit(solution)/shard_map/finish/pallas_call | solution.py:185
  (57 shorter events, 10.7 us)
Async XLA Ops:
  6.5 55.0 %all-gather.5.cloned.1.call-start = ((), (), s32[]{:S(2)}) async-start(), calls=%async_computation.4 | async-start | bytes 4456448 | tf_op jit(solution)/shard_map/all_gather | solution.py:132
  8.4 114.5 %all-gather.7.cloned.1.call-start = ((), (), s32[]{:S(2)}) async-start(), calls=%async_computation.5 | async-start | bytes 4456448 | tf_op jit(solution)/shard_map/all_gather | solution.py:132
  36.8 10.5 %collective-permute-start.2 = (f32[8,64,256]{2,1,0:T(8,128)S(1)}, f32[8,64,256]{2,1,0:T(8,128)S(1)}, u32[]{:S(2)}, u32[]{:S(2)}) collective-permute-start(f32[8,64,256]{2,1,0:T(8,128)S(1)} %all_to_all.20.refs_1_), channel_id=1, source_target_pairs={{0,48},{16,0},{32,16},{48,32},{1,49},{17,1},{33,17},{49,33},{2,50}... | collective-permute-start | bytes 1572872 | tf_op jit(solution)/shard_map/ppermute | solution.py:130
  39.6 10.9 %collective-permute-start.3 = (f32[8,64,256]{2,1,0:T(8,128)S(1)}, f32[8,64,256]{2,1,0:T(8,128)S(1)}, u32[]{:S(2)}, u32[]{:S(2)}) collective-permute-start(f32[8,64,256]{2,1,0:T(8,128)S(1)} %all_to_all.20.refs_1_), channel_id=1, source_target_pairs={{0,16},{16,32},{32,48},{48,0},{1,17},{17,33},{33,49},{49,1},{2,18}... | collective-permute-start | bytes 1572872 | tf_op jit(solution)/shard_map/ppermute | solution.py:130
  39.6 12.1 %collective-permute-start.1 = (f32[8,64,256]{2,1,0:T(8,128)S(1)}, f32[8,64,256]{2,1,0:T(8,128)S(1)}, u32[]{:S(2)}, u32[]{:S(2)}) collective-permute-start(f32[8,64,256]{2,1,0:T(8,128)S(1)} %all_to_all.20.refs_1_), channel_id=1, source_target_pairs={{0,64},{64,128},{128,192},{192,0},{1,65},{65,129},{129,193},{193,1... | collective-permute-start | bytes 1572872 | tf_op jit(solution)/shard_map/ppermute | solution.py:130
  40.8 13.1 %collective-permute-start = (f32[8,64,256]{2,1,0:T(8,128)S(1)}, f32[8,64,256]{2,1,0:T(8,128)S(1)}, u32[]{:S(2)}, u32[]{:S(2)}) collective-permute-start(f32[8,64,256]{2,1,0:T(8,128)S(1)} %all_to_all.20.refs_1_), channel_id=1, source_target_pairs={{0,192},{64,0},{128,64},{192,128},{1,193},{65,1},{129,65},{193,129... | collective-permute-start | bytes 1572872 | tf_op jit(solution)/shard_map/ppermute | solution.py:130
  47.2 14.3 %collective-permute-start.4 = (f32[8,64,256]{2,1,0:T(8,128)S(1)}, f32[8,64,256]{2,1,0:T(8,128)}, u32[]{:S(2)}, u32[]{:S(2)}) collective-permute-start(f32[8,64,256]{2,1,0:T(8,128)S(1)} %collective-permute-done.2.refs_4_), channel_id=1, source_target_pairs={{0,192},{64,0},{128,64},{192,128},{1,193},{65,1},{129,65},{193,129... | collective-permute-start | bytes 1572872 | tf_op jit(solution)/shard_map/ppermute | solution.py:130
  50.5 11.1 %collective-permute-start.5 = (f32[8,64,256]{2,1,0:T(8,128)S(1)}, f32[8,64,256]{2,1,0:T(8,128)S(1)}, u32[]{:S(2)}, u32[]{:S(2)}) collective-permute-start(f32[8,64,256]{2,1,0:T(8,128)S(1)} %collective-permute-done.3.refs_5_), channel_id=1, source_target_pairs={{0,64},{64,128},{128,192},{192,0},{1,65},{65,129},{129,193},{193,1... | collective-permute-start | bytes 1572872 | tf_op jit(solution)/shard_map/ppermute | solution.py:130
  51.7 9.9 %collective-permute-start.6 = (f32[8,64,256]{2,1,0:T(8,128)S(1)}, f32[8,64,256]{2,1,0:T(8,128)}, u32[]{:S(2)}, u32[]{:S(2)}) collective-permute-start(f32[8,64,256]{2,1,0:T(8,128)S(1)} %collective-permute-done.1.refs_3_), channel_id=1, source_target_pairs={{0,48},{16,0},{32,16},{48,32},{1,49},{17,1},{33,17},{49,33},{2,50}... | collective-permute-start | bytes 1572872 | tf_op jit(solution)/shard_map/ppermute | solution.py:130
  72.1 60.6 %all-to-all-start.1 = ((f32[16,32,512]{2,1,0:T(8,128)}), f32[16,32,512]{2,1,0:T(8,128)S(1)}, u32[]{:S(2)}, u32[]{:S(2)}) async-start(f32[16,32,512]{2,1,0:T(8,128)} %get-tuple-element.26), calls=%async_computation.1 | async-start | bytes 2097152 | tf_op jit(solution)/shard_map/all_to_all | solution.py:172
  80.6 15.2 %collective-permute-start.9 = (f32[8,64,256]{2,1,0:T(8,128)}, f32[8,64,256]{2,1,0:T(8,128)S(1)}, u32[]{:S(2)}, u32[]{:S(2)}) collective-permute-start(f32[8,64,256]{2,1,0:T(8,128)} %copy-done.9), channel_id=1, source_target_pairs={{0,16},{16,32},{32,48},{48,0},{1,17},{17,33},{33,49},{49,1},{2,18}... | collective-permute-start | bytes 1572872 | tf_op jit(solution)/shard_map/ppermute | solution.py:130
  80.6 17.4 %collective-permute-start.10 = (f32[8,64,256]{2,1,0:T(8,128)}, f32[8,64,256]{2,1,0:T(8,128)S(1)}, u32[]{:S(2)}, u32[]{:S(2)}) collective-permute-start(f32[8,64,256]{2,1,0:T(8,128)} %copy-done.9), channel_id=1, source_target_pairs={{0,192},{64,0},{128,64},{192,128},{1,193},{65,1},{129,65},{193,129... | collective-permute-start | bytes 1572872 | tf_op jit(solution)/shard_map/ppermute | solution.py:130
  83.3 14.8 %collective-permute-start.12 = (f32[8,64,256]{2,1,0:T(8,128)}, f32[8,64,256]{2,1,0:T(8,128)}, u32[]{:S(2)}, u32[]{:S(2)}) collective-permute-start(f32[8,64,256]{2,1,0:T(8,128)} %collective-permute-done.6.refs_8_), channel_id=1, source_target_pairs={{0,64},{64,128},{128,192},{192,0},{1,65},{65,129},{129,193},{193,1... | collective-permute-start | bytes 1572872 | tf_op jit(solution)/shard_map/ppermute | solution.py:130
  83.3 54.9 %collective-permute-start.11 = (f32[8,64,256]{2,1,0:T(8,128)}, f32[8,64,256]{2,1,0:T(8,128)}, u32[]{:S(2)}, u32[]{:S(2)}) collective-permute-start(f32[8,64,256]{2,1,0:T(8,128)} %copy-done.5), channel_id=1, source_target_pairs={{0,48},{16,0},{32,16},{48,32},{1,49},{17,1},{33,17},{49,33},{2,50}... | collective-permute-start | bytes 1572872 | tf_op jit(solution)/shard_map/ppermute | solution.py:130
  95.8 42.4 %collective-permute-start.13 = (f32[8,64,256]{2,1,0:T(8,128)S(1)}, f32[8,64,256]{2,1,0:T(8,128)}, u32[]{:S(2)}, u32[]{:S(2)}) collective-permute-start(f32[8,64,256]{2,1,0:T(8,128)S(1)} %collective-permute-done.9.refs_2_), channel_id=1, source_target_pairs={{0,16},{16,32},{32,48},{48,0},{1,17},{17,33},{33,49},{49,1},{2,18}... | collective-permute-start | bytes 1572872 | tf_op jit(solution)/shard_map/ppermute | solution.py:130
  95.8 42.4 %collective-permute-start.14 = (f32[8,64,256]{2,1,0:T(8,128)S(1)}, f32[8,64,256]{2,1,0:T(8,128)}, u32[]{:S(2)}, u32[]{:S(2)}) collective-permute-start(f32[8,64,256]{2,1,0:T(8,128)S(1)} %collective-permute-done.9.refs_2_), channel_id=1, source_target_pairs={{0,192},{64,0},{128,64},{192,128},{1,193},{65,1},{129,65},{193,129... | collective-permute-start | bytes 1572872 | tf_op jit(solution)/shard_map/ppermute | solution.py:130
  98.0 40.2 %collective-permute-start.15 = (f32[8,64,256]{2,1,0:T(8,128)}, f32[8,64,256]{2,1,0:T(8,128)}, u32[]{:S(2)}, u32[]{:S(2)}) collective-permute-start(f32[8,64,256]{2,1,0:T(8,128)} %copy-done.6), channel_id=1, source_target_pairs={{0,16},{16,32},{32,48},{48,0},{1,17},{17,33},{33,49},{49,1},{2,18}... | collective-permute-start | bytes 1572872 | tf_op jit(solution)/shard_map/ppermute | solution.py:130
  98.1 40.1 %collective-permute-start.16 = (f32[8,64,256]{2,1,0:T(8,128)}, f32[8,64,256]{2,1,0:T(8,128)}, u32[]{:S(2)}, u32[]{:S(2)}) collective-permute-start(f32[8,64,256]{2,1,0:T(8,128)} %collective-permute-done.12.refs_5_), channel_id=1, source_target_pairs={{0,48},{16,0},{32,16},{48,32},{1,49},{17,1},{33,17},{49,33},{2,50}... | collective-permute-start | bytes 1572872 | tf_op jit(solution)/shard_map/ppermute | solution.py:130
  132.7 32.1 %all-to-all-start.2 = ((f32[16,32,512]{2,1,0:T(8,128)}), f32[16,32,512]{2,1,0:T(8,128)S(1)}, u32[]{:S(2)}, u32[]{:S(2)}) async-start(f32[16,32,512]{2,1,0:T(8,128)} %get-tuple-element.34), calls=%async_computation.2 | async-start | bytes 2097152 | tf_op jit(solution)/shard_map/all_to_all | solution.py:172
  165.8 52.9 %all-to-all-start.3 = ((f32[16,64,512]{2,1,0:T(8,128)}), f32[16,64,512]{2,1,0:T(8,128)S(1)}, u32[]{:S(2)}, u32[]{:S(2)}) async-start(f32[16,64,512]{2,1,0:T(8,128)} %get-tuple-element.38), calls=%async_computation.3 | async-start | bytes 4194304 | tf_op jit(solution)/shard_map/all_to_all | solution.py:172
  170.6 4.5 %collective-permute-start.17 = (f32[8,64,512]{2,1,0:T(8,128)}, f32[8,64,512]{2,1,0:T(8,128)S(1)}, u32[]{:S(2)}, u32[]{:S(2)}) collective-permute-start(f32[8,64,512]{2,1,0:T(8,128)} %get-tuple-element.37), channel_id=1, source_target_pairs={{0,8},{8,0},{1,9},{9,1},{2,10},{10,2},{3,11},{11,3},{4,12},{12,4},... | collective-permute-start | bytes 3145736 | tf_op jit(solution)/shard_map/ppermute | solution.py:173
  170.8 3.6 %collective-permute-start.8 = (f32[8,32,512]{2,1,0:T(8,128)}, f32[8,32,512]{2,1,0:T(8,128)}, u32[]{:S(2)}, u32[]{:S(2)}) collective-permute-start(f32[8,32,512]{2,1,0:T(8,128)} %get-tuple-element.29), channel_id=1, source_target_pairs={{0,8},{8,0},{1,9},{9,1},{2,10},{10,2},{3,11},{11,3},{4,12},{12,4},... | collective-permute-start | bytes 1572872 | tf_op jit(solution)/shard_map/ppermute | solution.py:173
  171.1 4.0 %collective-permute-start.7 = (f32[8,32,512]{2,1,0:T(8,128)}, f32[8,32,512]{2,1,0:T(8,128)}, u32[]{:S(2)}, u32[]{:S(2)}) collective-permute-start(f32[8,32,512]{2,1,0:T(8,128)} %get-tuple-element.23), channel_id=1, source_target_pairs={{0,8},{8,0},{1,9},{9,1},{2,10},{10,2},{3,11},{11,3},{4,12},{12,4},... | collective-permute-start | bytes 1572872 | tf_op jit(solution)/shard_map/ppermute | solution.py:173
  175.1 43.6 %copy-start.4 = (f32[8,64,512]{2,1,0:T(8,128)}, f32[8,64,512]{2,1,0:T(8,128)S(1)}, u32[]{:S(2)}) copy-start(f32[8,64,512]{2,1,0:T(8,128)S(1)} %collective-permute-done.17.refs_7_) | copy-start | bytes 3145732
  (11 other events, 164.0 us)
Sparse Core Ops, SparseCore 0:
  9.2 51.4 all-gather.4
  62.5 60.4 all-gather.6
where the time goes:
time: 235 us; the launch traced here: 234 us
  waiting for transfers between devices  103 us (44%)
  Pallas kernels  42.5 us (18%)
  starting transfers between devices  40.7 us (17%)
  blocking collectives  27.6 us (12%)
  between operations  13.6 us (6%)
  local copies, waits for them, and re-layouts  6.41 us (3%)
    all_to_all x3, waiting for transfers between devices, body(): lax.all_to_all(whole, ('core', 'virt'), split_axis=0, concat_axis=0, tile...  54.3 us
    pallas_call x3, Pallas kernels, body(): pl.pallas_call(functools.partial(product_kernel, (occ, part, panel, width...  35.2 us
    all_to_all x1, blocking collectives, body(): lax.all_to_all(amps, 'virt', split_axis=0, concat_axis=0, tiled=True)  27.6 us
    ppermute x15, waiting for transfers between devices, move(): lax.ppermute(data, name, [(n, (n - step) % SIDE) for n in range(SIDE)])  23.2 us
    all_gather x2, waiting for transfers between devices, body(): lax.all_gather(ints[:, h * part:(h + 1) * part], ('core', 'virt'), axis=0)  22.2 us
    ppermute x15, starting transfers between devices, move(): lax.ppermute(data, name, [(n, (n - step) % SIDE) for n in range(SIDE)])  21.2 us
    all_to_all x3, starting transfers between devices, body(): lax.all_to_all(whole, ('core', 'virt'), split_axis=0, concat_axis=0, tile...  18.8 us
    pallas_call x1, Pallas kernels, body(): pl.pallas_call(functools.partial(finish_kernel, (occ, panel, virtuals), p...  7.26 us
  transfers between devices with their start and end apart: 23, of which 9 were waited for; matrix products, arithmetic and copies ran while one was open for 1% of the time, Pallas kernels for 15%

commit v1 on v0

--- a/solution.py
+++ b/solution.py
@@ -10,19 +10,36 @@
 SIDE = 4
 CORES = 2
 DEPTH = 8
-HALVES = 2
+HALVES = 1
 BLOCK = 256
 NT = (((1,), (1,)), ((), ()))
 SMEM = pl.BlockSpec(memory_space=pltpu.SMEM)
 ANY = pl.BlockSpec(memory_space=pl.ANY)
 VMEM = pl.BlockSpec(memory_space=pltpu.VMEM)
+HBM = pl.BlockSpec(memory_space=pltpu.HBM)
 LIMIT = pltpu.CompilerParams(vmem_limit_bytes=60 * 2**20)
-COSTS = [pl.CostEstimate(flops=f * 10**9, transcendentals=0, bytes_accessed=20_000_000) for f in (40, 2, 40)]
-ROUTES = [
-    [((1, 0), (1, 0)), ((-1, 0), (-1, 0)), ((0, 1), (0, 1)), ((0, -1), (0, -1)), ((1, 1), (1, 0)), ((-1, -1), (-1, 0)), ((-1, 1), (0, 1))],
-    [((1, -1), (0, -1)), ((2, 0), (1, 0)), ((0, 2), (0, 1)), ((2, 1), (-1, 0)), ((1, 2), (0, -1)), ((2, -1), (1, 0)), ((-1, 2), (0, -1)), ((2, 2), (0, 1))],
+COSTS = [pl.CostEstimate(flops=f * 10**9, transcendentals=0, bytes_accessed=f * 10**6) for f in (20, 40)]
+FIRST = [
+    ((1, 0), (1, 0)),
+    ((-1, 0), (-1, 0)),
+    ((0, 1), (0, 1)),
+    ((0, -1), (0, -1)),
+    ((1, 1), (1, 0)),
+    ((-1, -1), (-1, 0)),
+    ((-1, 1), (0, 1)),
+    ((1, -1), (0, -1)),
+    ((2, 0), (1, 0)),
+    ((0, 2), (0, 1)),
+    ((2, 1), (-1, 0)),
+    ((1, 2), (0, -1)),
 ]
-PIECES = [(0, (0,)), (0, (1,)), (1, (0, 1))]
+LAST = [((2, -1), (1, 0)), ((-1, 2), (0, -1)), ((2, 2), (0, 1))]
+SETS = [
+    [(0, 0), (1, 0), (-1, 0), (0, 1)],
+    [(0, -1), (1, 1), (-1, -1), (-1, 1), (1, -1), (2, 0), (0, 2), (2, 1), (1, 2), (2, -1), (-1, 2), (2, 2)],
+]
+SOON = [(1, 1), (-1, -1), (-1, 1), (1, -1)]
+PIECES = [(0, (0,)), (1, (0,))]
 
 
 def wrap(x, y):
@@ -131,14 +148,20 @@
 
     int_all = [lax.all_gather(ints[:, h * part : (h + 1) * part], ("core", "virt"), axis=0) for h in range(HALVES)]
     held = {(0, 0): lax.all_to_all(amps, "virt", split_axis=0, concat_axis=0, tiled=True)}
-    sets, starts = [], []
-    for k, routes in enumerate(ROUTES):
-        chips = [(0, 0)] if k == 0 else []
+    sets = [[wrap(*chip) for chip in chips] for chips in SETS]
+    starts = [sum(map(len, sets[:k])) * panel for k in range(len(sets))]
+
+    def bring(routes, after=()):
         for to, (dx, dy) in routes:
-            held[wrap(*to)] = move(held[wrap(to[0] - dx, to[1] - dy)], dx, dy)
-            chips.append(wrap(*to))
-        starts.append(sum(map(len, sets)) * panel)
-        sets.append(chips)
+            data = held[wrap(to[0] - dx, to[1] - dy)]
+            if after:
+                data = lax.optimization_barrier([data, *after])[0]
+            held[wrap(*to)] = move(data, dx, dy)
+
+    bring(FIRST)
+    soon = [wrap(*chip) for chip in SOON]
+    int_all[0], *ready = lax.optimization_barrier([int_all[0]] + [held[chip] for chip in soon])
+    held.update(zip(soon, ready))
 
     arrays, places_of, mirror = [], [], []
     for n, (k, halves) in enumerate(PIECES):
@@ -173,9 +196,8 @@
         arrays.append([own_all, lax.ppermute(other_all, "core", [(0, 1), (1, 0)])])
         places_of.append((starts[k], size, halves[0] * part, tall))
         if n + 1 < len(PIECES):
-            after = [own_all] + mirror[:-1]
-            tied = lax.optimization_barrier(int_all + after)
-            int_all = list(tied[:HALVES])
+            int_all = list(lax.optimization_barrier(int_all + [own_all])[:HALVES])
+            bring(LAST, [own_all])
     for pair_of, back in zip(arrays, mirror):
         pair_of.append(back)
 
@@ -185,7 +207,7 @@
     out = pl.pallas_call(
         functools.partial(finish_kernel, (occ, panel, virtuals), places_of, slots),
         out_shape=jax.ShapeDtypeStruct((occ, panel, virtuals), f32),
-        in_specs=[SMEM, SMEM, SMEM, VMEM, VMEM] + [ANY] * (3 * len(PIECES)),
+        in_specs=[SMEM, SMEM, SMEM, VMEM, VMEM] + [HBM] * (3 * len(PIECES) - 1) + [VMEM],
         out_specs=ANY,
         scratch_shapes=[
             pltpu.SMEM((virtuals // panel,), jnp.int32),
@@ -195,7 +217,7 @@
             pltpu.SemaphoreType.DMA((occ, 2 * CORES * len(PIECES))),
             pltpu.SemaphoreType.DMA((occ,)),
         ],
-        compiler_params=LIMIT,
+        compiler_params=pltpu.CompilerParams(vmem_limit_bytes=60 * 2**20),
         name="finish",
     )(places, panel_of, e_occ, e_b, e_vir.reshape(1, virtuals), *[a for group in arrays for a in group])
     return out[None]

time: 235 us -> 215 us (0.915)
  starting transfers between devices: 40.7 us -> 31.6 us
  Pallas kernels: 42.5 us -> 37.9 us
    all_to_all x3 -> x2, waiting for transfers between devices: 54.3 us -> 68.1 us  [body(): lax.all_to_all(whole, ('core', 'virt'), split_axis=0, concat_axis=0, tile...]
    all_gather x2 -> x1, waiting for transfers between devices: 22.2 us -> 9.71 us  [body(): lax.all_gather(ints[:, h * part:(h + 1) * part], ('core', 'virt'), axis=0)]
    all_to_all x3 -> x2, starting transfers between devices: 18.8 us -> 10.8 us  [body(): lax.all_to_all(whole, ('core', 'virt'), split_axis=0, concat_axis=0, tile...]
    pallas_call x3 -> x2, Pallas kernels: 35.2 us -> 30.5 us  [body(): pl.pallas_call(functools.partial(product_kernel, (occ, part, panel, width...]
    ppermute x15, waiting for transfers between devices: 23.2 us -> 19.7 us  [move(): lax.ppermute(data, name, [(n, (n - step) % SIDE) for n in range(SIDE)])]
  transfers between devices with their start and end apart: 23 -> 20, of which waited for: 9 -> 9; matrix products, arithmetic and copies ran while one was open for 1% -> 1% of each run, Pallas kernels for 15% -> 14%
where the time goes in v1:
time: 215 us
  waiting for transfers between devices  101 us (47%)
  Pallas kernels  37.9 us (18%)
  starting transfers between devices  31.6 us (15%)
  blocking collectives  26.2 us (12%)
  between operations  13.5 us (6%)
  local copies, waits for them, and re-layouts  4.11 us (2%)
    all_to_all x2, waiting for transfers between devices, body(): lax.all_to_all(whole, ('core', 'virt'), split_axis=0, concat_axis=0, tile...  68.1 us
    pallas_call x2, Pallas kernels, body(): pl.pallas_call(functools.partial(product_kernel, (occ, part, panel, width...  30.5 us
    all_to_all x1, blocking collectives, body(): lax.all_to_all(amps, 'virt', split_axis=0, concat_axis=0, tiled=True)  26.2 us
    ppermute x15, starting transfers between devices, move(): lax.ppermute(data, name, [(n, (n - step) % SIDE) for n in range(SIDE)])  20.2 us
    ppermute x15, waiting for transfers between devices, move(): lax.ppermute(data, name, [(n, (n - step) % SIDE) for n in range(SIDE)])  19.7 us
    all_to_all x2, starting transfers between devices, body(): lax.all_to_all(whole, ('core', 'virt'), split_axis=0, concat_axis=0, tile...  10.8 us
    all_gather x1, waiting for transfers between devices, body(): lax.all_gather(ints[:, h * part:(h + 1) * part], ('core', 'virt'), axis=0)  9.71 us
    pallas_call x1, Pallas kernels, body(): pl.pallas_call(functools.partial(finish_kernel, (occ, panel, virtuals), p...  7.44 us
  transfers between devices with their start and end apart: 20, of which 9 were waited for; matrix products, arithmetic and copies ran while one was open for 1% of the time, Pallas kernels for 14%

profile of v1, /device:TPU:1, one launch (start us, length us, event | category | flops | bytes accessed | tf_op | source)
XLA Modules:
  0.0 214.7 jit_solution(647980529918870079)
XLA Ops:
  7.3 26.2 %all_to_all.15.refs_1_ = f32[8,64,256]{2,1,0:T(8,128)S(1)} all-to-all(f32[8,64,256]{2,1,0:T(8,128)} %param.5), channel_id=1, replica_groups=mesh['x'=4,'y'=4,'core'=2,'virt'=8] {'virt'}, dimensions={0} | all-to-all | bytes 1048576 | tf_op jit(solution)/shard_map/all_to_all | solution.py:150
  33.4 2.5 %collective-permute-start.6 = (f32[8,64,256]{2,1,0:T(8,128)S(1)}, f32[8,64,256]{2,1,0:T(8,128)S(1)}, u32[]{:S(2)}, u32[]{:S(2)}) collective-permute-start(f32[8,64,256]{2,1,0:T(8,128)S(1)} %all_to_all.15.refs_1_), channel_id=1, source_target_pairs={{0,192},{64,0},{128,64},{192,128},{1,193},{65,1},{129,65},{193,129... | collective-permute-start | bytes 1572872 | tf_op jit(solution)/shard_map/ppermute | solution.py:147
  35.9 2.9 %collective-permute-start = (f32[8,64,256]{2,1,0:T(8,128)S(1)}, f32[8,64,256]{2,1,0:T(8,128)}, u32[]{:S(2)}, u32[]{:S(2)}) collective-permute-start(f32[8,64,256]{2,1,0:T(8,128)S(1)} %all_to_all.15.refs_1_), channel_id=1, source_target_pairs={{0,48},{16,0},{32,16},{48,32},{1,49},{17,1},{33,17},{49,33},{2,50}... | collective-permute-start | bytes 1572872 | tf_op jit(solution)/shard_map/ppermute | solution.py:147
  38.8 4.5 %collective-permute-done.6.refs_2_ = f32[8,64,256]{2,1,0:T(8,128)S(1)} collective-permute-done((f32[8,64,256]{2,1,0:T(8,128)S(1)}, f32[8,64,256]{2,1,0:T(8,128)S(1)}, u32[]{:S(2)}, u32[]{:S(2)}) %collective-permute-start.6) | collective-permute-done | bytes 524320 | tf_op jit(solution)/shard_map/ppermute | solution.py:147
  43.3 1.4 collective-permute-start.7
  44.7 1.9 collective-permute-done.4.refs_3_
  46.5 2.9 %collective-permute-start.5 = (f32[8,64,256]{2,1,0:T(8,128)}, f32[8,64,256]{2,1,0:T(8,128)S(1)}, u32[]{:S(2)}, u32[]{:S(2)}) collective-permute-start(f32[8,64,256]{2,1,0:T(8,128)} %collective-permute-done.4.refs_3_), channel_id=1, source_target_pairs={{0,48},{16,0},{32,16},{48,32},{1,49},{17,1},{33,17},{49,33},{2,50}... | collective-permute-start | bytes 1572872 | tf_op jit(solution)/shard_map/ppermute | solution.py:147
  52.6 7.8 %collective-permute-done.7.refs_5_ = f32[8,64,256]{2,1,0:T(8,128)S(1)} collective-permute-done((f32[8,64,256]{2,1,0:T(8,128)S(1)}, f32[8,64,256]{2,1,0:T(8,128)S(1)}, u32[]{:S(2)}, u32[]{:S(2)}) %collective-permute-start.7) | collective-permute-done | bytes 524320 | tf_op jit(solution)/shard_map/ppermute | solution.py:147
  60.4 2.4 %collective-permute-start.9 = (f32[8,64,256]{2,1,0:T(8,128)S(1)}, f32[8,64,256]{2,1,0:T(8,128)}, u32[]{:S(2)}, u32[]{:S(2)}) collective-permute-start(f32[8,64,256]{2,1,0:T(8,128)S(1)} %collective-permute-done.6.refs_2_), channel_id=1, source_target_pairs={{0,192},{64,0},{128,64},{192,128},{1,193},{65,1},{129,65},{193,129... | collective-permute-start | bytes 1572872 | tf_op jit(solution)/shard_map/ppermute | solution.py:147
  63.1 9.7 %all-gather.3.cloned.1.call-done = f32[128,64,256]{2,1,0:T(8,128)} async-done(((f32[8,64,256]{2,1,0:T(8,128)}), f32[128,64,256]{2,1,0:T(8,128)}) %all-gather.3.cloned.1.call-update) | async-done | bytes 8388624 | tf_op jit(solution)/shard_map/all_gather | solution.py:149
  72.8 10.7 %product_0.1 = (f32[8,64,256]{2,1,0:T(8,128)}, f32[8,64,256]{2,1,0:T(8,128)}, f32[16,64,256]{2,1,0:T(8,128)}) custom-call(s32[4]{0:T(128)} %pad_add_fusion.places, f32[16,8,64,256]{3,2,1,0:T(8,128)} %bitcast.10, f32[8,64,256]{2,1,0:T(8,128)} %copy-done.2, f32[8,64,256]{2,1,0:T(8,128)} %copy-done.5, f32[8,64,256]{2,1,0:T(8,128)} %collective-permute-done.4.refs_3_, ...), custom_call_target="tpu_custom_call" | custom-call | flops 20000000000 | bytes 20000000 | tf_op jit(solution)/shard_map/product_0/pallas_call | solution.py:172
  83.6 1.4 collective-permute-start.14
  84.9 2.5 %collective-permute-start.13 = (f32[8,64,256]{2,1,0:T(8,128)S(1)}, f32[8,64,256]{2,1,0:T(8,128)S(1)}, u32[]{:S(2)}, u32[]{:S(2)}) collective-permute-start(f32[8,64,256]{2,1,0:T(8,128)S(1)} %collective-permute-done.7.refs_5_), channel_id=1, source_target_pairs={{0,192},{64,0},{128,64},{192,128},{1,193},{65,1},{129,65},{193,129... | collective-permute-start | bytes 1572872 | tf_op jit(solution)/shard_map/ppermute | solution.py:147
  87.4 1.6 collective-permute-start.15
  89.0 5.8 %all-to-all-start.1 = ((f32[16,64,256]{2,1,0:T(8,128)}), f32[16,64,256]{2,1,0:T(8,128)S(1)}, u32[]{:S(2)}, u32[]{:S(2)}) async-start(f32[16,64,256]{2,1,0:T(8,128)} %get-tuple-element.34), calls=%async_computation.1 | async-start | bytes 2097152 | tf_op jit(solution)/shard_map/all_to_all | solution.py:195
  94.8 3.7 %collective-permute-done.14.refs_11_ = f32[8,64,256]{2,1,0:T(8,128)S(1)} collective-permute-done((f32[8,64,256]{2,1,0:T(8,128)}, f32[8,64,256]{2,1,0:T(8,128)S(1)}, u32[]{:S(2)}, u32[]{:S(2)}) %collective-permute-start.14) | collective-permute-done | bytes 524320 | tf_op jit(solution)/shard_map/ppermute | solution.py:147
  98.5 1.9 collective-permute-done.15.refs_12_
  100.4 19.8 %product_1.1 = (f32[8,64,768]{2,1,0:T(8,128)}, f32[8,64,768]{2,1,0:T(8,128)}, f32[16,64,768]{2,1,0:T(8,128)}) custom-call(s32[4]{0:T(128)} %pad_add_fusion.places, f32[16,8,64,256]{3,2,1,0:T(8,128)} %bitcast.11, f32[8,64,256]{2,1,0:T(8,128)} %copy-done.3, f32[8,64,256]{2,1,0:T(8,128)} %copy-done.7, f32[8,64,256]{2,1,0:T(8,128)} %collective-permute-done.3.refs_3_, ...), custom_call_target="tpu_custom_call" | custom-call | flops 40000000000 | bytes 40000000 | tf_op jit(solution)/shard_map/product_1/pallas_call | solution.py:172
  120.1 1.3 all-to-all-done.1.refs_2_
  122.4 5.0 %all-to-all-start.2 = ((f32[16,64,768]{2,1,0:T(8,128)}), f32[16,64,768]{2,1,0:T(8,128)S(1)}, u32[]{:S(2)}, u32[]{:S(2)}) async-start(f32[16,64,768]{2,1,0:T(8,128)} %get-tuple-element.38), calls=%async_computation.2 | async-start | bytes 6291456 | tf_op jit(solution)/shard_map/all_to_all | solution.py:195
  129.4 2.5 %collective-permute-done.8.refs_1_ = f32[8,64,256]{2,1,0:T(8,128)} collective-permute-done((f32[8,64,256]{2,1,0:T(8,128)}, f32[8,64,256]{2,1,0:T(8,128)}, u32[]{:S(2)}, u32[]{:S(2)}) %collective-permute-start.8) | collective-permute-done | bytes 524320 | tf_op jit(solution)/shard_map/ppermute | solution.py:196
  131.9 66.9 %all-to-all-done.2.refs_5_ = f32[16,64,768]{2,1,0:T(8,128)S(1)} async-done(((f32[16,64,768]{2,1,0:T(8,128)}), f32[16,64,768]{2,1,0:T(8,128)S(1)}, u32[]{:S(2)}, u32[]{:S(2)}) %all-to-all-start.2) | async-done | bytes 3145760 | tf_op jit(solution)/shard_map/all_to_all | solution.py:195
  198.8 1.6 copy-done
  200.4 7.4 %finish.1 = f32[8,64,2048]{2,1,0:T(8,128)} custom-call(s32[4]{0:T(128)} %pad_add_fusion.places, s32[32]{0:T(128)} %panel_of.1, f32[8]{0:T(128)} %e_occ.1, f32[64,1]{1,0:T(8,128)} %copy.7.e_b, f32[1,2048]{1,0:T(1,128)} %bitcast.9, f32[8,64,256]{2,1,0:T(8,128)} %get-tuple-element.23.refs_0_, f32[8,64,256]{2,1,0:T(8,128)} %collective-permute-done.8.refs_1_, ...), custom_call_target="tpu_custom_call" | custom-call | tf_op jit(solution)/shard_map/finish/pallas_call | solution.py:207
  (44 shorter events, 7.2 us)
Async XLA Ops:
  6.5 66.3 %all-gather.3.cloned.1.call-start = ((), (), s32[]{:S(2)}) async-start(), calls=%async_computation.3 | async-start | bytes 8912896 | tf_op jit(solution)/shard_map/all_gather | solution.py:149
  33.4 39.4 %copy-start.2 = (f32[8,64,256]{2,1,0:T(8,128)}, f32[8,64,256]{2,1,0:T(8,128)S(1)}, u32[]{:S(2)}) copy-start(f32[8,64,256]{2,1,0:T(8,128)S(1)} %all_to_all.15.refs_1_) | copy-start | bytes 1572868
  33.4 9.9 %collective-permute-start.6 = (f32[8,64,256]{2,1,0:T(8,128)S(1)}, f32[8,64,256]{2,1,0:T(8,128)S(1)}, u32[]{:S(2)}, u32[]{:S(2)}) collective-permute-start(f32[8,64,256]{2,1,0:T(8,128)S(1)} %all_to_all.15.refs_1_), channel_id=1, source_target_pairs={{0,192},{64,0},{128,64},{192,128},{1,193},{65,1},{129,65},{193,129... | collective-permute-start | bytes 1572872 | tf_op jit(solution)/shard_map/ppermute | solution.py:147
  35.9 10.6 %collective-permute-start.4 = (f32[8,64,256]{2,1,0:T(8,128)S(1)}, f32[8,64,256]{2,1,0:T(8,128)}, u32[]{:S(2)}, u32[]{:S(2)}) collective-permute-start(f32[8,64,256]{2,1,0:T(8,128)S(1)} %all_to_all.15.refs_1_), channel_id=1, source_target_pairs={{0,64},{64,128},{128,192},{192,0},{1,65},{65,129},{129,193},{193,1... | collective-permute-start | bytes 1572872 | tf_op jit(solution)/shard_map/ppermute | solution.py:147
  35.9 13.5 %collective-permute-start = (f32[8,64,256]{2,1,0:T(8,128)S(1)}, f32[8,64,256]{2,1,0:T(8,128)}, u32[]{:S(2)}, u32[]{:S(2)}) collective-permute-start(f32[8,64,256]{2,1,0:T(8,128)S(1)} %all_to_all.15.refs_1_), channel_id=1, source_target_pairs={{0,48},{16,0},{32,16},{48,32},{1,49},{17,1},{33,17},{49,33},{2,50}... | collective-permute-start | bytes 1572872 | tf_op jit(solution)/shard_map/ppermute | solution.py:147
  38.8 11.0 %collective-permute-start.2 = (f32[8,64,256]{2,1,0:T(8,128)S(1)}, f32[8,64,256]{2,1,0:T(8,128)S(1)}, u32[]{:S(2)}, u32[]{:S(2)}) collective-permute-start(f32[8,64,256]{2,1,0:T(8,128)S(1)} %all_to_all.15.refs_1_), channel_id=1, source_target_pairs={{0,16},{16,32},{32,48},{48,0},{1,17},{17,33},{33,49},{49,1},{2,18}... | collective-permute-start | bytes 1572872 | tf_op jit(solution)/shard_map/ppermute | solution.py:147
  43.3 29.5 %copy-start.5 = (f32[8,64,256]{2,1,0:T(8,128)}, f32[8,64,256]{2,1,0:T(8,128)S(1)}, u32[]{:S(2)}) copy-start(f32[8,64,256]{2,1,0:T(8,128)S(1)} %collective-permute-done.6.refs_2_) | copy-start | bytes 1572868
  43.3 17.1 %collective-permute-start.7 = (f32[8,64,256]{2,1,0:T(8,128)S(1)}, f32[8,64,256]{2,1,0:T(8,128)S(1)}, u32[]{:S(2)}, u32[]{:S(2)}) collective-permute-start(f32[8,64,256]{2,1,0:T(8,128)S(1)} %collective-permute-done.6.refs_2_), channel_id=1, source_target_pairs={{0,16},{16,32},{32,48},{48,0},{1,17},{17,33},{33,49},{49,1},{2,18}... | collective-permute-start | bytes 1572872 | tf_op jit(solution)/shard_map/ppermute | solution.py:147
  46.5 16.3 %collective-permute-start.5 = (f32[8,64,256]{2,1,0:T(8,128)}, f32[8,64,256]{2,1,0:T(8,128)S(1)}, u32[]{:S(2)}, u32[]{:S(2)}) collective-permute-start(f32[8,64,256]{2,1,0:T(8,128)} %collective-permute-done.4.refs_3_), channel_id=1, source_target_pairs={{0,48},{16,0},{32,16},{48,32},{1,49},{17,1},{33,17},{49,33},{2,50}... | collective-permute-start | bytes 1572872 | tf_op jit(solution)/shard_map/ppermute | solution.py:147
  49.4 13.4 %collective-permute-start.1 = (f32[8,64,256]{2,1,0:T(8,128)}, f32[8,64,256]{2,1,0:T(8,128)S(1)}, u32[]{:S(2)}, u32[]{:S(2)}) collective-permute-start(f32[8,64,256]{2,1,0:T(8,128)} %collective-permute-done.refs_4_), channel_id=1, source_target_pairs={{0,192},{64,0},{128,64},{192,128},{1,193},{65,1},{129,65},{193,129... | collective-permute-start | bytes 1572872 | tf_op jit(solution)/shard_map/ppermute | solution.py:147
  49.8 33.7 %copy-start.3 = (f32[8,64,256]{2,1,0:T(8,128)}, f32[8,64,256]{2,1,0:T(8,128)S(1)}, u32[]{:S(2)}) copy-start(f32[8,64,256]{2,1,0:T(8,128)S(1)} %collective-permute-done.2.refs_1_) | copy-start | bytes 1572868
  49.8 13.3 %collective-permute-start.3 = (f32[8,64,256]{2,1,0:T(8,128)S(1)}, f32[8,64,256]{2,1,0:T(8,128)}, u32[]{:S(2)}, u32[]{:S(2)}) collective-permute-start(f32[8,64,256]{2,1,0:T(8,128)S(1)} %collective-permute-done.2.refs_1_), channel_id=1, source_target_pairs={{0,64},{64,128},{128,192},{192,0},{1,65},{65,129},{129,193},{193,1... | collective-permute-start | bytes 1572872 | tf_op jit(solution)/shard_map/ppermute | solution.py:147
  51.6 35.8 %collective-permute-start.10 = (f32[8,64,256]{2,1,0:T(8,128)}, f32[8,64,256]{2,1,0:T(8,128)}, u32[]{:S(2)}, u32[]{:S(2)}) collective-permute-start(f32[8,64,256]{2,1,0:T(8,128)} %collective-permute-done.refs_4_), channel_id=1, source_target_pairs={{0,48},{16,0},{32,16},{48,32},{1,49},{17,1},{33,17},{49,33},{2,50}... | collective-permute-start | bytes 1572872 | tf_op jit(solution)/shard_map/ppermute | solution.py:147
  60.4 24.5 %copy-start.4 = (f32[8,64,256]{2,1,0:T(8,128)}, f32[8,64,256]{2,1,0:T(8,128)S(1)}, u32[]{:S(2)}) copy-start(f32[8,64,256]{2,1,0:T(8,128)S(1)} %collective-permute-done.7.refs_5_) | copy-start | bytes 1572868
  60.4 34.4 %collective-permute-start.9 = (f32[8,64,256]{2,1,0:T(8,128)S(1)}, f32[8,64,256]{2,1,0:T(8,128)}, u32[]{:S(2)}, u32[]{:S(2)}) collective-permute-start(f32[8,64,256]{2,1,0:T(8,128)S(1)} %collective-permute-done.6.refs_2_), channel_id=1, source_target_pairs={{0,192},{64,0},{128,64},{192,128},{1,193},{65,1},{129,65},{193,129... | collective-permute-start | bytes 1572872 | tf_op jit(solution)/shard_map/ppermute | solution.py:147
  62.8 22.1 %collective-permute-start.11 = (f32[8,64,256]{2,1,0:T(8,128)S(1)}, f32[8,64,256]{2,1,0:T(8,128)}, u32[]{:S(2)}, u32[]{:S(2)}) collective-permute-start(f32[8,64,256]{2,1,0:T(8,128)S(1)} %collective-permute-done.5.refs_4_), channel_id=1, source_target_pairs={{0,64},{64,128},{128,192},{192,0},{1,65},{65,129},{129,193},{193,1... | collective-permute-start | bytes 1572872 | tf_op jit(solution)/shard_map/ppermute | solution.py:147
  62.8 31.9 %collective-permute-start.12 = (f32[8,64,256]{2,1,0:T(8,128)S(1)}, f32[8,64,256]{2,1,0:T(8,128)}, u32[]{:S(2)}, u32[]{:S(2)}) collective-permute-start(f32[8,64,256]{2,1,0:T(8,128)S(1)} %collective-permute-done.7.refs_5_), channel_id=1, source_target_pairs={{0,16},{16,32},{32,48},{48,0},{1,17},{17,33},{33,49},{49,1},{2,18}... | collective-permute-start | bytes 1572872 | tf_op jit(solution)/shard_map/ppermute | solution.py:147
  83.6 14.9 %collective-permute-start.14 = (f32[8,64,256]{2,1,0:T(8,128)}, f32[8,64,256]{2,1,0:T(8,128)S(1)}, u32[]{:S(2)}, u32[]{:S(2)}) collective-permute-start(f32[8,64,256]{2,1,0:T(8,128)} %collective-permute-done.3.refs_3_), channel_id=1, source_target_pairs={{0,16},{16,32},{32,48},{48,0},{1,17},{17,33},{33,49},{49,1},{2,18}... | collective-permute-start | bytes 1572872 | tf_op jit(solution)/shard_map/ppermute | solution.py:147
  84.9 13.5 %collective-permute-start.13 = (f32[8,64,256]{2,1,0:T(8,128)S(1)}, f32[8,64,256]{2,1,0:T(8,128)S(1)}, u32[]{:S(2)}, u32[]{:S(2)}) collective-permute-start(f32[8,64,256]{2,1,0:T(8,128)S(1)} %collective-permute-done.7.refs_5_), channel_id=1, source_target_pairs={{0,192},{64,0},{128,64},{192,128},{1,193},{65,1},{129,65},{193,129... | collective-permute-start | bytes 1572872 | tf_op jit(solution)/shard_map/ppermute | solution.py:147
  87.4 12.9 %collective-permute-start.15 = (f32[8,64,256]{2,1,0:T(8,128)}, f32[8,64,256]{2,1,0:T(8,128)}, u32[]{:S(2)}, u32[]{:S(2)}) collective-permute-start(f32[8,64,256]{2,1,0:T(8,128)} %collective-permute-done.11.refs_8_), channel_id=1, source_target_pairs={{0,48},{16,0},{32,16},{48,32},{1,49},{17,1},{33,17},{49,33},{2,50}... | collective-permute-start | bytes 1572872 | tf_op jit(solution)/shard_map/ppermute | solution.py:147
  89.0 32.4 %all-to-all-start.1 = ((f32[16,64,256]{2,1,0:T(8,128)}), f32[16,64,256]{2,1,0:T(8,128)S(1)}, u32[]{:S(2)}, u32[]{:S(2)}) async-start(f32[16,64,256]{2,1,0:T(8,128)} %get-tuple-element.34), calls=%async_computation.1 | async-start | bytes 2097152 | tf_op jit(solution)/shard_map/all_to_all | solution.py:195
  122.4 76.4 %all-to-all-start.2 = ((f32[16,64,768]{2,1,0:T(8,128)}), f32[16,64,768]{2,1,0:T(8,128)S(1)}, u32[]{:S(2)}, u32[]{:S(2)}) async-start(f32[16,64,768]{2,1,0:T(8,128)} %get-tuple-element.38), calls=%async_computation.2 | async-start | bytes 6291456 | tf_op jit(solution)/shard_map/all_to_all | solution.py:195
  127.4 4.5 %collective-permute-start.16 = (f32[8,64,768]{2,1,0:T(8,128)}, f32[8,64,768]{2,1,0:T(8,128)}, u32[]{:S(2)}, u32[]{:S(2)}) collective-permute-start(f32[8,64,768]{2,1,0:T(8,128)} %get-tuple-element.37), channel_id=1, source_target_pairs={{0,8},{8,0},{1,9},{9,1},{2,10},{10,2},{3,11},{11,3},{4,12},{12,4},... | collective-permute-start | bytes 4718600 | tf_op jit(solution)/shard_map/ppermute | solution.py:196
  127.6 4.3 %collective-permute-start.8 = (f32[8,64,256]{2,1,0:T(8,128)}, f32[8,64,256]{2,1,0:T(8,128)}, u32[]{:S(2)}, u32[]{:S(2)}) collective-permute-start(f32[8,64,256]{2,1,0:T(8,128)} %get-tuple-element.24), channel_id=1, source_target_pairs={{0,8},{8,0},{1,9},{9,1},{2,10},{10,2},{3,11},{11,3},{4,12},{12,4},... | collective-permute-start | bytes 1572872 | tf_op jit(solution)/shard_map/ppermute | solution.py:196
  (6 other events, 47.9 us)
Sparse Core Ops, SparseCore 0:
  9.2 63.5 all-gather.2

commit v2 on v1

--- a/solution.py
+++ b/solution.py
@@ -18,7 +18,7 @@
 VMEM = pl.BlockSpec(memory_space=pltpu.VMEM)
 HBM = pl.BlockSpec(memory_space=pltpu.HBM)
 LIMIT = pltpu.CompilerParams(vmem_limit_bytes=60 * 2**20)
-COSTS = [pl.CostEstimate(flops=f * 10**9, transcendentals=0, bytes_accessed=f * 10**6) for f in (20, 40)]
+COSTS = [pl.CostEstimate(flops=f * 10**9, transcendentals=0, bytes_accessed=f * 10**6) for f in (60, 8)]
 FIRST = [
     ((1, 0), (1, 0)),
     ((-1, 0), (-1, 0)),
@@ -35,8 +35,8 @@
 ]
 LAST = [((2, -1), (1, 0)), ((-1, 2), (0, -1)), ((2, 2), (0, 1))]
 SETS = [
-    [(0, 0), (1, 0), (-1, 0), (0, 1)],
-    [(0, -1), (1, 1), (-1, -1), (-1, 1), (1, -1), (2, 0), (0, 2), (2, 1), (1, 2), (2, -1), (-1, 2), (2, 2)],
+    [(0, 0), (1, 0), (-1, 0), (0, 1), (0, -1), (1, 1), (-1, -1), (-1, 1)],
+    [(1, -1), (2, 0), (0, 2), (2, 1), (1, 2), (2, -1), (-1, 2), (2, 2)],
 ]
 SOON = [(1, 1), (-1, -1), (-1, 1), (1, -1)]
 PIECES = [(0, (0,)), (1, (0,))]
@@ -72,17 +72,28 @@
             a_hi[rows, cols], a_lo[rows, cols] = split(amps[g, s])
     height = occ * part
     dot = functools.partial(lax.dot_general, dimension_numbers=NT, preferred_element_type=jnp.float32)
-    for h in range(parts):
-        for c in range(CORES):
-            for s in range(DEPTH):
-                int_loads[(h * CORES + c) * DEPTH + s].wait()
-                cols = slice(s * width, (s + 1) * width)
-                i_hi[:, cols], i_lo[:, cols] = split(ints[h, c * DEPTH + s].reshape(height, width))
-            for m in range(0, height, BLOCK):
-                at = slice(m, m + BLOCK)
-                sums = dot(i_hi[at], a_lo[...]) + dot(i_lo[at], a_hi[...]) + dot(i_hi[at], a_hi[...])
-                at = slice(c * occ + m // part, c * occ + (m + BLOCK) // part)
-                out[at, h * part : (h + 1) * part, :] = sums.reshape(BLOCK // part, part, chips * panel)
+    groups = [(h, c) for h in range(parts) for c in range(CORES)]
+    blocks = height // BLOCK
+
+    def cut(n, s):
+        h, c = groups[n]
+        rows, cols = slice(n * height, (n + 1) * height), slice(s * width, (s + 1) * width)
+        i_hi[rows, cols], i_lo[rows, cols] = split(ints[h, c * DEPTH + s].reshape(height, width))
+
+    for s in range(DEPTH):
+        int_loads[s].wait()
+        cut(0, s)
+    for n, (h, c) in enumerate(groups):
+        more = n + 1 < len(groups)
+        for copy in int_loads[(n + 1) * DEPTH : (n + 2) * DEPTH] if more else []:
+            copy.wait()
+        for m in range(blocks):
+            at = slice(n * height + m * BLOCK, n * height + (m + 1) * BLOCK)
+            sums = dot(i_hi[at], a_lo[...]) + dot(i_lo[at], a_hi[...]) + dot(i_hi[at], a_hi[...])
+            at = slice(c * occ + m * BLOCK // part, c * occ + (m + 1) * BLOCK // part)
+            out[at, h * part : (h + 1) * part, :] = sums.reshape(BLOCK // part, part, chips * panel)
+            for s in range(m * DEPTH // blocks, (m + 1) * DEPTH // blocks) if more else []:
+                cut(n + 1, s)
     core = places[3]
     copies = [
         pltpu.make_async_copy(out, whole, out_sem.at[0]),
@@ -177,8 +188,8 @@
             scratch_shapes=[
                 pltpu.VMEM((parts, CORES * DEPTH, occ, part, width), f32),
                 pltpu.VMEM((len(chips), DEPTH, panel, width), f32),
-                pltpu.VMEM((occ * part, DEPTH * width), bf16),
-                pltpu.VMEM((occ * part, DEPTH * width), bf16),
+                pltpu.VMEM((CORES * occ * tall, DEPTH * width), bf16),
+                pltpu.VMEM((CORES * occ * tall, DEPTH * width), bf16),
                 pltpu.VMEM((size, DEPTH * width), bf16),
                 pltpu.VMEM((size, DEPTH * width), bf16),
                 pltpu.VMEM(both.shape, f32),
@@ -197,9 +208,11 @@
         places_of.append((starts[k], size, halves[0] * part, tall))
         if n + 1 < len(PIECES):
             int_all = list(lax.optimization_barrier(int_all + [own_all])[:HALVES])
-            bring(LAST, [own_all])
-    for pair_of, back in zip(arrays, mirror):
+            bring(LAST, [arrays[-1][1]])
+    for n, (pair_of, back) in enumerate(zip(arrays, mirror)):
         pair_of.append(back)
+        where = [pltpu.HBM, pltpu.HBM, pltpu.HBM if n + 1 < len(PIECES) else pltpu.VMEM]
+        arrays[n] = [pltpu.with_memory_space_constraint(*both) for both in zip(pair_of, where)]
 
     slots = [(chip, e) for e in range(CORES) for chips in sets for chip in chips]
     pair = (index[1] * SIDE + index[2]) * CORES + index[3]
@@ -217,7 +230,7 @@
             pltpu.SemaphoreType.DMA((occ, 2 * CORES * len(PIECES))),
             pltpu.SemaphoreType.DMA((occ,)),
         ],
-        compiler_params=pltpu.CompilerParams(vmem_limit_bytes=60 * 2**20),
+        compiler_params=pltpu.CompilerParams(vmem_limit_bytes=48 * 2**20),
         name="finish",
     )(places, panel_of, e_occ, e_b, e_vir.reshape(1, virtuals), *[a for group in arrays for a in group])
     return out[None]

time: 215 us -> 209 us (0.972)
  Pallas kernels: 37.9 us -> 35.2 us
  local copies, waits for them, and re-layouts: 4.11 us -> 1.57 us
    all_to_all x2, waiting for transfers between devices: 68.1 us -> 48.1 us  [body(): lax.all_to_all(whole, ('core', 'virt'), split_axis=0, concat_axis=0, tile...]
    ppermute x15, waiting for transfers between devices: 19.7 us -> 36.6 us  [move(): lax.ppermute(data, name, [(n, (n - step) % SIDE) for n in range(SIDE)])]
    all_gather x1, waiting for transfers between devices: 9.71 us -> 12.4 us  [body(): lax.all_gather(ints[:, h * part:(h + 1) * part], ('core', 'virt'), axis=0)]
  transfers between devices with their start and end apart: 20 -> 20, of which waited for: 9 -> 11; matrix products, arithmetic and copies ran while one was open for 1% -> 0% of each run, Pallas kernels for 14% -> 7%
where the time goes in v2:
time: 209 us
  waiting for transfers between devices  100 us (48%)
  Pallas kernels  35.2 us (17%)
  starting transfers between devices  31.7 us (15%)
  blocking collectives  26.2 us (13%)
  between operations  13.5 us (6%)
    all_to_all x2, waiting for transfers between devices, body(): lax.all_to_all(whole, ('core', 'virt'), split_axis=0, concat_axis=0, tile...  48.1 us
    ppermute x15, waiting for transfers between devices, move(): lax.ppermute(data, name, [(n, (n - step) % SIDE) for n in range(SIDE)])  36.6 us
    pallas_call x2, Pallas kernels, body(): pl.pallas_call(functools.partial(product_kernel, (occ, part, panel, width...  29.1 us
    all_to_all x1, blocking collectives, body(): lax.all_to_all(amps, 'virt', split_axis=0, concat_axis=0, tiled=True)  26.2 us
    ppermute x15, starting transfers between devices, move(): lax.ppermute(data, name, [(n, (n - step) % SIDE) for n in range(SIDE)])  20.3 us
    all_gather x1, waiting for transfers between devices, body(): lax.all_gather(ints[:, h * part:(h + 1) * part], ('core', 'virt'), axis=0)  12.4 us
    all_to_all x2, starting transfers between devices, body(): lax.all_to_all(whole, ('core', 'virt'), split_axis=0, concat_axis=0, tile...  11 us
    pallas_call x1, Pallas kernels, body(): pl.pallas_call(functools.partial(finish_kernel, (occ, panel, virtuals), p...  6.11 us
  transfers between devices with their start and end apart: 20, of which 11 were waited for; matrix products, arithmetic and copies ran while one was open for 0% of the time, Pallas kernels for 7%

profile of v2, /device:TPU:1, one launch (start us, length us, event | category | flops | bytes accessed | tf_op | source)
XLA Modules:
  0.0 209.0 jit_solution(9859941415305043891)
XLA Ops:
  7.3 26.2 %all_to_all.15.refs_1_ = f32[8,64,256]{2,1,0:T(8,128)S(1)} all-to-all(f32[8,64,256]{2,1,0:T(8,128)} %param.5), channel_id=1, replica_groups=mesh['x'=4,'y'=4,'core'=2,'virt'=8] {'virt'}, dimensions={0} | all-to-all | bytes 1048576 | tf_op jit(solution)/shard_map/all_to_all | solution.py:161
  33.4 2.5 %collective-permute-start.6 = (f32[8,64,256]{2,1,0:T(8,128)S(1)}, f32[8,64,256]{2,1,0:T(8,128)S(1)}, u32[]{:S(2)}, u32[]{:S(2)}) collective-permute-start(f32[8,64,256]{2,1,0:T(8,128)S(1)} %all_to_all.15.refs_1_), channel_id=1, source_target_pairs={{0,192},{64,0},{128,64},{192,128},{1,193},{65,1},{129,65},{193,129... | collective-permute-start | bytes 1572872 | tf_op jit(solution)/shard_map/ppermute | solution.py:158
  35.9 2.9 %collective-permute-start = (f32[8,64,256]{2,1,0:T(8,128)S(1)}, f32[8,64,256]{2,1,0:T(8,128)S(1)}, u32[]{:S(2)}, u32[]{:S(2)}) collective-permute-start(f32[8,64,256]{2,1,0:T(8,128)S(1)} %all_to_all.15.refs_1_), channel_id=1, source_target_pairs={{0,48},{16,0},{32,16},{48,32},{1,49},{17,1},{33,17},{49,33},{2,50}... | collective-permute-start | bytes 1572872 | tf_op jit(solution)/shard_map/ppermute | solution.py:158
  38.8 4.5 %collective-permute-done.6.refs_2_ = f32[8,64,256]{2,1,0:T(8,128)S(1)} collective-permute-done((f32[8,64,256]{2,1,0:T(8,128)S(1)}, f32[8,64,256]{2,1,0:T(8,128)S(1)}, u32[]{:S(2)}, u32[]{:S(2)}) %collective-permute-start.6) | collective-permute-done | bytes 524320 | tf_op jit(solution)/shard_map/ppermute | solution.py:158
  43.3 1.4 collective-permute-start.7
  44.7 1.3 collective-permute-done.refs_4_
  45.9 2.3 %collective-permute-start.1 = (f32[8,64,256]{2,1,0:T(8,128)S(1)}, f32[8,64,256]{2,1,0:T(8,128)}, u32[]{:S(2)}, u32[]{:S(2)}) collective-permute-start(f32[8,64,256]{2,1,0:T(8,128)S(1)} %collective-permute-done.refs_4_), channel_id=1, source_target_pairs={{0,192},{64,0},{128,64},{192,128},{1,193},{65,1},{129,65},{193,129... | collective-permute-start | bytes 1572872 | tf_op jit(solution)/shard_map/ppermute | solution.py:158
  51.5 8.9 %collective-permute-done.7.refs_1_ = f32[8,64,256]{2,1,0:T(8,128)S(1)} collective-permute-done((f32[8,64,256]{2,1,0:T(8,128)S(1)}, f32[8,64,256]{2,1,0:T(8,128)S(1)}, u32[]{:S(2)}, u32[]{:S(2)}) %collective-permute-start.7) | collective-permute-done | bytes 524320 | tf_op jit(solution)/shard_map/ppermute | solution.py:158
  60.4 12.4 %all-gather.3.cloned.1.call-done = f32[128,64,256]{2,1,0:T(8,128)} async-done(((f32[8,64,256]{2,1,0:T(8,128)}), f32[128,64,256]{2,1,0:T(8,128)}) %all-gather.3.cloned.1.call-update) | async-done | bytes 8388624 | tf_op jit(solution)/shard_map/all_gather | solution.py:160
  72.8 14.6 %product_0.1 = (f32[8,64,512]{2,1,0:T(8,128)}, f32[8,64,512]{2,1,0:T(8,128)}, f32[16,64,512]{2,1,0:T(8,128)}) custom-call(s32[4]{0:T(128)} %pad_add_fusion.places, f32[16,8,64,256]{3,2,1,0:T(8,128)} %bitcast.10, f32[8,64,256]{2,1,0:T(8,128)} %copy-done.7, f32[8,64,256]{2,1,0:T(8,128)} %copy-done.9, f32[8,64,256]{2,1,0:T(8,128)} %collective-permute-done.4.refs_3_, ...), custom_call_target="tpu_custom_call" | custom-call | flops 60000002048 | bytes 60000000 | tf_op jit(solution)/shard_map/product_0/pallas_call | solution.py:183
  87.5 4.8 %all-to-all-start.1 = ((f32[16,64,512]{2,1,0:T(8,128)}), f32[16,64,512]{2,1,0:T(8,128)S(1)}, u32[]{:S(2)}, u32[]{:S(2)}) async-start(f32[16,64,512]{2,1,0:T(8,128)} %get-tuple-element.34), calls=%async_computation.1 | async-start | bytes 4194304 | tf_op jit(solution)/shard_map/all_to_all | solution.py:206
  93.7 2.7 %collective-permute-start.10 = (f32[8,64,256]{2,1,0:T(8,128)}, f32[8,64,256]{2,1,0:T(8,128)}, u32[]{:S(2)}, u32[]{:S(2)}) collective-permute-start(f32[8,64,256]{2,1,0:T(8,128)} %copy-done.10), channel_id=1, source_target_pairs={{0,48},{16,0},{32,16},{48,32},{1,49},{17,1},{33,17},{49,33},{2,50}... | collective-permute-start | bytes 1572872 | tf_op jit(solution)/shard_map/ppermute | solution.py:158
  96.4 1.5 collective-permute-start.9
  98.0 9.2 %collective-permute-done.11.refs_4_ = f32[8,64,256]{2,1,0:T(8,128)S(1)} collective-permute-done((f32[8,64,256]{2,1,0:T(8,128)}, f32[8,64,256]{2,1,0:T(8,128)S(1)}, u32[]{:S(2)}, u32[]{:S(2)}) %collective-permute-start.11) | collective-permute-done | bytes 524320 | tf_op jit(solution)/shard_map/ppermute | solution.py:158
  107.2 1.3 collective-permute-start.13
  108.5 2.7 %collective-permute-start.15 = (f32[8,64,256]{2,1,0:T(8,128)S(1)}, f32[8,64,256]{2,1,0:T(8,128)}, u32[]{:S(2)}, u32[]{:S(2)}) collective-permute-start(f32[8,64,256]{2,1,0:T(8,128)S(1)} %collective-permute-done.11.refs_4_), channel_id=1, source_target_pairs={{0,48},{16,0},{32,16},{48,32},{1,49},{17,1},{33,17},{49,33},{2,50}... | collective-permute-start | bytes 1572872 | tf_op jit(solution)/shard_map/ppermute | solution.py:158
  111.7 11.2 %collective-permute-done.14.refs_7_ = f32[8,64,256]{2,1,0:T(8,128)} collective-permute-done((f32[8,64,256]{2,1,0:T(8,128)}, f32[8,64,256]{2,1,0:T(8,128)}, u32[]{:S(2)}, u32[]{:S(2)}) %collective-permute-start.14) | collective-permute-done | bytes 524320 | tf_op jit(solution)/shard_map/ppermute | solution.py:158
  122.9 14.5 %product_1.1 = (f32[8,64,512]{2,1,0:T(8,128)}, f32[8,64,512]{2,1,0:T(8,128)}, f32[16,64,512]{2,1,0:T(8,128)}) custom-call(s32[4]{0:T(128)} %pad_add_fusion.places, f32[16,8,64,256]{3,2,1,0:T(8,128)} %bitcast.11, f32[8,64,256]{2,1,0:T(8,128)} %copy-done.8, f32[8,64,256]{2,1,0:T(8,128)} %collective-permute-done.9.refs_2_, ...), custom_call_target="tpu_custom_call" | custom-call | flops 8000000000 | bytes 8000000 | tf_op jit(solution)/shard_map/product_1/pallas_call | solution.py:183
  137.5 2.9 %all-to-all-done.1.refs_2_ = f32[16,64,512]{2,1,0:T(8,128)S(1)} async-done(((f32[16,64,512]{2,1,0:T(8,128)}), f32[16,64,512]{2,1,0:T(8,128)S(1)}, u32[]{:S(2)}, u32[]{:S(2)}) %all-to-all-start.1) | async-done | bytes 2097184 | tf_op jit(solution)/shard_map/all_to_all | solution.py:206
  140.4 1.3 copy-done.4
  141.7 6.2 %all-to-all-start.2 = ((f32[16,64,512]{2,1,0:T(8,128)}), f32[16,64,512]{2,1,0:T(8,128)S(1)}, u32[]{:S(2)}, u32[]{:S(2)}) async-start(f32[16,64,512]{2,1,0:T(8,128)} %get-tuple-element.38), calls=%async_computation.2 | async-start | bytes 4194304 | tf_op jit(solution)/shard_map/all_to_all | solution.py:206
  148.3 2.5 %collective-permute-done.16.refs_4_ = f32[8,64,512]{2,1,0:T(8,128)S(1)} collective-permute-done((f32[8,64,512]{2,1,0:T(8,128)}, f32[8,64,512]{2,1,0:T(8,128)S(1)}, u32[]{:S(2)}, u32[]{:S(2)}) %collective-permute-start.16) | collective-permute-done | bytes 1048608 | tf_op jit(solution)/shard_map/ppermute | solution.py:207
  150.8 45.2 %all-to-all-done.2.refs_5_ = f32[16,64,512]{2,1,0:T(8,128)S(1)} async-done(((f32[16,64,512]{2,1,0:T(8,128)}), f32[16,64,512]{2,1,0:T(8,128)S(1)}, u32[]{:S(2)}, u32[]{:S(2)}) %all-to-all-start.2) | async-done | bytes 2097184 | tf_op jit(solution)/shard_map/all_to_all | solution.py:206
  196.0 6.1 %finish.1 = f32[8,64,2048]{2,1,0:T(8,128)} custom-call(s32[4]{0:T(128)S(1)} %copy-done.1, s32[32]{0:T(128)S(1)} %copy-done.2, f32[8]{0:T(128)S(1)} %copy-done.3, f32[64,1]{1,0:T(8,128)S(1)} %copy.7.e_b, f32[1,2048]{1,0:T(1,128)S(1)} %bitcast.9, f32[8,64,512]{2,1,0:T(8,128)} %get-tuple-element.26.refs_0_, f32[8,64,512]{2,1,0:T(8,128)} %copy-done.5, ...), custom_call_target="tpu_custom_call" | custom-call | tf_op jit(solution)/shard_map/finish/pallas_call | solution.py:220
  (52 shorter events, 6.4 us)
Async XLA Ops:
  6.5 66.3 %all-gather.3.cloned.1.call-start = ((), (), s32[]{:S(2)}) async-start(), calls=%async_computation.3 | async-start | bytes 8912896 | tf_op jit(solution)/shard_map/all_gather | solution.py:160
  33.4 9.9 %collective-permute-start.6 = (f32[8,64,256]{2,1,0:T(8,128)S(1)}, f32[8,64,256]{2,1,0:T(8,128)S(1)}, u32[]{:S(2)}, u32[]{:S(2)}) collective-permute-start(f32[8,64,256]{2,1,0:T(8,128)S(1)} %all_to_all.15.refs_1_), channel_id=1, source_target_pairs={{0,192},{64,0},{128,64},{192,128},{1,193},{65,1},{129,65},{193,129... | collective-permute-start | bytes 1572872 | tf_op jit(solution)/shard_map/ppermute | solution.py:158
  35.9 10.0 %collective-permute-start = (f32[8,64,256]{2,1,0:T(8,128)S(1)}, f32[8,64,256]{2,1,0:T(8,128)S(1)}, u32[]{:S(2)}, u32[]{:S(2)}) collective-permute-start(f32[8,64,256]{2,1,0:T(8,128)S(1)} %all_to_all.15.refs_1_), channel_id=1, source_target_pairs={{0,48},{16,0},{32,16},{48,32},{1,49},{17,1},{33,17},{49,33},{2,50}... | collective-permute-start | bytes 1572872 | tf_op jit(solution)/shard_map/ppermute | solution.py:158
  38.8 10.3 %collective-permute-start.4 = (f32[8,64,256]{2,1,0:T(8,128)S(1)}, f32[8,64,256]{2,1,0:T(8,128)}, u32[]{:S(2)}, u32[]{:S(2)}) collective-permute-start(f32[8,64,256]{2,1,0:T(8,128)S(1)} %all_to_all.15.refs_1_), channel_id=1, source_target_pairs={{0,64},{64,128},{128,192},{192,0},{1,65},{65,129},{129,193},{193,1... | collective-permute-start | bytes 1572872 | tf_op jit(solution)/shard_map/ppermute | solution.py:158
  38.8 11.2 %collective-permute-start.2 = (f32[8,64,256]{2,1,0:T(8,128)S(1)}, f32[8,64,256]{2,1,0:T(8,128)}, u32[]{:S(2)}, u32[]{:S(2)}) collective-permute-start(f32[8,64,256]{2,1,0:T(8,128)S(1)} %all_to_all.15.refs_1_), channel_id=1, source_target_pairs={{0,16},{16,32},{32,48},{48,0},{1,17},{17,33},{33,49},{49,1},{2,18}... | collective-permute-start | bytes 1572872 | tf_op jit(solution)/shard_map/ppermute | solution.py:158
  43.3 17.1 %collective-permute-start.7 = (f32[8,64,256]{2,1,0:T(8,128)S(1)}, f32[8,64,256]{2,1,0:T(8,128)S(1)}, u32[]{:S(2)}, u32[]{:S(2)}) collective-permute-start(f32[8,64,256]{2,1,0:T(8,128)S(1)} %collective-permute-done.6.refs_2_), channel_id=1, source_target_pairs={{0,16},{16,32},{32,48},{48,0},{1,17},{17,33},{33,49},{49,1},{2,18}... | collective-permute-start | bytes 1572872 | tf_op jit(solution)/shard_map/ppermute | solution.py:158
  45.9 14.5 %collective-permute-start.1 = (f32[8,64,256]{2,1,0:T(8,128)S(1)}, f32[8,64,256]{2,1,0:T(8,128)}, u32[]{:S(2)}, u32[]{:S(2)}) collective-permute-start(f32[8,64,256]{2,1,0:T(8,128)S(1)} %collective-permute-done.refs_4_), channel_id=1, source_target_pairs={{0,192},{64,0},{128,64},{192,128},{1,193},{65,1},{129,65},{193,129... | collective-permute-start | bytes 1572872 | tf_op jit(solution)/shard_map/ppermute | solution.py:158
  49.2 11.2 %collective-permute-start.5 = (f32[8,64,256]{2,1,0:T(8,128)}, f32[8,64,256]{2,1,0:T(8,128)S(1)}, u32[]{:S(2)}, u32[]{:S(2)}) collective-permute-start(f32[8,64,256]{2,1,0:T(8,128)} %collective-permute-done.4.refs_3_), channel_id=1, source_target_pairs={{0,48},{16,0},{32,16},{48,32},{1,49},{17,1},{33,17},{49,33},{2,50}... | collective-permute-start | bytes 1572872 | tf_op jit(solution)/shard_map/ppermute | solution.py:158
  50.0 10.4 %collective-permute-start.3 = (f32[8,64,256]{2,1,0:T(8,128)}, f32[8,64,256]{2,1,0:T(8,128)S(1)}, u32[]{:S(2)}, u32[]{:S(2)}) collective-permute-start(f32[8,64,256]{2,1,0:T(8,128)} %collective-permute-done.2.refs_5_), channel_id=1, source_target_pairs={{0,64},{64,128},{128,192},{192,0},{1,65},{65,129},{129,193},{193,1... | collective-permute-start | bytes 1572872 | tf_op jit(solution)/shard_map/ppermute | solution.py:158
  87.5 52.9 %all-to-all-start.1 = ((f32[16,64,512]{2,1,0:T(8,128)}), f32[16,64,512]{2,1,0:T(8,128)S(1)}, u32[]{:S(2)}, u32[]{:S(2)}) async-start(f32[16,64,512]{2,1,0:T(8,128)} %get-tuple-element.34), calls=%async_computation.1 | async-start | bytes 4194304 | tf_op jit(solution)/shard_map/all_to_all | solution.py:206
  92.3 5.6 %collective-permute-start.8 = (f32[8,64,512]{2,1,0:T(8,128)}, f32[8,64,512]{2,1,0:T(8,128)S(1)}, u32[]{:S(2)}, u32[]{:S(2)}) collective-permute-start(f32[8,64,512]{2,1,0:T(8,128)} %get-tuple-element.27), channel_id=1, source_target_pairs={{0,8},{8,0},{1,9},{9,1},{2,10},{10,2},{3,11},{11,3},{4,12},{12,4},... | collective-permute-start | bytes 3145736 | tf_op jit(solution)/shard_map/ppermute | solution.py:207
  92.5 14.7 %collective-permute-start.11 = (f32[8,64,256]{2,1,0:T(8,128)}, f32[8,64,256]{2,1,0:T(8,128)S(1)}, u32[]{:S(2)}, u32[]{:S(2)}) collective-permute-start(f32[8,64,256]{2,1,0:T(8,128)} %copy-done.12), channel_id=1, source_target_pairs={{0,64},{64,128},{128,192},{192,0},{1,65},{65,129},{129,193},{193,1... | collective-permute-start | bytes 1572872 | tf_op jit(solution)/shard_map/ppermute | solution.py:158
  93.7 14.8 %collective-permute-start.10 = (f32[8,64,256]{2,1,0:T(8,128)}, f32[8,64,256]{2,1,0:T(8,128)}, u32[]{:S(2)}, u32[]{:S(2)}) collective-permute-start(f32[8,64,256]{2,1,0:T(8,128)} %copy-done.10), channel_id=1, source_target_pairs={{0,48},{16,0},{32,16},{48,32},{1,49},{17,1},{33,17},{49,33},{2,50}... | collective-permute-start | bytes 1572872 | tf_op jit(solution)/shard_map/ppermute | solution.py:158
  96.4 14.8 %collective-permute-start.9 = (f32[8,64,256]{2,1,0:T(8,128)}, f32[8,64,256]{2,1,0:T(8,128)}, u32[]{:S(2)}, u32[]{:S(2)}) collective-permute-start(f32[8,64,256]{2,1,0:T(8,128)} %copy-done.9), channel_id=1, source_target_pairs={{0,192},{64,0},{128,64},{192,128},{1,193},{65,1},{129,65},{193,129... | collective-permute-start | bytes 1572872 | tf_op jit(solution)/shard_map/ppermute | solution.py:158
  97.9 13.8 %collective-permute-start.12 = (f32[8,64,256]{2,1,0:T(8,128)}, f32[8,64,256]{2,1,0:T(8,128)}, u32[]{:S(2)}, u32[]{:S(2)}) collective-permute-start(f32[8,64,256]{2,1,0:T(8,128)} %copy-done.8), channel_id=1, source_target_pairs={{0,16},{16,32},{32,48},{48,0},{1,17},{17,33},{33,49},{49,1},{2,18}... | collective-permute-start | bytes 1572872 | tf_op jit(solution)/shard_map/ppermute | solution.py:158
  97.9 25.0 %collective-permute-start.14 = (f32[8,64,256]{2,1,0:T(8,128)}, f32[8,64,256]{2,1,0:T(8,128)}, u32[]{:S(2)}, u32[]{:S(2)}) collective-permute-start(f32[8,64,256]{2,1,0:T(8,128)} %copy-done.11), channel_id=1, source_target_pairs={{0,16},{16,32},{32,48},{48,0},{1,17},{17,33},{33,49},{49,1},{2,18}... | collective-permute-start | bytes 1572872 | tf_op jit(solution)/shard_map/ppermute | solution.py:158
  107.2 15.7 %collective-permute-start.13 = (f32[8,64,256]{2,1,0:T(8,128)}, f32[8,64,256]{2,1,0:T(8,128)}, u32[]{:S(2)}, u32[]{:S(2)}) collective-permute-start(f32[8,64,256]{2,1,0:T(8,128)} %copy-done.8), channel_id=1, source_target_pairs={{0,192},{64,0},{128,64},{192,128},{1,193},{65,1},{129,65},{193,129... | collective-permute-start | bytes 1572872 | tf_op jit(solution)/shard_map/ppermute | solution.py:158
  108.5 14.4 %collective-permute-start.15 = (f32[8,64,256]{2,1,0:T(8,128)S(1)}, f32[8,64,256]{2,1,0:T(8,128)}, u32[]{:S(2)}, u32[]{:S(2)}) collective-permute-start(f32[8,64,256]{2,1,0:T(8,128)S(1)} %collective-permute-done.11.refs_4_), channel_id=1, source_target_pairs={{0,48},{16,0},{32,16},{48,32},{1,49},{17,1},{33,17},{49,33},{2,50}... | collective-permute-start | bytes 1572872 | tf_op jit(solution)/shard_map/ppermute | solution.py:158
  140.4 55.7 %copy-start.1 = (s32[4]{0:T(128)S(1)}, s32[4]{0:T(128)}, u32[]{:S(2)}) copy-start(s32[4]{0:T(128)} %pad_add_fusion.places) | copy-start | bytes 52
  140.4 55.7 %copy-start.2 = (s32[32]{0:T(128)S(1)}, s32[32]{0:T(128)}, u32[]{:S(2)}) copy-start(s32[32]{0:T(128)} %panel_of.1) | copy-start | bytes 388
  140.4 55.7 %copy-start.3 = (f32[8]{0:T(128)S(1)}, f32[8]{0:T(128)}, u32[]{:S(2)}) copy-start(f32[8]{0:T(128)} %e_occ.1) | copy-start | bytes 100
  141.7 54.3 %all-to-all-start.2 = ((f32[16,64,512]{2,1,0:T(8,128)}), f32[16,64,512]{2,1,0:T(8,128)S(1)}, u32[]{:S(2)}, u32[]{:S(2)}) async-start(f32[16,64,512]{2,1,0:T(8,128)} %get-tuple-element.38), calls=%async_computation.2 | async-start | bytes 4194304 | tf_op jit(solution)/shard_map/all_to_all | solution.py:206
  147.9 2.9 %collective-permute-start.16 = (f32[8,64,512]{2,1,0:T(8,128)}, f32[8,64,512]{2,1,0:T(8,128)S(1)}, u32[]{:S(2)}, u32[]{:S(2)}) collective-permute-start(f32[8,64,512]{2,1,0:T(8,128)} %get-tuple-element.37), channel_id=1, source_target_pairs={{0,8},{8,0},{1,9},{9,1},{2,10},{10,2},{3,11},{11,3},{4,12},{12,4},... | collective-permute-start | bytes 3145736 | tf_op jit(solution)/shard_map/ppermute | solution.py:207
  150.8 45.2 %copy-start.6 = (f32[8,64,512]{2,1,0:T(8,128)}, f32[8,64,512]{2,1,0:T(8,128)S(1)}, u32[]{:S(2)}) copy-start(f32[8,64,512]{2,1,0:T(8,128)S(1)} %collective-permute-done.16.refs_4_) | copy-start | bytes 3145732
  (10 other events, 212.1 us)
Sparse Core Ops, SparseCore 0:
  9.2 63.5 all-gather.2

commit v3 on v2

v3 whole, which is shorter than its diff:
```python
import functools

import jax
import jax.numpy as jnp
from jax import lax
from jax.experimental import pallas as pl
from jax.experimental.pallas import tpu as pltpu
from jax.sharding import Mesh, PartitionSpec as P

SIDE = 4
CORES = 2
DEPTH = 8
BLOCK = 256
NT = (((1,), (1,)), ((), ()))
SMEM = pl.BlockSpec(memory_space=pltpu.SMEM)
ANY = pl.BlockSpec(memory_space=pl.ANY)
VMEM = pl.BlockSpec(memory_space=pltpu.VMEM)
COSTS = [pl.CostEstimate(flops=f * 10**9, transcendentals=0, bytes_accessed=f * 10**6) for f in (60, 8)]
FIRST = [
    ((1, 0), (1, 0)),
    ((-1, 0), (-1, 0)),
    ((0, 1), (0, 1)),
    ((0, -1), (0, -1)),
    ((1, 1), (1, 0)),
    ((-1, -1), (-1, 0)),
    ((-1, 1), (0, 1)),
    ((1, -1), (0, -1)),
    ((2, 0), (1, 0)),
    ((0, 2), (0, 1)),
    ((2, 1), (-1, 0)),
    ((1, 2), (0, -1)),
]
LAST = [((2, -1), (1, 0)), ((-1, 2), (0, -1)), ((2, 2), (0, 1))]
SETS = [
    [(0, 0), (1, 0), (-1, 0), (0, 1), (0, -1), (1, 1), (-1, -1), (-1, 1)],
    [(1, -1), (2, 0), (0, 2), (2, 1), (1, 2), (2, -1), (-1, 2), (2, 2)],
]
EARLY = [(1, -1), (2, 0)]


def wrap(x, y):
    return x % SIDE, y % SIDE


def split(x):
    high = x.astype(jnp.bfloat16)
    return high, (x - high.astype(jnp.float32)).astype(jnp.bfloat16)


def split_kernel(dims, *refs):
    panel, width, chips = dims
    amps_hbm = refs[:chips]
    a_hi, a_lo, amps, amp_sem = refs[chips:]
    loads = [pltpu.make_async_copy(amps_hbm[g], amps.at[g], amp_sem.at[g]) for g in range(chips)]
    for copy in loads:
        copy.start()
    for g in range(chips):
        loads[g].wait()
        rows = slice(g * panel, (g + 1) * panel)
        for s in range(DEPTH):
            cols = slice(s * width, (s + 1) * width)
            a_hi[rows, cols], a_lo[rows, cols] = split(amps[g, s])


def product_kernel(dims, ints_hbm, a_hi, a_lo, whole, ints, i_hi, i_lo, out, int_sem, out_sem):
    occ, panel, width = dims
    loads = [pltpu.make_async_copy(ints_hbm.at[s], ints.at[s], int_sem.at[s]) for s in range(CORES * DEPTH)]
    for copy in loads:
        copy.start()
    height = occ * panel
    blocks = height // BLOCK
    dot = functools.partial(lax.dot_general, dimension_numbers=NT, preferred_element_type=jnp.float32)

    def cut(c, s):
        rows, cols = slice(c * height, (c + 1) * height), slice(s * width, (s + 1) * width)
        i_hi[rows, cols], i_lo[rows, cols] = split(ints[c * DEPTH + s].reshape(height, width))

    for s in range(DEPTH):
        loads[s].wait()
        cut(0, s)
    for copy in loads[DEPTH:]:
        copy.wait()
    stores = []
    for c in range(CORES):
        for m in range(blocks):
            at = slice(c * height + m * BLOCK, c * height + (m + 1) * BLOCK)
            sums = dot(i_hi[at], a_lo[...]) + dot(i_lo[at], a_hi[...]) + dot(i_hi[at], a_hi[...])
            at = slice(at.start // panel, at.stop // panel)
            out[at] = sums.reshape(BLOCK // panel, panel, -1)
            stores.append(pltpu.make_async_copy(out.at[at], whole.at[at], out_sem.at[len(stores)]))
            stores[-1].start()
            for s in range(m * DEPTH // blocks, (m + 1) * DEPTH // blocks) if c == 0 else []:
                cut(1, s)
    for copy in stores:
        copy.wait()


def finish_kernel(dims, pieces, slots, places, panel_of, e_occ, e_b, e_vir, *refs):
    occ, panel, virtuals = dims
    out_hbm, slot_of, dir_v, mir_v, out_v, in_sem, out_sem = refs[3 * len(pieces) :]
    v, x, y, core = places[0], places[1], places[2], places[3]
    loads = []
    for j in range(occ):
        mine = []
        for n, (first, size) in enumerate(pieces):
            own, other, mirror = refs[3 * n : 3 * n + 3]
            for e in range(CORES):
                at = (j, slice(None), pl.ds(e * virtuals // 2 + first, size))
                mine.append(((other if e else own).at[core * occ + j], dir_v.at[at]))
                mine.append((mirror.at[lax.rem(core + e, CORES) * occ + j], mir_v.at[at]))
        loads.append([pltpu.make_async_copy(a, b, in_sem.at[j, n]) for n, (a, b) in enumerate(mine)])
        for copy in loads[j]:
            copy.start()
    for s, ((dx, dy), e) in enumerate(slots):
        chip = lax.rem(x + dx, SIDE) * SIDE + lax.rem(y + dy, SIDE)
        slot_of[panel_of[chip * CORES + lax.rem(core + e, CORES)]] = s
    lanes = 2 * panel
    lane = lax.broadcasted_iota(jnp.int32, (panel, lanes), 1)
    for j in range(occ):
        for copy in loads[j]:
            copy.wait()
        base = (e_occ[v] + e_occ[j]) - e_b[...]
        for t in range(virtuals // lanes):
            sides = []
            for h in range(2):
                s = slot_of[2 * t + h]
                cols = pl.ds(pl.multiple_of((s // 2) * lanes, lanes), lanes)
                diff = dir_v[j, :, cols] - mir_v[j, :, cols]
                sides.append(pltpu.roll(diff, lax.rem(s + h, 2) * panel, 1))
            cols = slice(t * lanes, (t + 1) * lanes)
            out_v[j, :, cols] = jnp.where(lane < panel, sides[0], sides[1]) / (base - e_vir[:, cols])
        pltpu.make_async_copy(out_v.at[j], out_hbm.at[j], out_sem.at[j]).start()
    for j in range(occ):
        pltpu.make_async_copy(out_v.at[j], out_hbm.at[j], out_sem.at[j]).wait()


def body(amps, ints, panel_of, e_occ, e_vir):
    occ, panel, width = amps.shape
    virtuals = e_vir.shape[0]
    f32, bf16 = jnp.float32, jnp.bfloat16
    index = [lax.axis_index(name).astype(jnp.int32) for name in ("virt", "x", "y", "core")]
    places = jnp.stack(index)

    def move(data, dx, dy):
        name, step = ("x", dx) if dx else ("y", dy)
        return lax.ppermute(data, name, [(n, (n - step) % SIDE) for n in range(SIDE)])

    int_all = lax.all_gather(ints, ("core", "virt"), axis=0)
    held = {(0, 0): lax.all_to_all(amps, "virt", split_axis=0, concat_axis=0, tiled=True)}
    sets = [[wrap(*chip) for chip in chips] for chips in SETS]
    starts = [sum(map(len, sets[:k])) * panel for k in range(len(sets))]

    def bring(routes, after=()):
        for to, (dx, dy) in routes:
            data = held[wrap(to[0] - dx, to[1] - dy)]
            if after:
                data = lax.optimization_barrier([data, *after])[0]
            held[wrap(*to)] = move(data, dx, dy)

    bring(FIRST)
    arrays, places_of = [], []
    for n, chips in enumerate(sets):
        size = len(chips) * panel
        height = occ * panel
        wide = jax.ShapeDtypeStruct((size, DEPTH * width), bf16)
        parts = pl.pallas_call(
            functools.partial(split_kernel, (panel, width, len(chips))),
            out_shape=[wide, wide],
            in_specs=[ANY] * len(chips),
            out_specs=[VMEM, VMEM],
            scratch_shapes=[
                pltpu.VMEM((len(chips), DEPTH, panel, width), f32),
                pltpu.SemaphoreType.DMA((len(chips),)),
            ],
            compiler_params=pltpu.CompilerParams(vmem_limit_bytes=24 * 2**20),
            cost_estimate=COSTS[n],
            name=f"split_{n}",
        )(*[pltpu.with_memory_space_constraint(held[chip], pltpu.HBM) for chip in chips])
        if n == 0:
            early = [held[wrap(*chip)] for chip in EARLY]
            int_all, *parts = lax.optimization_barrier([int_all, *parts, *early])[: 1 + len(parts)]
        parts = [pltpu.with_memory_space_constraint(part, pltpu.VMEM) for part in parts]
        both = pltpu.HBM((CORES * occ, panel, size), f32)
        whole = pl.pallas_call(
            functools.partial(product_kernel, (occ, panel, width)),
            out_shape=both,
            in_specs=[ANY, VMEM, VMEM],
            out_specs=ANY,
            scratch_shapes=[
                pltpu.VMEM((CORES * DEPTH, occ, panel, width), f32),
                pltpu.VMEM((CORES * height, DEPTH * width), bf16),
                pltpu.VMEM((CORES * height, DEPTH * width), bf16),
                pltpu.VMEM(both.shape, f32),
                pltpu.SemaphoreType.DMA((CORES * DEPTH,)),
                pltpu.SemaphoreType.DMA((CORES * height // BLOCK,)),
            ],
            compiler_params=pltpu.CompilerParams(vmem_limit_bytes=36 * 2**20),
            cost_estimate=COSTS[n],
            name=f"product_{n}",
        )(pltpu.with_memory_space_constraint(int_all, pltpu.HBM), *parts)
        sent = lax.optimization_barrier([whole, arrays[-1][2]])[0] if arrays else whole
        swapped = lax.ppermute(whole, "core", [(0, 1), (1, 0)])
        mirror = lax.all_to_all(sent, ("core", "virt"), split_axis=0, concat_axis=0, tiled=True)
        arrays.append([whole, swapped, mirror])
        places_of.append((starts[n], size))
        if n == 0:
            int_all = lax.optimization_barrier([int_all, whole])[0]
            bring(LAST, [swapped])
    where = [pltpu.HBM, pltpu.HBM, pltpu.VMEM]
    arrays = [[pltpu.with_memory_space_constraint(*both) for both in zip(group, where)] for group in arrays]

    slots = [(chip, e) for e in range(CORES) for chips in sets for chip in chips]
    pair = (index[1] * SIDE + index[2]) * CORES + index[3]
    e_b = lax.dynamic_slice(e_vir, (pair * panel,), (panel,)).reshape(panel, 1)
    out = pl.pallas_call(
        functools.partial(finish_kernel, (occ, panel, virtuals), places_of, slots),
        out_shape=jax.ShapeDtypeStruct((occ, panel, virtuals), f32),
        in_specs=[SMEM, SMEM, SMEM, VMEM, VMEM] + [ANY, ANY, VMEM] * len(sets),
        out_specs=ANY,
        scratch_shapes=[
            pltpu.SMEM((virtuals // panel,), jnp.int32),
            pltpu.VMEM((occ, panel, virtuals), f32),
            pltpu.VMEM((occ, panel, virtuals), f32),
            pltpu.VMEM((occ, panel, virtuals), f32),
            pltpu.SemaphoreType.DMA((occ, 2 * CORES * len(sets))),
            pltpu.SemaphoreType.DMA((occ,)),
        ],
        compiler_params=pltpu.CompilerParams(vmem_limit_bytes=48 * 2**20),
        name="finish",
    )(places, panel_of, e_occ, e_b, e_vir.reshape(1, virtuals), *[a for group in arrays for a in group])
    return out[None]


def solution(mesh):
    fine = Mesh(mesh.devices.reshape(SIDE, SIDE, CORES, DEPTH), ("x", "y", "core", "virt"))
    rows = ("x", "y", "core")
    in_specs = (P(None, rows, "virt"), P(None, rows, "virt"), P(), P(), P())
    out_specs = P("virt", None, rows, None)
    return jax.shard_map(body, mesh=fine, in_specs=in_specs, out_specs=out_specs, check_vma=False)
```

time: 209 us -> 209 us (level)
  waiting for transfers between devices: 100 us -> 95.1 us
  local copies, waits for them, and re-layouts: 1.57 us -> 4.88 us
  starting transfers between devices: 31.7 us -> 34.8 us
    all_gather x1, waiting for transfers between devices: 12.4 us -> 3.58 us  [body(): int_all = lax.all_gather(ints, ('core', 'virt'), axis=0)]
    ppermute x15, waiting for transfers between devices: 36.6 us -> 41.2 us  [move(): lax.ppermute(data, name, [(n, (n - step) % SIDE) for n in range(SIDE)])]
    unnamed x28 -> x40, local copies, waits for them, and re-layouts: 1.39 us -> 4.71 us
    all_to_all x2, waiting for transfers between devices: 48.1 us -> 45.6 us  [body(): lax.all_to_all(sent, ('core', 'virt'), split_axis=0, concat_axis=0, tiled...]
    pallas_call x2 -> x4, Pallas kernels: 29.1 us -> 26.7 us  [the longest x2 22 us: body(): pl.pallas_call(functools.partial(product_kernel, (occ, panel, width)), ou...]
  transfers between devices with their start and end apart: 20 -> 20, of which waited for: 11 -> 12; matrix products, arithmetic and copies ran while one was open for 0% -> 0% of each run, Pallas kernels for 7% -> 8%
where the time goes in v3:
time: 209 us; the launch traced here: 208 us
  waiting for transfers between devices  95.1 us (46%)
  starting transfers between devices  34.8 us (17%)
  Pallas kernels  33.7 us (16%)
  blocking collectives  26.2 us (13%)
  between operations  13.6 us (7%)
  local copies, waits for them, and re-layouts  4.88 us (2%)
    all_to_all x2, waiting for transfers between devices, body(): lax.all_to_all(sent, ('core', 'virt'), split_axis=0, concat_axis=0, tiled...  45.6 us
    ppermute x15, waiting for transfers between devices, move(): lax.ppermute(data, name, [(n, (n - step) % SIDE) for n in range(SIDE)])  41.2 us
    all_to_all x1, blocking collectives, body(): lax.all_to_all(amps, 'virt', split_axis=0, concat_axis=0, tiled=True)  26.2 us
    pallas_call x2, Pallas kernels, body(): pl.pallas_call(functools.partial(product_kernel, (occ, panel, width)), ou...  22 us
    ppermute x15, starting transfers between devices, move(): lax.ppermute(data, name, [(n, (n - step) % SIDE) for n in range(SIDE)])  21.9 us
    all_to_all x2, starting transfers between devices, body(): lax.all_to_all(sent, ('core', 'virt'), split_axis=0, concat_axis=0, tiled...  11 us
    pallas_call x1, Pallas kernels, body(): pl.pallas_call(functools.partial(finish_kernel, (occ, panel, virtuals), p...  7.05 us
    unnamed x40, local copies, waits for them, and re-layouts  4.71 us
  transfers between devices with their start and end apart: 20, of which 12 were waited for; matrix products, arithmetic and copies ran while one was open for 0% of the time, Pallas kernels for 8%

profile of v3, /device:TPU:1, one launch (start us, length us, event | category | flops | bytes accessed | tf_op | source)
XLA Modules:
  0.0 208.4 jit_solution(13968072880151007438)
XLA Ops:
  7.3 26.2 %all_to_all.15.refs_0_ = f32[8,64,256]{2,1,0:T(8,128)S(1)} all-to-all(f32[8,64,256]{2,1,0:T(8,128)} %param.5), channel_id=1, replica_groups=mesh['x'=4,'y'=4,'core'=2,'virt'=8] {'virt'}, dimensions={0} | all-to-all | bytes 1048576 | tf_op jit(solution)/shard_map/all_to_all | solution.py:149
  33.4 2.9 %collective-permute-start.2 = (f32[8,64,256]{2,1,0:T(8,128)S(1)}, f32[8,64,256]{2,1,0:T(8,128)S(1)}, u32[]{:S(2)}, u32[]{:S(2)}) collective-permute-start(f32[8,64,256]{2,1,0:T(8,128)S(1)} %all_to_all.15.refs_0_), channel_id=1, source_target_pairs={{0,48},{16,0},{32,16},{48,32},{1,49},{17,1},{33,17},{49,33},{2,50}... | collective-permute-start | bytes 1572872 | tf_op jit(solution)/shard_map/ppermute | solution.py:146
  39.0 4.7 %collective-permute-done.2.refs_3_ = f32[8,64,256]{2,1,0:T(8,128)S(1)} collective-permute-done((f32[8,64,256]{2,1,0:T(8,128)S(1)}, f32[8,64,256]{2,1,0:T(8,128)S(1)}, u32[]{:S(2)}, u32[]{:S(2)}) %collective-permute-start.2) | collective-permute-done | bytes 524320 | tf_op jit(solution)/shard_map/ppermute | solution.py:146
  43.7 2.5 %collective-permute-start.4 = (f32[8,64,256]{2,1,0:T(8,128)S(1)}, f32[8,64,256]{2,1,0:T(8,128)S(1)}, u32[]{:S(2)}, u32[]{:S(2)}) collective-permute-start(f32[8,64,256]{2,1,0:T(8,128)S(1)} %collective-permute-done.2.refs_3_), channel_id=1, source_target_pairs={{0,192},{64,0},{128,64},{192,128},{1,193},{65,1},{129,65},{193,129... | collective-permute-start | bytes 1572872 | tf_op jit(solution)/shard_map/ppermute | solution.py:146
  49.8 2.8 %collective-permute-start.8 = (f32[8,64,256]{2,1,0:T(8,128)S(1)}, f32[8,64,256]{2,1,0:T(8,128)}, u32[]{:S(2)}, u32[]{:S(2)}) collective-permute-start(f32[8,64,256]{2,1,0:T(8,128)S(1)} %collective-permute-done.refs_1_), channel_id=1, source_target_pairs={{0,192},{64,0},{128,64},{192,128},{1,193},{65,1},{129,65},{193,129... | collective-permute-start | bytes 1572872 | tf_op jit(solution)/shard_map/ppermute | solution.py:146
  52.7 5.3 %collective-permute-done.4.refs_5_ = f32[8,64,256]{2,1,0:T(8,128)S(1)} collective-permute-done((f32[8,64,256]{2,1,0:T(8,128)S(1)}, f32[8,64,256]{2,1,0:T(8,128)S(1)}, u32[]{:S(2)}, u32[]{:S(2)}) %collective-permute-start.4) | collective-permute-done | bytes 524320 | tf_op jit(solution)/shard_map/ppermute | solution.py:146
  59.0 2.4 %split_0.1 = (bf16[512,2048]{1,0:T(8,128)(2,1)S(1)}, bf16[512,2048]{1,0:T(8,128)(2,1)S(1)}) custom-call(f32[8,64,256]{2,1,0:T(8,128)} %copy-done.5, f32[8,64,256]{2,1,0:T(8,128)} %copy-done.11, f32[8,64,256]{2,1,0:T(8,128)} %copy-done.12, f32[8,64,256]{2,1,0:T(8,128)} %copy-done.6, f32[8,64,256]{2,1,0:T(8,128)} %copy-done.10, f32[8,64,256]{2,1,0:T(8,128)} %copy-done.16, ...), custom_call_target="tpu_custom_call" | custom-call | flops 60000002048 | bytes 60000000 | tf_op jit(solution)/shard_map/split_0/pallas_call | solution.py:166
  62.7 6.6 %collective-permute-done.8.refs_1_ = f32[8,64,256]{2,1,0:T(8,128)} collective-permute-done((f32[8,64,256]{2,1,0:T(8,128)S(1)}, f32[8,64,256]{2,1,0:T(8,128)}, u32[]{:S(2)}, u32[]{:S(2)}) %collective-permute-start.8) | collective-permute-done | bytes 524320 | tf_op jit(solution)/shard_map/ppermute | solution.py:146
  69.2 3.6 %all-gather.3.cloned.1.call-done = f32[128,64,256]{2,1,0:T(8,128)} async-done(((f32[8,64,256]{2,1,0:T(8,128)}), f32[128,64,256]{2,1,0:T(8,128)}) %all-gather.3.cloned.1.call-update) | async-done | bytes 8388624 | tf_op jit(solution)/shard_map/all_gather | solution.py:148
  74.4 11.0 %product_0.1.refs_0_ = f32[16,64,512]{2,1,0:T(8,128)} custom-call(f32[16,8,64,256]{3,2,1,0:T(8,128)} %bitcast.10, bf16[512,2048]{1,0:T(8,128)(2,1)S(1)} %get-tuple-element.20.a_hi, bf16[512,2048]{1,0:T(8,128)(2,1)S(1)} %copy-done.4), custom_call_target="tpu_custom_call" | custom-call | flops 60000002048 | bytes 60000000 | tf_op jit(solution)/shard_map/product_0/pallas_call | solution.py:184
  87.2 3.7 %all-to-all-start.1 = ((f32[16,64,512]{2,1,0:T(8,128)}), f32[16,64,512]{2,1,0:T(8,128)S(1)}, u32[]{:S(2)}, u32[]{:S(2)}) async-start(f32[16,64,512]{2,1,0:T(8,128)} %product_0.1.refs_0_), calls=%async_computation.1 | async-start | bytes 4194304 | tf_op jit(solution)/shard_map/all_to_all | solution.py:203
  92.2 2.7 %collective-permute-start.10 = (f32[8,64,256]{2,1,0:T(8,128)S(1)}, f32[8,64,256]{2,1,0:T(8,128)S(1)}, u32[]{:S(2)}, u32[]{:S(2)}) collective-permute-start(f32[8,64,256]{2,1,0:T(8,128)S(1)} %copy-done.7), channel_id=1, source_target_pairs={{0,48},{16,0},{32,16},{48,32},{1,49},{17,1},{33,17},{49,33},{2,50}... | collective-permute-start | bytes 1572872 | tf_op jit(solution)/shard_map/ppermute | solution.py:146
  94.8 10.8 %collective-permute-done.11.refs_3_ = f32[8,64,256]{2,1,0:T(8,128)S(1)} collective-permute-done((f32[8,64,256]{2,1,0:T(8,128)}, f32[8,64,256]{2,1,0:T(8,128)S(1)}, u32[]{:S(2)}, u32[]{:S(2)}) %collective-permute-start.11) | collective-permute-done | bytes 524320 | tf_op jit(solution)/shard_map/ppermute | solution.py:146
  105.7 2.7 %collective-permute-start.15 = (f32[8,64,256]{2,1,0:T(8,128)S(1)}, f32[8,64,256]{2,1,0:T(8,128)S(1)}, u32[]{:S(2)}, u32[]{:S(2)}) collective-permute-start(f32[8,64,256]{2,1,0:T(8,128)S(1)} %collective-permute-done.11.refs_3_), channel_id=1, source_target_pairs={{0,48},{16,0},{32,16},{48,32},{1,49},{17,1},{33,17},{49,33},{2,50}... | collective-permute-start | bytes 1572872 | tf_op jit(solution)/shard_map/ppermute | solution.py:146
  109.9 8.7 %collective-permute-done.15.refs_7_ = f32[8,64,256]{2,1,0:T(8,128)S(1)} collective-permute-done((f32[8,64,256]{2,1,0:T(8,128)S(1)}, f32[8,64,256]{2,1,0:T(8,128)S(1)}, u32[]{:S(2)}, u32[]{:S(2)}) %collective-permute-start.15) | collective-permute-done | bytes 524320 | tf_op jit(solution)/shard_map/ppermute | solution.py:146
  118.6 2.1 %collective-permute-done.13.refs_5_ = f32[8,64,256]{2,1,0:T(8,128)S(1)} collective-permute-done((f32[8,64,256]{2,1,0:T(8,128)}, f32[8,64,256]{2,1,0:T(8,128)S(1)}, u32[]{:S(2)}, u32[]{:S(2)}) %collective-permute-start.13) | collective-permute-done | bytes 524320 | tf_op jit(solution)/shard_map/ppermute | solution.py:146
  120.7 2.2 %collective-permute-done.14.refs_6_ = f32[8,64,256]{2,1,0:T(8,128)S(1)} collective-permute-done((f32[8,64,256]{2,1,0:T(8,128)S(1)}, f32[8,64,256]{2,1,0:T(8,128)S(1)}, u32[]{:S(2)}, u32[]{:S(2)}) %collective-permute-start.14) | collective-permute-done | bytes 524320 | tf_op jit(solution)/shard_map/ppermute | solution.py:146
  123.7 2.3 %split_1.1 = (bf16[512,2048]{1,0:T(8,128)(2,1)S(1)}, bf16[512,2048]{1,0:T(8,128)(2,1)S(1)}) custom-call(f32[8,64,256]{2,1,0:T(8,128)} %collective-permute-done.7.refs_0_, f32[8,64,256]{2,1,0:T(8,128)} %collective-permute-done.8.refs_1_, f32[8,64,256]{2,1,0:T(8,128)} %copy-done.14, f32[8,64,256]{2,1,0:T(8,128)} %copy-done.13, f32[8,64,256]{2,1,0:T(8,128)} %copy-done.15, ...), custom_call_target="tpu_custom_call" | custom-call | flops 8000000000 | bytes 8000000 | tf_op jit(solution)/shard_map/split_1/pallas_call | solution.py:166
  126.0 11.0 %product_1.1.refs_3_ = f32[16,64,512]{2,1,0:T(8,128)} custom-call(f32[16,8,64,256]{3,2,1,0:T(8,128)} %bitcast.11, bf16[512,2048]{1,0:T(8,128)(2,1)S(1)} %get-tuple-element.26.a_hi, bf16[512,2048]{1,0:T(8,128)(2,1)S(1)} %get-tuple-element.27.a_lo), custom_call_target="tpu_custom_call" | custom-call | flops 8000000000 | bytes 8000000 | tf_op jit(solution)/shard_map/product_1/pallas_call | solution.py:184
  137.1 1.9 all-to-all-done.1.refs_2_
  139.0 7.3 %all-to-all-start.2 = ((f32[16,64,512]{2,1,0:T(8,128)}), f32[16,64,512]{2,1,0:T(8,128)}, u32[]{:S(2)}, u32[]{:S(2)}) async-start(f32[16,64,512]{2,1,0:T(8,128)} %product_1.1.refs_3_), calls=%async_computation.2 | async-start | bytes 4194304 | tf_op jit(solution)/shard_map/all_to_all | solution.py:203
  146.8 4.0 %collective-permute-done.16.refs_4_ = f32[16,64,512]{2,1,0:T(8,128)} collective-permute-done((f32[16,64,512]{2,1,0:T(8,128)}, f32[16,64,512]{2,1,0:T(8,128)}, u32[]{:S(2)}, u32[]{:S(2)}) %collective-permute-start.16) | collective-permute-done | bytes 2097184 | tf_op jit(solution)/shard_map/ppermute | solution.py:202
  150.8 43.7 %all-to-all-done.2.refs_5_ = f32[16,64,512]{2,1,0:T(8,128)} async-done(((f32[16,64,512]{2,1,0:T(8,128)}), f32[16,64,512]{2,1,0:T(8,128)}, u32[]{:S(2)}, u32[]{:S(2)}) %all-to-all-start.2) | async-done | bytes 2097184 | tf_op jit(solution)/shard_map/all_to_all | solution.py:203
  194.4 7.1 %finish.1 = f32[8,64,2048]{2,1,0:T(8,128)} custom-call(s32[4]{0:T(128)S(1)} %pad_add_fusion.places, s32[32]{0:T(128)S(1)} %copy-done.1, f32[8]{0:T(128)S(1)} %copy-done.2, f32[64,1]{1,0:T(8,128)S(1)} %copy.7.e_b, f32[1,2048]{1,0:T(1,128)S(1)} %bitcast.9, f32[16,64,512]{2,1,0:T(8,128)} %product_0.1.refs_0_, f32[16,64,512]{2,1,0:T(8,128)} %collective-permute-done.9.refs_1_, ...), custom_call_target="tpu_custom_call" | custom-call | tf_op jit(solution)/shard_map/finish/pallas_call | solution.py:215
  (66 shorter events, 16.6 us)
Async XLA Ops:
  6.5 66.3 %all-gather.3.cloned.1.call-start = ((), (), s32[]{:S(2)}) async-start(), calls=%async_computation.3 | async-start | bytes 8912896 | tf_op jit(solution)/shard_map/all_gather | solution.py:148
  33.4 24.6 %copy-start.5 = (f32[8,64,256]{2,1,0:T(8,128)}, f32[8,64,256]{2,1,0:T(8,128)S(1)}, u32[]{:S(2)}) copy-start(f32[8,64,256]{2,1,0:T(8,128)S(1)} %all_to_all.15.refs_0_) | copy-start | bytes 1572868
  33.4 10.3 %collective-permute-start.2 = (f32[8,64,256]{2,1,0:T(8,128)S(1)}, f32[8,64,256]{2,1,0:T(8,128)S(1)}, u32[]{:S(2)}, u32[]{:S(2)}) collective-permute-start(f32[8,64,256]{2,1,0:T(8,128)S(1)} %all_to_all.15.refs_0_), channel_id=1, source_target_pairs={{0,48},{16,0},{32,16},{48,32},{1,49},{17,1},{33,17},{49,33},{2,50}... | collective-permute-start | bytes 1572872 | tf_op jit(solution)/shard_map/ppermute | solution.py:146
  36.3 10.6 %collective-permute-start.3 = (f32[8,64,256]{2,1,0:T(8,128)S(1)}, f32[8,64,256]{2,1,0:T(8,128)S(1)}, u32[]{:S(2)}, u32[]{:S(2)}) collective-permute-start(f32[8,64,256]{2,1,0:T(8,128)S(1)} %all_to_all.15.refs_0_), channel_id=1, source_target_pairs={{0,16},{16,32},{32,48},{48,0},{1,17},{17,33},{33,49},{49,1},{2,18}... | collective-permute-start | bytes 1572872 | tf_op jit(solution)/shard_map/ppermute | solution.py:146
  36.3 11.9 %collective-permute-start.1 = (f32[8,64,256]{2,1,0:T(8,128)S(1)}, f32[8,64,256]{2,1,0:T(8,128)S(1)}, u32[]{:S(2)}, u32[]{:S(2)}) collective-permute-start(f32[8,64,256]{2,1,0:T(8,128)S(1)} %all_to_all.15.refs_0_), channel_id=1, source_target_pairs={{0,64},{64,128},{128,192},{192,0},{1,65},{65,129},{129,193},{193,1... | collective-permute-start | bytes 1572872 | tf_op jit(solution)/shard_map/ppermute | solution.py:146
  37.5 12.3 %collective-permute-start = (f32[8,64,256]{2,1,0:T(8,128)S(1)}, f32[8,64,256]{2,1,0:T(8,128)S(1)}, u32[]{:S(2)}, u32[]{:S(2)}) collective-permute-start(f32[8,64,256]{2,1,0:T(8,128)S(1)} %all_to_all.15.refs_0_), channel_id=1, source_target_pairs={{0,192},{64,0},{128,64},{192,128},{1,193},{65,1},{129,65},{193,129... | collective-permute-start | bytes 1572872 | tf_op jit(solution)/shard_map/ppermute | solution.py:146
  43.7 14.3 %collective-permute-start.4 = (f32[8,64,256]{2,1,0:T(8,128)S(1)}, f32[8,64,256]{2,1,0:T(8,128)S(1)}, u32[]{:S(2)}, u32[]{:S(2)}) collective-permute-start(f32[8,64,256]{2,1,0:T(8,128)S(1)} %collective-permute-done.2.refs_3_), channel_id=1, source_target_pairs={{0,192},{64,0},{128,64},{192,128},{1,193},{65,1},{129,65},{193,129... | collective-permute-start | bytes 1572872 | tf_op jit(solution)/shard_map/ppermute | solution.py:146
  46.9 11.1 %collective-permute-start.5 = (f32[8,64,256]{2,1,0:T(8,128)S(1)}, f32[8,64,256]{2,1,0:T(8,128)S(1)}, u32[]{:S(2)}, u32[]{:S(2)}) collective-permute-start(f32[8,64,256]{2,1,0:T(8,128)S(1)} %collective-permute-done.3.refs_4_), channel_id=1, source_target_pairs={{0,64},{64,128},{128,192},{192,0},{1,65},{65,129},{129,193},{193,1... | collective-permute-start | bytes 1572872 | tf_op jit(solution)/shard_map/ppermute | solution.py:146
  48.2 9.9 %collective-permute-start.6 = (f32[8,64,256]{2,1,0:T(8,128)S(1)}, f32[8,64,256]{2,1,0:T(8,128)}, u32[]{:S(2)}, u32[]{:S(2)}) collective-permute-start(f32[8,64,256]{2,1,0:T(8,128)S(1)} %collective-permute-done.1.refs_2_), channel_id=1, source_target_pairs={{0,48},{16,0},{32,16},{48,32},{1,49},{17,1},{33,17},{49,33},{2,50}... | collective-permute-start | bytes 1572872 | tf_op jit(solution)/shard_map/ppermute | solution.py:146
  49.8 12.8 %collective-permute-start.7 = (f32[8,64,256]{2,1,0:T(8,128)S(1)}, f32[8,64,256]{2,1,0:T(8,128)}, u32[]{:S(2)}, u32[]{:S(2)}) collective-permute-start(f32[8,64,256]{2,1,0:T(8,128)S(1)} %collective-permute-done.refs_1_), channel_id=1, source_target_pairs={{0,16},{16,32},{32,48},{48,0},{1,17},{17,33},{33,49},{49,1},{2,18}... | collective-permute-start | bytes 1572872 | tf_op jit(solution)/shard_map/ppermute | solution.py:146
  49.8 19.4 %collective-permute-start.8 = (f32[8,64,256]{2,1,0:T(8,128)S(1)}, f32[8,64,256]{2,1,0:T(8,128)}, u32[]{:S(2)}, u32[]{:S(2)}) collective-permute-start(f32[8,64,256]{2,1,0:T(8,128)S(1)} %collective-permute-done.refs_1_), channel_id=1, source_target_pairs={{0,192},{64,0},{128,64},{192,128},{1,193},{65,1},{129,65},{193,129... | collective-permute-start | bytes 1572872 | tf_op jit(solution)/shard_map/ppermute | solution.py:146
  85.5 24.4 %copy-start.9 = (f32[8,64,256]{2,1,0:T(8,128)S(1)}, f32[8,64,256]{2,1,0:T(8,128)}, u32[]{:S(2)}) copy-start(f32[8,64,256]{2,1,0:T(8,128)} %copy-done.8) | copy-start | bytes 1572868
  85.5 20.2 %collective-permute-start.9 = (f32[16,64,512]{2,1,0:T(8,128)}, f32[16,64,512]{2,1,0:T(8,128)}, u32[]{:S(2)}, u32[]{:S(2)}) collective-permute-start(f32[16,64,512]{2,1,0:T(8,128)} %product_0.1.refs_0_), channel_id=1, source_target_pairs={{0,8},{8,0},{1,9},{9,1},{2,10},{10,2},{3,11},{11,3},{4,12},{12,4},... | collective-permute-start | bytes 6291464 | tf_op jit(solution)/shard_map/ppermute | solution.py:202
  87.2 51.8 %all-to-all-start.1 = ((f32[16,64,512]{2,1,0:T(8,128)}), f32[16,64,512]{2,1,0:T(8,128)S(1)}, u32[]{:S(2)}, u32[]{:S(2)}) async-start(f32[16,64,512]{2,1,0:T(8,128)} %product_0.1.refs_0_), calls=%async_computation.1 | async-start | bytes 4194304 | tf_op jit(solution)/shard_map/all_to_all | solution.py:203
  90.9 14.8 %collective-permute-start.11 = (f32[8,64,256]{2,1,0:T(8,128)}, f32[8,64,256]{2,1,0:T(8,128)S(1)}, u32[]{:S(2)}, u32[]{:S(2)}) collective-permute-start(f32[8,64,256]{2,1,0:T(8,128)} %collective-permute-done.6.refs_7_), channel_id=1, source_target_pairs={{0,64},{64,128},{128,192},{192,0},{1,65},{65,129},{129,193},{193,1... | collective-permute-start | bytes 1572872 | tf_op jit(solution)/shard_map/ppermute | solution.py:146
  92.2 17.7 %collective-permute-start.10 = (f32[8,64,256]{2,1,0:T(8,128)S(1)}, f32[8,64,256]{2,1,0:T(8,128)S(1)}, u32[]{:S(2)}, u32[]{:S(2)}) collective-permute-start(f32[8,64,256]{2,1,0:T(8,128)S(1)} %copy-done.7), channel_id=1, source_target_pairs={{0,48},{16,0},{32,16},{48,32},{1,49},{17,1},{33,17},{49,33},{2,50}... | collective-permute-start | bytes 1572872 | tf_op jit(solution)/shard_map/ppermute | solution.py:146
  94.8 15.0 %collective-permute-start.12 = (f32[8,64,256]{2,1,0:T(8,128)}, f32[8,64,256]{2,1,0:T(8,128)S(1)}, u32[]{:S(2)}, u32[]{:S(2)}) collective-permute-start(f32[8,64,256]{2,1,0:T(8,128)} %collective-permute-done.7.refs_0_), channel_id=1, source_target_pairs={{0,16},{16,32},{32,48},{48,0},{1,17},{17,33},{33,49},{49,1},{2,18}... | collective-permute-start | bytes 1572872 | tf_op jit(solution)/shard_map/ppermute | solution.py:146
  105.7 12.9 %collective-permute-start.15 = (f32[8,64,256]{2,1,0:T(8,128)S(1)}, f32[8,64,256]{2,1,0:T(8,128)S(1)}, u32[]{:S(2)}, u32[]{:S(2)}) collective-permute-start(f32[8,64,256]{2,1,0:T(8,128)S(1)} %collective-permute-done.11.refs_3_), channel_id=1, source_target_pairs={{0,48},{16,0},{32,16},{48,32},{1,49},{17,1},{33,17},{49,33},{2,50}... | collective-permute-start | bytes 1572872 | tf_op jit(solution)/shard_map/ppermute | solution.py:146
  108.4 12.3 %collective-permute-start.13 = (f32[8,64,256]{2,1,0:T(8,128)}, f32[8,64,256]{2,1,0:T(8,128)S(1)}, u32[]{:S(2)}, u32[]{:S(2)}) collective-permute-start(f32[8,64,256]{2,1,0:T(8,128)} %collective-permute-done.7.refs_0_), channel_id=1, source_target_pairs={{0,192},{64,0},{128,64},{192,128},{1,193},{65,1},{129,65},{193,129... | collective-permute-start | bytes 1572872 | tf_op jit(solution)/shard_map/ppermute | solution.py:146
  109.8 13.1 %collective-permute-start.14 = (f32[8,64,256]{2,1,0:T(8,128)S(1)}, f32[8,64,256]{2,1,0:T(8,128)S(1)}, u32[]{:S(2)}, u32[]{:S(2)}) collective-permute-start(f32[8,64,256]{2,1,0:T(8,128)S(1)} %copy-done.9), channel_id=1, source_target_pairs={{0,16},{16,32},{32,48},{48,0},{1,17},{17,33},{33,49},{49,1},{2,18}... | collective-permute-start | bytes 1572872 | tf_op jit(solution)/shard_map/ppermute | solution.py:146
  137.1 57.4 %copy-start.1 = (s32[32]{0:T(128)S(1)}, s32[32]{0:T(128)}, u32[]{:S(2)}) copy-start(s32[32]{0:T(128)} %panel_of.1) | copy-start | bytes 388
  137.1 57.4 %copy-start.2 = (f32[8]{0:T(128)S(1)}, f32[8]{0:T(128)}, u32[]{:S(2)}) copy-start(f32[8]{0:T(128)} %e_occ.1) | copy-start | bytes 100
  139.0 55.5 %all-to-all-start.2 = ((f32[16,64,512]{2,1,0:T(8,128)}), f32[16,64,512]{2,1,0:T(8,128)}, u32[]{:S(2)}, u32[]{:S(2)}) async-start(f32[16,64,512]{2,1,0:T(8,128)} %product_1.1.refs_3_), calls=%async_computation.2 | async-start | bytes 4194304 | tf_op jit(solution)/shard_map/all_to_all | solution.py:203
  146.3 4.5 %collective-permute-start.16 = (f32[16,64,512]{2,1,0:T(8,128)}, f32[16,64,512]{2,1,0:T(8,128)}, u32[]{:S(2)}, u32[]{:S(2)}) collective-permute-start(f32[16,64,512]{2,1,0:T(8,128)} %product_1.1.refs_3_), channel_id=1, source_target_pairs={{0,8},{8,0},{1,9},{9,1},{2,10},{10,2},{3,11},{11,3},{4,12},{12,4},... | collective-permute-start | bytes 6291464 | tf_op jit(solution)/shard_map/ppermute | solution.py:202
  (16 other events, 115.1 us)
Sparse Core Ops, SparseCore 0:
  9.2 63.5 all-gather.2

commit v4 on v3

--- a/solution.py
+++ b/solution.py
@@ -50,7 +50,7 @@
 def split_kernel(dims, *refs):
     panel, width, chips = dims
     amps_hbm = refs[:chips]
-    a_hi, a_lo, amps, amp_sem = refs[chips:]
+    a_hi, a_lo_hbm, amps, a_lo, amp_sem, out_sem = refs[chips:]
     loads = [pltpu.make_async_copy(amps_hbm[g], amps.at[g], amp_sem.at[g]) for g in range(chips)]
     for copy in loads:
         copy.start()
@@ -60,12 +60,16 @@
         for s in range(DEPTH):
             cols = slice(s * width, (s + 1) * width)
             a_hi[rows, cols], a_lo[rows, cols] = split(amps[g, s])
-
-
-def product_kernel(dims, ints_hbm, a_hi, a_lo, whole, ints, i_hi, i_lo, out, int_sem, out_sem):
+    store = pltpu.make_async_copy(a_lo, a_lo_hbm, out_sem)
+    store.start()
+    store.wait()
+
+
+def product_kernel(dims, ints_hbm, a_hi, a_lo_hbm, whole, a_lo, ints, i_hi, i_lo, out, a_sem, int_sem, out_sem):
     occ, panel, width = dims
     loads = [pltpu.make_async_copy(ints_hbm.at[s], ints.at[s], int_sem.at[s]) for s in range(CORES * DEPTH)]
-    for copy in loads:
+    low = pltpu.make_async_copy(a_lo_hbm, a_lo, a_sem)
+    for copy in loads[:DEPTH] + [low] + loads[DEPTH:]:
         copy.start()
     height = occ * panel
     blocks = height // BLOCK
@@ -78,7 +82,7 @@
     for s in range(DEPTH):
         loads[s].wait()
         cut(0, s)
-    for copy in loads[DEPTH:]:
+    for copy in [low] + loads[DEPTH:]:
         copy.wait()
     stores = []
     for c in range(CORES):
@@ -165,36 +169,40 @@
         wide = jax.ShapeDtypeStruct((size, DEPTH * width), bf16)
         parts = pl.pallas_call(
             functools.partial(split_kernel, (panel, width, len(chips))),
-            out_shape=[wide, wide],
+            out_shape=[wide, pltpu.HBM(wide.shape, bf16)],
             in_specs=[ANY] * len(chips),
-            out_specs=[VMEM, VMEM],
+            out_specs=[VMEM, ANY],
             scratch_shapes=[
                 pltpu.VMEM((len(chips), DEPTH, panel, width), f32),
+                pltpu.VMEM(wide.shape, bf16),
                 pltpu.SemaphoreType.DMA((len(chips),)),
+                pltpu.SemaphoreType.DMA,
             ],
-            compiler_params=pltpu.CompilerParams(vmem_limit_bytes=24 * 2**20),
+            compiler_params=pltpu.CompilerParams(vmem_limit_bytes=8 * 2**20),
             cost_estimate=COSTS[n],
             name=f"split_{n}",
         )(*[pltpu.with_memory_space_constraint(held[chip], pltpu.HBM) for chip in chips])
         if n == 0:
             early = [held[wrap(*chip)] for chip in EARLY]
             int_all, *parts = lax.optimization_barrier([int_all, *parts, *early])[: 1 + len(parts)]
-        parts = [pltpu.with_memory_space_constraint(part, pltpu.VMEM) for part in parts]
+        parts = [pltpu.with_memory_space_constraint(*both) for both in zip(parts, [pltpu.VMEM, pltpu.HBM])]
         both = pltpu.HBM((CORES * occ, panel, size), f32)
         whole = pl.pallas_call(
             functools.partial(product_kernel, (occ, panel, width)),
             out_shape=both,
-            in_specs=[ANY, VMEM, VMEM],
+            in_specs=[ANY, VMEM, ANY],
             out_specs=ANY,
             scratch_shapes=[
+                pltpu.VMEM(wide.shape, bf16),
                 pltpu.VMEM((CORES * DEPTH, occ, panel, width), f32),
                 pltpu.VMEM((CORES * height, DEPTH * width), bf16),
                 pltpu.VMEM((CORES * height, DEPTH * width), bf16),
                 pltpu.VMEM(both.shape, f32),
+                pltpu.SemaphoreType.DMA,
                 pltpu.SemaphoreType.DMA((CORES * DEPTH,)),
                 pltpu.SemaphoreType.DMA((CORES * height // BLOCK,)),
             ],
-            compiler_params=pltpu.CompilerParams(vmem_limit_bytes=36 * 2**20),
+            compiler_params=pltpu.CompilerParams(vmem_limit_bytes=24 * 2**20),
             cost_estimate=COSTS[n],
             name=f"product_{n}",
         )(pltpu.with_memory_space_constraint(int_all, pltpu.HBM), *parts)
@@ -206,8 +214,9 @@
         if n == 0:
             int_all = lax.optimization_barrier([int_all, whole])[0]
             bring(LAST, [swapped])
-    where = [pltpu.HBM, pltpu.HBM, pltpu.VMEM]
-    arrays = [[pltpu.with_memory_space_constraint(*both) for both in zip(group, where)] for group in arrays]
+    fixed = lambda array, place: array if place is None else pltpu.with_memory_space_constraint(array, place)
+    where = [[pltpu.HBM, pltpu.HBM, pltpu.VMEM], [pltpu.HBM, pltpu.HBM, None]]
+    arrays = [[fixed(*both) for both in zip(*groups)] for groups in zip(arrays, where)]
 
     slots = [(chip, e) for e in range(CORES) for chips in sets for chip in chips]
     pair = (index[1] * SIDE + index[2]) * CORES + index[3]
@@ -215,7 +224,7 @@
     out = pl.pallas_call(
         functools.partial(finish_kernel, (occ, panel, virtuals), places_of, slots),
         out_shape=jax.ShapeDtypeStruct((occ, panel, virtuals), f32),
-        in_specs=[SMEM, SMEM, SMEM, VMEM, VMEM] + [ANY, ANY, VMEM] * len(sets),
+        in_specs=[SMEM, SMEM, SMEM, VMEM, VMEM] + [ANY, ANY, VMEM, ANY, ANY, ANY],
         out_specs=ANY,
         scratch_shapes=[
             pltpu.SMEM((virtuals // panel,), jnp.int32),
@@ -225,7 +234,7 @@
             pltpu.SemaphoreType.DMA((occ, 2 * CORES * len(sets))),
             pltpu.SemaphoreType.DMA((occ,)),
         ],
-        compiler_params=pltpu.CompilerParams(vmem_limit_bytes=48 * 2**20),
+        compiler_params=pltpu.CompilerParams(vmem_limit_bytes=16 * 2**20),
         name="finish",
     )(places, panel_of, e_occ, e_b, e_vir.reshape(1, virtuals), *[a for group in arrays for a in group])
     return out[None]

time: 209 us -> 209 us (level)
  local copies, waits for them, and re-layouts: 4.88 us -> 1.93 us
  Pallas kernels: 33.7 us -> 36.6 us
    unnamed x40 -> x36, local copies, waits for them, and re-layouts: 4.71 us -> 1.76 us
    pallas_call x2, Pallas kernels: 4.64 us -> 7.28 us  [body(): pl.pallas_call(functools.partial(split_kernel, (panel, width, len(chips))...]
  transfers between devices with their start and end apart: 20 -> 20, of which waited for: 12 -> 11; matrix products, arithmetic and copies ran while one was open for 0% -> 0% of each run, Pallas kernels for 8% -> 9%
where the time goes in v4:
time: 209 us; the launch traced here: 208 us
  waiting for transfers between devices  93.2 us (45%)
  starting transfers between devices  36.7 us (18%)
  Pallas kernels  36.6 us (18%)
  blocking collectives  26.2 us (13%)
  between operations  13.6 us (7%)
    all_to_all x2, waiting for transfers between devices, body(): lax.all_to_all(sent, ('core', 'virt'), split_axis=0, concat_axis=0, tiled...  43.7 us
    ppermute x15, waiting for transfers between devices, move(): lax.ppermute(data, name, [(n, (n - step) % SIDE) for n in range(SIDE)])  41.2 us
    all_to_all x1, blocking collectives, body(): lax.all_to_all(amps, 'virt', split_axis=0, concat_axis=0, tiled=True)  26.2 us
    pallas_call x2, Pallas kernels, body(): pl.pallas_call(functools.partial(product_kernel, (occ, panel, width)), ou...  23.3 us
    ppermute x15, starting transfers between devices, move(): lax.ppermute(data, name, [(n, (n - step) % SIDE) for n in range(SIDE)])  21.9 us
    all_to_all x2, starting transfers between devices, body(): lax.all_to_all(sent, ('core', 'virt'), split_axis=0, concat_axis=0, tiled...  12.9 us
    pallas_call x2, Pallas kernels, body(): pl.pallas_call(functools.partial(split_kernel, (panel, width, len(chips))...  7.28 us
    pallas_call x1, Pallas kernels, body(): pl.pallas_call(functools.partial(finish_kernel, (occ, panel, virtuals), p...  6.11 us
  transfers between devices with their start and end apart: 20, of which 11 were waited for; matrix products, arithmetic and copies ran while one was open for 0% of the time, Pallas kernels for 9%

profile of v4, /device:TPU:1, one launch (start us, length us, event | category | flops | bytes accessed | tf_op | source)
XLA Modules:
  0.0 208.3 jit_solution(5607094753874472149)
XLA Ops:
  7.3 26.2 %all_to_all.15.refs_0_ = f32[8,64,256]{2,1,0:T(8,128)S(1)} all-to-all(f32[8,64,256]{2,1,0:T(8,128)} %param.5), channel_id=1, replica_groups=mesh['x'=4,'y'=4,'core'=2,'virt'=8] {'virt'}, dimensions={0} | all-to-all | bytes 1048576 | tf_op jit(solution)/shard_map/all_to_all | solution.py:153
  33.4 2.9 %collective-permute-start.2 = (f32[8,64,256]{2,1,0:T(8,128)S(1)}, f32[8,64,256]{2,1,0:T(8,128)S(1)}, u32[]{:S(2)}, u32[]{:S(2)}) collective-permute-start(f32[8,64,256]{2,1,0:T(8,128)S(1)} %all_to_all.15.refs_0_), channel_id=1, source_target_pairs={{0,48},{16,0},{32,16},{48,32},{1,49},{17,1},{33,17},{49,33},{2,50}... | collective-permute-start | bytes 1572872 | tf_op jit(solution)/shard_map/ppermute | solution.py:150
  39.0 4.7 %collective-permute-done.2.refs_3_ = f32[8,64,256]{2,1,0:T(8,128)S(1)} collective-permute-done((f32[8,64,256]{2,1,0:T(8,128)S(1)}, f32[8,64,256]{2,1,0:T(8,128)S(1)}, u32[]{:S(2)}, u32[]{:S(2)}) %collective-permute-start.2) | collective-permute-done | bytes 524320 | tf_op jit(solution)/shard_map/ppermute | solution.py:150
  43.7 2.5 %collective-permute-start.4 = (f32[8,64,256]{2,1,0:T(8,128)S(1)}, f32[8,64,256]{2,1,0:T(8,128)S(1)}, u32[]{:S(2)}, u32[]{:S(2)}) collective-permute-start(f32[8,64,256]{2,1,0:T(8,128)S(1)} %collective-permute-done.2.refs_3_), channel_id=1, source_target_pairs={{0,192},{64,0},{128,64},{192,128},{1,193},{65,1},{129,65},{193,129... | collective-permute-start | bytes 1572872 | tf_op jit(solution)/shard_map/ppermute | solution.py:150
  49.8 2.8 %collective-permute-start.8 = (f32[8,64,256]{2,1,0:T(8,128)S(1)}, f32[8,64,256]{2,1,0:T(8,128)}, u32[]{:S(2)}, u32[]{:S(2)}) collective-permute-start(f32[8,64,256]{2,1,0:T(8,128)S(1)} %collective-permute-done.refs_1_), channel_id=1, source_target_pairs={{0,192},{64,0},{128,64},{192,128},{1,193},{65,1},{129,65},{193,129... | collective-permute-start | bytes 1572872 | tf_op jit(solution)/shard_map/ppermute | solution.py:150
  52.7 5.3 %collective-permute-done.4.refs_5_ = f32[8,64,256]{2,1,0:T(8,128)S(1)} collective-permute-done((f32[8,64,256]{2,1,0:T(8,128)S(1)}, f32[8,64,256]{2,1,0:T(8,128)S(1)}, u32[]{:S(2)}, u32[]{:S(2)}) %collective-permute-start.4) | collective-permute-done | bytes 524320 | tf_op jit(solution)/shard_map/ppermute | solution.py:150
  59.0 3.7 %split_0.1 = (bf16[512,2048]{1,0:T(8,128)(2,1)S(1)}, bf16[512,2048]{1,0:T(8,128)(2,1)}) custom-call(f32[8,64,256]{2,1,0:T(8,128)} %copy-done.3, f32[8,64,256]{2,1,0:T(8,128)} %copy-done.9, f32[8,64,256]{2,1,0:T(8,128)} %copy-done.10, f32[8,64,256]{2,1,0:T(8,128)} %copy-done.4, f32[8,64,256]{2,1,0:T(8,128)} %copy-done.8, f32[8,64,256]{2,1,0:T(8,128)} %copy-done.14, ...), custom_call_target="tpu_custom_call" | custom-call | flops 60000002048 | bytes 60000000 | tf_op jit(solution)/shard_map/split_0/pallas_call | solution.py:170
  62.7 6.6 %collective-permute-done.8.refs_1_ = f32[8,64,256]{2,1,0:T(8,128)} collective-permute-done((f32[8,64,256]{2,1,0:T(8,128)S(1)}, f32[8,64,256]{2,1,0:T(8,128)}, u32[]{:S(2)}, u32[]{:S(2)}) %collective-permute-start.8) | collective-permute-done | bytes 524320 | tf_op jit(solution)/shard_map/ppermute | solution.py:150
  69.2 3.6 %all-gather.3.cloned.1.call-done = f32[128,64,256]{2,1,0:T(8,128)} async-done(((f32[8,64,256]{2,1,0:T(8,128)}), f32[128,64,256]{2,1,0:T(8,128)}) %all-gather.3.cloned.1.call-update) | async-done | bytes 8388624 | tf_op jit(solution)/shard_map/all_gather | solution.py:152
  72.8 11.6 %product_0.1.refs_0_ = f32[16,64,512]{2,1,0:T(8,128)} custom-call(f32[16,8,64,256]{3,2,1,0:T(8,128)} %bitcast.10, bf16[512,2048]{1,0:T(8,128)(2,1)S(1)} %get-tuple-element.20.a_hi, bf16[512,2048]{1,0:T(8,128)(2,1)} %get-tuple-element.21.a_lo_hbm), custom_call_target="tpu_custom_call" | custom-call | flops 60000002048 | bytes 60000000 | tf_op jit(solution)/shard_map/product_0/pallas_call | solution.py:190
  84.5 1.7 collective-permute-start.9
  86.2 3.7 %all-to-all-start.1 = ((f32[16,64,512]{2,1,0:T(8,128)}), f32[16,64,512]{2,1,0:T(8,128)S(1)}, u32[]{:S(2)}, u32[]{:S(2)}) async-start(f32[16,64,512]{2,1,0:T(8,128)} %product_0.1.refs_0_), calls=%async_computation.1 | async-start | bytes 4194304 | tf_op jit(solution)/shard_map/all_to_all | solution.py:211
  91.2 2.7 %collective-permute-start.10 = (f32[8,64,256]{2,1,0:T(8,128)S(1)}, f32[8,64,256]{2,1,0:T(8,128)S(1)}, u32[]{:S(2)}, u32[]{:S(2)}) collective-permute-start(f32[8,64,256]{2,1,0:T(8,128)S(1)} %copy-done.5), channel_id=1, source_target_pairs={{0,48},{16,0},{32,16},{48,32},{1,49},{17,1},{33,17},{49,33},{2,50}... | collective-permute-start | bytes 1572872 | tf_op jit(solution)/shard_map/ppermute | solution.py:150
  93.8 10.9 %collective-permute-done.11.refs_3_ = f32[8,64,256]{2,1,0:T(8,128)S(1)} collective-permute-done((f32[8,64,256]{2,1,0:T(8,128)}, f32[8,64,256]{2,1,0:T(8,128)S(1)}, u32[]{:S(2)}, u32[]{:S(2)}) %collective-permute-start.11) | collective-permute-done | bytes 524320 | tf_op jit(solution)/shard_map/ppermute | solution.py:150
  104.7 2.7 %collective-permute-start.15 = (f32[8,64,256]{2,1,0:T(8,128)S(1)}, f32[8,64,256]{2,1,0:T(8,128)S(1)}, u32[]{:S(2)}, u32[]{:S(2)}) collective-permute-start(f32[8,64,256]{2,1,0:T(8,128)S(1)} %collective-permute-done.11.refs_3_), channel_id=1, source_target_pairs={{0,48},{16,0},{32,16},{48,32},{1,49},{17,1},{33,17},{49,33},{2,50}... | collective-permute-start | bytes 1572872 | tf_op jit(solution)/shard_map/ppermute | solution.py:150
  108.9 8.7 %collective-permute-done.15.refs_7_ = f32[8,64,256]{2,1,0:T(8,128)S(1)} collective-permute-done((f32[8,64,256]{2,1,0:T(8,128)S(1)}, f32[8,64,256]{2,1,0:T(8,128)S(1)}, u32[]{:S(2)}, u32[]{:S(2)}) %collective-permute-start.15) | collective-permute-done | bytes 524320 | tf_op jit(solution)/shard_map/ppermute | solution.py:150
  117.6 2.1 %collective-permute-done.13.refs_5_ = f32[8,64,256]{2,1,0:T(8,128)S(1)} collective-permute-done((f32[8,64,256]{2,1,0:T(8,128)}, f32[8,64,256]{2,1,0:T(8,128)S(1)}, u32[]{:S(2)}, u32[]{:S(2)}) %collective-permute-start.13) | collective-permute-done | bytes 524320 | tf_op jit(solution)/shard_map/ppermute | solution.py:150
  119.7 2.2 %collective-permute-done.14.refs_6_ = f32[8,64,256]{2,1,0:T(8,128)S(1)} collective-permute-done((f32[8,64,256]{2,1,0:T(8,128)S(1)}, f32[8,64,256]{2,1,0:T(8,128)S(1)}, u32[]{:S(2)}, u32[]{:S(2)}) %collective-permute-start.14) | collective-permute-done | bytes 524320 | tf_op jit(solution)/shard_map/ppermute | solution.py:150
  122.7 3.6 %split_1.1 = (bf16[512,2048]{1,0:T(8,128)(2,1)S(1)}, bf16[512,2048]{1,0:T(8,128)(2,1)}) custom-call(f32[8,64,256]{2,1,0:T(8,128)} %collective-permute-done.7.refs_0_, f32[8,64,256]{2,1,0:T(8,128)} %collective-permute-done.8.refs_1_, f32[8,64,256]{2,1,0:T(8,128)} %copy-done.12, f32[8,64,256]{2,1,0:T(8,128)} %copy-done.11, f32[8,64,256]{2,1,0:T(8,128)} %copy-done.13, ...), custom_call_target="tpu_custom_call" | custom-call | flops 8000000000 | bytes 8000000 | tf_op jit(solution)/shard_map/split_1/pallas_call | solution.py:170
  126.3 11.6 %product_1.1.refs_3_ = f32[16,64,512]{2,1,0:T(8,128)} custom-call(f32[16,8,64,256]{3,2,1,0:T(8,128)} %bitcast.11, bf16[512,2048]{1,0:T(8,128)(2,1)S(1)} %get-tuple-element.26.a_hi, bf16[512,2048]{1,0:T(8,128)(2,1)} %get-tuple-element.27.a_lo_hbm), custom_call_target="tpu_custom_call" | custom-call | flops 8000000000 | bytes 8000000 | tf_op jit(solution)/shard_map/product_1/pallas_call | solution.py:190
  138.0 9.2 %all-to-all-start.2 = ((f32[16,64,512]{2,1,0:T(8,128)}), f32[16,64,512]{2,1,0:T(8,128)}, u32[]{:S(2)}, u32[]{:S(2)}) async-start(f32[16,64,512]{2,1,0:T(8,128)} %product_1.1.refs_3_), calls=%async_computation.2 | async-start | bytes 4194304 | tf_op jit(solution)/shard_map/all_to_all | solution.py:211
  147.7 4.0 %collective-permute-done.16.refs_4_ = f32[16,64,512]{2,1,0:T(8,128)} collective-permute-done((f32[16,64,512]{2,1,0:T(8,128)}, f32[16,64,512]{2,1,0:T(8,128)}, u32[]{:S(2)}, u32[]{:S(2)}) %collective-permute-start.16) | collective-permute-done | bytes 2097184 | tf_op jit(solution)/shard_map/ppermute | solution.py:210
  151.7 43.7 %all-to-all-done.2.refs_5_ = f32[16,64,512]{2,1,0:T(8,128)} async-done(((f32[16,64,512]{2,1,0:T(8,128)}), f32[16,64,512]{2,1,0:T(8,128)}, u32[]{:S(2)}, u32[]{:S(2)}) %all-to-all-start.2) | async-done | bytes 2097184 | tf_op jit(solution)/shard_map/all_to_all | solution.py:211
  195.3 6.1 %finish.1 = f32[8,64,2048]{2,1,0:T(8,128)} custom-call(s32[4]{0:T(128)S(1)} %pad_add_fusion.places, s32[32]{0:T(128)S(1)} %copy-done.1, f32[8]{0:T(128)S(1)} %copy-done.2, f32[64,1]{1,0:T(8,128)S(1)} %copy.7.e_b, f32[1,2048]{1,0:T(1,128)S(1)} %bitcast.9, f32[16,64,512]{2,1,0:T(8,128)} %product_0.1.refs_0_, f32[16,64,512]{2,1,0:T(8,128)} %collective-permute-done.9.refs_1_, ...), custom_call_target="tpu_custom_call" | custom-call | tf_op jit(solution)/shard_map/finish/pallas_call | solution.py:224
  (62 shorter events, 12.0 us)
Async XLA Ops:
  6.5 66.3 %all-gather.3.cloned.1.call-start = ((), (), s32[]{:S(2)}) async-start(), calls=%async_computation.3 | async-start | bytes 8912896 | tf_op jit(solution)/shard_map/all_gather | solution.py:152
  33.4 24.6 %copy-start.3 = (f32[8,64,256]{2,1,0:T(8,128)}, f32[8,64,256]{2,1,0:T(8,128)S(1)}, u32[]{:S(2)}) copy-start(f32[8,64,256]{2,1,0:T(8,128)S(1)} %all_to_all.15.refs_0_) | copy-start | bytes 1572868
  33.4 10.3 %collective-permute-start.2 = (f32[8,64,256]{2,1,0:T(8,128)S(1)}, f32[8,64,256]{2,1,0:T(8,128)S(1)}, u32[]{:S(2)}, u32[]{:S(2)}) collective-permute-start(f32[8,64,256]{2,1,0:T(8,128)S(1)} %all_to_all.15.refs_0_), channel_id=1, source_target_pairs={{0,48},{16,0},{32,16},{48,32},{1,49},{17,1},{33,17},{49,33},{2,50}... | collective-permute-start | bytes 1572872 | tf_op jit(solution)/shard_map/ppermute | solution.py:150
  36.3 10.6 %collective-permute-start.3 = (f32[8,64,256]{2,1,0:T(8,128)S(1)}, f32[8,64,256]{2,1,0:T(8,128)S(1)}, u32[]{:S(2)}, u32[]{:S(2)}) collective-permute-start(f32[8,64,256]{2,1,0:T(8,128)S(1)} %all_to_all.15.refs_0_), channel_id=1, source_target_pairs={{0,16},{16,32},{32,48},{48,0},{1,17},{17,33},{33,49},{49,1},{2,18}... | collective-permute-start | bytes 1572872 | tf_op jit(solution)/shard_map/ppermute | solution.py:150
  36.3 11.9 %collective-permute-start.1 = (f32[8,64,256]{2,1,0:T(8,128)S(1)}, f32[8,64,256]{2,1,0:T(8,128)S(1)}, u32[]{:S(2)}, u32[]{:S(2)}) collective-permute-start(f32[8,64,256]{2,1,0:T(8,128)S(1)} %all_to_all.15.refs_0_), channel_id=1, source_target_pairs={{0,64},{64,128},{128,192},{192,0},{1,65},{65,129},{129,193},{193,1... | collective-permute-start | bytes 1572872 | tf_op jit(solution)/shard_map/ppermute | solution.py:150
  37.5 12.3 %collective-permute-start = (f32[8,64,256]{2,1,0:T(8,128)S(1)}, f32[8,64,256]{2,1,0:T(8,128)S(1)}, u32[]{:S(2)}, u32[]{:S(2)}) collective-permute-start(f32[8,64,256]{2,1,0:T(8,128)S(1)} %all_to_all.15.refs_0_), channel_id=1, source_target_pairs={{0,192},{64,0},{128,64},{192,128},{1,193},{65,1},{129,65},{193,129... | collective-permute-start | bytes 1572872 | tf_op jit(solution)/shard_map/ppermute | solution.py:150
  43.7 14.3 %collective-permute-start.4 = (f32[8,64,256]{2,1,0:T(8,128)S(1)}, f32[8,64,256]{2,1,0:T(8,128)S(1)}, u32[]{:S(2)}, u32[]{:S(2)}) collective-permute-start(f32[8,64,256]{2,1,0:T(8,128)S(1)} %collective-permute-done.2.refs_3_), channel_id=1, source_target_pairs={{0,192},{64,0},{128,64},{192,128},{1,193},{65,1},{129,65},{193,129... | collective-permute-start | bytes 1572872 | tf_op jit(solution)/shard_map/ppermute | solution.py:150
  46.9 11.1 %collective-permute-start.5 = (f32[8,64,256]{2,1,0:T(8,128)S(1)}, f32[8,64,256]{2,1,0:T(8,128)S(1)}, u32[]{:S(2)}, u32[]{:S(2)}) collective-permute-start(f32[8,64,256]{2,1,0:T(8,128)S(1)} %collective-permute-done.3.refs_4_), channel_id=1, source_target_pairs={{0,64},{64,128},{128,192},{192,0},{1,65},{65,129},{129,193},{193,1... | collective-permute-start | bytes 1572872 | tf_op jit(solution)/shard_map/ppermute | solution.py:150
  48.2 9.9 %collective-permute-start.6 = (f32[8,64,256]{2,1,0:T(8,128)S(1)}, f32[8,64,256]{2,1,0:T(8,128)}, u32[]{:S(2)}, u32[]{:S(2)}) collective-permute-start(f32[8,64,256]{2,1,0:T(8,128)S(1)} %collective-permute-done.1.refs_2_), channel_id=1, source_target_pairs={{0,48},{16,0},{32,16},{48,32},{1,49},{17,1},{33,17},{49,33},{2,50}... | collective-permute-start | bytes 1572872 | tf_op jit(solution)/shard_map/ppermute | solution.py:150
  49.8 12.8 %collective-permute-start.7 = (f32[8,64,256]{2,1,0:T(8,128)S(1)}, f32[8,64,256]{2,1,0:T(8,128)}, u32[]{:S(2)}, u32[]{:S(2)}) collective-permute-start(f32[8,64,256]{2,1,0:T(8,128)S(1)} %collective-permute-done.refs_1_), channel_id=1, source_target_pairs={{0,16},{16,32},{32,48},{48,0},{1,17},{17,33},{33,49},{49,1},{2,18}... | collective-permute-start | bytes 1572872 | tf_op jit(solution)/shard_map/ppermute | solution.py:150
  49.8 19.4 %collective-permute-start.8 = (f32[8,64,256]{2,1,0:T(8,128)S(1)}, f32[8,64,256]{2,1,0:T(8,128)}, u32[]{:S(2)}, u32[]{:S(2)}) collective-permute-start(f32[8,64,256]{2,1,0:T(8,128)S(1)} %collective-permute-done.refs_1_), channel_id=1, source_target_pairs={{0,192},{64,0},{128,64},{192,128},{1,193},{65,1},{129,65},{193,129... | collective-permute-start | bytes 1572872 | tf_op jit(solution)/shard_map/ppermute | solution.py:150
  84.5 24.4 %copy-start.7 = (f32[8,64,256]{2,1,0:T(8,128)S(1)}, f32[8,64,256]{2,1,0:T(8,128)}, u32[]{:S(2)}) copy-start(f32[8,64,256]{2,1,0:T(8,128)} %copy-done.6) | copy-start | bytes 1572868
  84.5 20.2 %collective-permute-start.9 = (f32[16,64,512]{2,1,0:T(8,128)}, f32[16,64,512]{2,1,0:T(8,128)}, u32[]{:S(2)}, u32[]{:S(2)}) collective-permute-start(f32[16,64,512]{2,1,0:T(8,128)} %product_0.1.refs_0_), channel_id=1, source_target_pairs={{0,8},{8,0},{1,9},{9,1},{2,10},{10,2},{3,11},{11,3},{4,12},{12,4},... | collective-permute-start | bytes 6291464 | tf_op jit(solution)/shard_map/ppermute | solution.py:210
  86.2 51.8 %all-to-all-start.1 = ((f32[16,64,512]{2,1,0:T(8,128)}), f32[16,64,512]{2,1,0:T(8,128)S(1)}, u32[]{:S(2)}, u32[]{:S(2)}) async-start(f32[16,64,512]{2,1,0:T(8,128)} %product_0.1.refs_0_), calls=%async_computation.1 | async-start | bytes 4194304 | tf_op jit(solution)/shard_map/all_to_all | solution.py:211
  89.9 14.8 %collective-permute-start.11 = (f32[8,64,256]{2,1,0:T(8,128)}, f32[8,64,256]{2,1,0:T(8,128)S(1)}, u32[]{:S(2)}, u32[]{:S(2)}) collective-permute-start(f32[8,64,256]{2,1,0:T(8,128)} %collective-permute-done.6.refs_7_), channel_id=1, source_target_pairs={{0,64},{64,128},{128,192},{192,0},{1,65},{65,129},{129,193},{193,1... | collective-permute-start | bytes 1572872 | tf_op jit(solution)/shard_map/ppermute | solution.py:150
  91.2 17.7 %collective-permute-start.10 = (f32[8,64,256]{2,1,0:T(8,128)S(1)}, f32[8,64,256]{2,1,0:T(8,128)S(1)}, u32[]{:S(2)}, u32[]{:S(2)}) collective-permute-start(f32[8,64,256]{2,1,0:T(8,128)S(1)} %copy-done.5), channel_id=1, source_target_pairs={{0,48},{16,0},{32,16},{48,32},{1,49},{17,1},{33,17},{49,33},{2,50}... | collective-permute-start | bytes 1572872 | tf_op jit(solution)/shard_map/ppermute | solution.py:150
  93.8 15.0 %collective-permute-start.12 = (f32[8,64,256]{2,1,0:T(8,128)}, f32[8,64,256]{2,1,0:T(8,128)S(1)}, u32[]{:S(2)}, u32[]{:S(2)}) collective-permute-start(f32[8,64,256]{2,1,0:T(8,128)} %collective-permute-done.7.refs_0_), channel_id=1, source_target_pairs={{0,16},{16,32},{32,48},{48,0},{1,17},{17,33},{33,49},{49,1},{2,18}... | collective-permute-start | bytes 1572872 | tf_op jit(solution)/shard_map/ppermute | solution.py:150
  104.7 12.9 %collective-permute-start.15 = (f32[8,64,256]{2,1,0:T(8,128)S(1)}, f32[8,64,256]{2,1,0:T(8,128)S(1)}, u32[]{:S(2)}, u32[]{:S(2)}) collective-permute-start(f32[8,64,256]{2,1,0:T(8,128)S(1)} %collective-permute-done.11.refs_3_), channel_id=1, source_target_pairs={{0,48},{16,0},{32,16},{48,32},{1,49},{17,1},{33,17},{49,33},{2,50}... | collective-permute-start | bytes 1572872 | tf_op jit(solution)/shard_map/ppermute | solution.py:150
  107.4 12.3 %collective-permute-start.13 = (f32[8,64,256]{2,1,0:T(8,128)}, f32[8,64,256]{2,1,0:T(8,128)S(1)}, u32[]{:S(2)}, u32[]{:S(2)}) collective-permute-start(f32[8,64,256]{2,1,0:T(8,128)} %collective-permute-done.7.refs_0_), channel_id=1, source_target_pairs={{0,192},{64,0},{128,64},{192,128},{1,193},{65,1},{129,65},{193,129... | collective-permute-start | bytes 1572872 | tf_op jit(solution)/shard_map/ppermute | solution.py:150
  108.8 13.1 %collective-permute-start.14 = (f32[8,64,256]{2,1,0:T(8,128)S(1)}, f32[8,64,256]{2,1,0:T(8,128)S(1)}, u32[]{:S(2)}, u32[]{:S(2)}) collective-permute-start(f32[8,64,256]{2,1,0:T(8,128)S(1)} %copy-done.7), channel_id=1, source_target_pairs={{0,16},{16,32},{32,48},{48,0},{1,17},{17,33},{33,49},{49,1},{2,18}... | collective-permute-start | bytes 1572872 | tf_op jit(solution)/shard_map/ppermute | solution.py:150
  138.0 57.4 %copy-start.1 = (s32[32]{0:T(128)S(1)}, s32[32]{0:T(128)}, u32[]{:S(2)}) copy-start(s32[32]{0:T(128)} %panel_of.1) | copy-start | bytes 388
  138.0 57.4 %copy-start.2 = (f32[8]{0:T(128)S(1)}, f32[8]{0:T(128)}, u32[]{:S(2)}) copy-start(f32[8]{0:T(128)} %e_occ.1) | copy-start | bytes 100
  138.0 57.3 %all-to-all-start.2 = ((f32[16,64,512]{2,1,0:T(8,128)}), f32[16,64,512]{2,1,0:T(8,128)}, u32[]{:S(2)}, u32[]{:S(2)}) async-start(f32[16,64,512]{2,1,0:T(8,128)} %product_1.1.refs_3_), calls=%async_computation.2 | async-start | bytes 4194304 | tf_op jit(solution)/shard_map/all_to_all | solution.py:211
  147.2 4.5 %collective-permute-start.16 = (f32[16,64,512]{2,1,0:T(8,128)}, f32[16,64,512]{2,1,0:T(8,128)}, u32[]{:S(2)}, u32[]{:S(2)}) collective-permute-start(f32[16,64,512]{2,1,0:T(8,128)} %product_1.1.refs_3_), channel_id=1, source_target_pairs={{0,8},{8,0},{1,9},{9,1},{2,10},{10,2},{3,11},{11,3},{4,12},{12,4},... | collective-permute-start | bytes 6291464 | tf_op jit(solution)/shard_map/ppermute | solution.py:210
  (14 other events, 112.1 us)
Sparse Core Ops, SparseCore 0:
  9.2 63.5 all-gather.2

commit v5 on v4

--- a/solution.py
+++ b/solution.py
@@ -99,40 +99,83 @@
         copy.wait()
 
 
-def finish_kernel(dims, pieces, slots, places, panel_of, e_occ, e_b, e_vir, *refs):
-    occ, panel, virtuals = dims
-    out_hbm, slot_of, dir_v, mir_v, out_v, in_sem, out_sem = refs[3 * len(pieces) :]
-    v, x, y, core = places[0], places[1], places[2], places[3]
+def find_slots(slot_of, slots, places, panel_of):
+    x, y, core = places[1], places[2], places[3]
+    for s, ((dx, dy), e) in enumerate(slots):
+        chip = lax.rem(x + dx, SIDE) * SIDE + lax.rem(y + dy, SIDE)
+        slot_of[panel_of[chip * CORES + lax.rem(core + e, CORES)]] = s
+
+
+def pick(data, j, t, slot_of, panel):
+    lanes = 2 * panel
+    lane = lax.broadcasted_iota(jnp.int32, (panel, lanes), 1)
+    sides = []
+    for h in range(2):
+        s = slot_of[2 * t + h]
+        cols = pl.ds(pl.multiple_of((s // 2) * lanes, lanes), lanes)
+        sides.append(pltpu.roll(data(j, cols), lax.rem(s + h, 2) * panel, 1))
+    return jnp.where(lane < panel, sides[0], sides[1])
+
+
+def clear(block, columns):
+    for first, size in columns:
+        block[:, :, first : first + size] = jnp.zeros(block.shape[:2] + (size,), block.dtype)
+
+
+def place_kernel(dims, slots, places, panel_of, own_0, other_0, mirror_0, own_1, other_1, placed_hbm, slot_of, dir_v, mir_v, placed, in_sem, out_sem):
+    occ, panel, virtuals, pieces = dims
+    core = places[3]
     loads = []
     for j in range(occ):
         mine = []
-        for n, (first, size) in enumerate(pieces):
-            own, other, mirror = refs[3 * n : 3 * n + 3]
-            for e in range(CORES):
+        for e in range(CORES):
+            for (first, size), direct in zip(pieces, ((own_0, other_0), (own_1, other_1))):
                 at = (j, slice(None), pl.ds(e * virtuals // 2 + first, size))
-                mine.append(((other if e else own).at[core * occ + j], dir_v.at[at]))
-                mine.append((mirror.at[lax.rem(core + e, CORES) * occ + j], mir_v.at[at]))
+                mine.append((direct[e].at[core * occ + j], dir_v.at[at]))
+            first, size = pieces[0]
+            at = (j, slice(None), pl.ds(e * virtuals // 2 + first, size))
+            mine.append((mirror_0.at[lax.rem(core + e, CORES) * occ + j], mir_v.at[at]))
         loads.append([pltpu.make_async_copy(a, b, in_sem.at[j, n]) for n, (a, b) in enumerate(mine)])
         for copy in loads[j]:
             copy.start()
-    for s, ((dx, dy), e) in enumerate(slots):
-        chip = lax.rem(x + dx, SIDE) * SIDE + lax.rem(y + dy, SIDE)
-        slot_of[panel_of[chip * CORES + lax.rem(core + e, CORES)]] = s
-    lanes = 2 * panel
-    lane = lax.broadcasted_iota(jnp.int32, (panel, lanes), 1)
+    find_slots(slot_of, slots, places, panel_of)
+    first, size = pieces[1]
+    clear(mir_v, [(e * virtuals // 2 + first, size) for e in range(CORES)])
     for j in range(occ):
         for copy in loads[j]:
             copy.wait()
+        for t in range(virtuals // (2 * panel)):
+            part = pick(lambda j, cols: dir_v[j, :, cols] - mir_v[j, :, cols], j, t, slot_of, panel)
+            placed[j, :, t * 2 * panel : (t + 1) * 2 * panel] = part
+        pltpu.make_async_copy(placed.at[j], placed_hbm.at[j], out_sem.at[j]).start()
+    for j in range(occ):
+        pltpu.make_async_copy(placed.at[j], placed_hbm.at[j], out_sem.at[j]).wait()
+
+
+def finish_kernel(dims, slots, places, panel_of, e_occ, e_b, e_vir, placed_hbm, mirror_1, out_hbm, slot_of, mir_v, placed, out_v, in_sem, out_sem):
+    occ, panel, virtuals, pieces = dims
+    v, core = places[0], places[3]
+    first, size = pieces[1]
+    loads = []
+    for j in range(occ):
+        for e in range(CORES):
+            at = (j, slice(None), pl.ds(e * virtuals // 2 + first, size))
+            source = mirror_1.at[lax.rem(core + e, CORES) * occ + j]
+            loads.append(pltpu.make_async_copy(source, mir_v.at[at], in_sem.at[j, e]))
+        loads.append(pltpu.make_async_copy(placed_hbm.at[j], placed.at[j], in_sem.at[j, CORES]))
+    for copy in loads:
+        copy.start()
+    find_slots(slot_of, slots, places, panel_of)
+    first, size = pieces[0]
+    clear(mir_v, [(e * virtuals // 2 + first, size) for e in range(CORES)])
+    for j in range(occ):
+        for copy in loads[(CORES + 1) * j : (CORES + 1) * (j + 1)]:
+            copy.wait()
         base = (e_occ[v] + e_occ[j]) - e_b[...]
-        for t in range(virtuals // lanes):
-            sides = []
-            for h in range(2):
-                s = slot_of[2 * t + h]
-                cols = pl.ds(pl.multiple_of((s // 2) * lanes, lanes), lanes)
-                diff = dir_v[j, :, cols] - mir_v[j, :, cols]
-                sides.append(pltpu.roll(diff, lax.rem(s + h, 2) * panel, 1))
-            cols = slice(t * lanes, (t + 1) * lanes)
-            out_v[j, :, cols] = jnp.where(lane < panel, sides[0], sides[1]) / (base - e_vir[:, cols])
+        for t in range(virtuals // (2 * panel)):
+            cols = slice(t * 2 * panel, (t + 1) * 2 * panel)
+            part = pick(lambda j, cols: mir_v[j, :, cols], j, t, slot_of, panel)
+            out_v[j, :, cols] = (placed[j, :, cols] - part) / (base - e_vir[:, cols])
         pltpu.make_async_copy(out_v.at[j], out_hbm.at[j], out_sem.at[j]).start()
     for j in range(occ):
         pltpu.make_async_copy(out_v.at[j], out_hbm.at[j], out_sem.at[j]).wait()
@@ -213,30 +256,33 @@
         places_of.append((starts[n], size))
         if n == 0:
             int_all = lax.optimization_barrier([int_all, whole])[0]
-            bring(LAST, [swapped])
-    fixed = lambda array, place: array if place is None else pltpu.with_memory_space_constraint(array, place)
-    where = [[pltpu.HBM, pltpu.HBM, pltpu.VMEM], [pltpu.HBM, pltpu.HBM, None]]
-    arrays = [[fixed(*both) for both in zip(*groups)] for groups in zip(arrays, where)]
-
+            bring(LAST, [whole])
     slots = [(chip, e) for e in range(CORES) for chips in sets for chip in chips]
     pair = (index[1] * SIDE + index[2]) * CORES + index[3]
     e_b = lax.dynamic_slice(e_vir, (pair * panel,), (panel,)).reshape(panel, 1)
+    dims = (occ, panel, virtuals, tuple(places_of))
+    block = pltpu.VMEM((occ, panel, virtuals), f32)
+    table = pltpu.SMEM((virtuals // panel,), jnp.int32)
+    (own_0, other_0, mirror_0), (own_1, other_1, mirror_1) = arrays
+    hbm = lambda array: pltpu.with_memory_space_constraint(array, pltpu.HBM)
+    placed = pl.pallas_call(
+        functools.partial(place_kernel, dims, slots),
+        out_shape=pltpu.HBM((occ, panel, virtuals), f32),
+        in_specs=[SMEM, SMEM, ANY, ANY, VMEM, ANY, ANY],
+        out_specs=ANY,
+        scratch_shapes=[table, block, block, block, pltpu.SemaphoreType.DMA((occ, 3 * CORES)), pltpu.SemaphoreType.DMA((occ,))],
+        compiler_params=pltpu.CompilerParams(vmem_limit_bytes=16 * 2**20),
+        name="place",
+    )(places, panel_of, hbm(own_0), hbm(other_0), mirror_0, hbm(own_1), hbm(other_1))
     out = pl.pallas_call(
-        functools.partial(finish_kernel, (occ, panel, virtuals), places_of, slots),
+        functools.partial(finish_kernel, dims, slots),
         out_shape=jax.ShapeDtypeStruct((occ, panel, virtuals), f32),
-        in_specs=[SMEM, SMEM, SMEM, VMEM, VMEM] + [ANY, ANY, VMEM, ANY, ANY, ANY],
+        in_specs=[SMEM, SMEM, SMEM, VMEM, VMEM, ANY, ANY],
         out_specs=ANY,
-        scratch_shapes=[
-            pltpu.SMEM((virtuals // panel,), jnp.int32),
-            pltpu.VMEM((occ, panel, virtuals), f32),
-            pltpu.VMEM((occ, panel, virtuals), f32),
-            pltpu.VMEM((occ, panel, virtuals), f32),
-            pltpu.SemaphoreType.DMA((occ, 2 * CORES * len(sets))),
-            pltpu.SemaphoreType.DMA((occ,)),
-        ],
+        scratch_shapes=[table, block, block, block, pltpu.SemaphoreType.DMA((occ, CORES + 1)), pltpu.SemaphoreType.DMA((occ,))],
         compiler_params=pltpu.CompilerParams(vmem_limit_bytes=16 * 2**20),
         name="finish",
-    )(places, panel_of, e_occ, e_b, e_vir.reshape(1, virtuals), *[a for group in arrays for a in group])
+    )(places, panel_of, e_occ, e_b, e_vir.reshape(1, virtuals), hbm(placed), mirror_1)
     return out[None]
 
 

time: 209 us -> 209 us (level)
  waiting for transfers between devices: 93.2 us -> 84.6 us
  Pallas kernels: 36.6 us -> 42 us
  local copies, waits for them, and re-layouts: 1.93 us -> 5.68 us
    all_to_all x2, waiting for transfers between devices: 43.7 us -> 33.4 us  [body(): lax.all_to_all(sent, ('core', 'virt'), split_axis=0, concat_axis=0, tiled...]
    pallas_call x1 -> x2, Pallas kernels: 6.11 us -> 11.4 us  [the longest x1 5.76 us: body(): pl.pallas_call(functools.partial(place_kernel, dims, slots), out_shape=pl...]
    unnamed x36 -> x42, local copies, waits for them, and re-layouts: 1.76 us -> 5.51 us
    ppermute x2, waiting for transfers between devices: 4.02 us -> 6.7 us  [body(): swapped = lax.ppermute(whole, 'core', [(0, 1), (1, 0)])]
  transfers between devices with their start and end apart: 20 -> 20, of which waited for: 11 -> 13; matrix products, arithmetic and copies ran while one was open for 0% -> 0% of each run, Pallas kernels for 9% -> 12%
where the time goes in v5:
time: 209 us
  waiting for transfers between devices  84.6 us (40%)
  Pallas kernels  42 us (20%)
  starting transfers between devices  36.9 us (18%)
  blocking collectives  26.2 us (13%)
  between operations  13.6 us (7%)
  local copies, waits for them, and re-layouts  5.68 us (3%)
    ppermute x15, waiting for transfers between devices, move(): lax.ppermute(data, name, [(n, (n - step) % SIDE) for n in range(SIDE)])  40.2 us
    all_to_all x2, waiting for transfers between devices, body(): lax.all_to_all(sent, ('core', 'virt'), split_axis=0, concat_axis=0, tiled...  33.4 us
    all_to_all x1, blocking collectives, body(): lax.all_to_all(amps, 'virt', split_axis=0, concat_axis=0, tiled=True)  26.2 us
    pallas_call x2, Pallas kernels, body(): pl.pallas_call(functools.partial(product_kernel, (occ, panel, width)), ou...  23.3 us
    ppermute x15, starting transfers between devices, move(): lax.ppermute(data, name, [(n, (n - step) % SIDE) for n in range(SIDE)])  21.8 us
    all_to_all x2, starting transfers between devices, body(): lax.all_to_all(sent, ('core', 'virt'), split_axis=0, concat_axis=0, tiled...  14.5 us
    pallas_call x2, Pallas kernels, body(): pl.pallas_call(functools.partial(split_kernel, (panel, width, len(chips))...  7.28 us
    ppermute x2, waiting for transfers between devices, body(): swapped = lax.ppermute(whole, 'core', [(0, 1), (1, 0)])  6.7 us
  transfers between devices with their start and end apart: 20, of which 13 were waited for; matrix products, arithmetic and copies ran while one was open for 0% of the time, Pallas kernels for 12%

profile of v5, /device:TPU:1, one launch (start us, length us, event | category | flops | bytes accessed | tf_op | source)
XLA Modules:
  0.0 209.0 jit_solution(12458842266007019277)
XLA Ops:
  7.3 26.2 %all_to_all.15.refs_0_ = f32[8,64,256]{2,1,0:T(8,128)S(1)} all-to-all(f32[8,64,256]{2,1,0:T(8,128)} %param.5), channel_id=1, replica_groups=mesh['x'=4,'y'=4,'core'=2,'virt'=8] {'virt'}, dimensions={0} | all-to-all | bytes 1048576 | tf_op jit(solution)/shard_map/all_to_all | solution.py:196
  33.4 2.9 %collective-permute-start.2 = (f32[8,64,256]{2,1,0:T(8,128)S(1)}, f32[8,64,256]{2,1,0:T(8,128)S(1)}, u32[]{:S(2)}, u32[]{:S(2)}) collective-permute-start(f32[8,64,256]{2,1,0:T(8,128)S(1)} %all_to_all.15.refs_0_), channel_id=1, source_target_pairs={{0,48},{16,0},{32,16},{48,32},{1,49},{17,1},{33,17},{49,33},{2,50}... | collective-permute-start | bytes 1572872 | tf_op jit(solution)/shard_map/ppermute | solution.py:193
  39.0 4.7 %collective-permute-done.2.refs_3_ = f32[8,64,256]{2,1,0:T(8,128)S(1)} collective-permute-done((f32[8,64,256]{2,1,0:T(8,128)S(1)}, f32[8,64,256]{2,1,0:T(8,128)S(1)}, u32[]{:S(2)}, u32[]{:S(2)}) %collective-permute-start.2) | collective-permute-done | bytes 524320 | tf_op jit(solution)/shard_map/ppermute | solution.py:193
  43.7 2.5 %collective-permute-start.4 = (f32[8,64,256]{2,1,0:T(8,128)S(1)}, f32[8,64,256]{2,1,0:T(8,128)S(1)}, u32[]{:S(2)}, u32[]{:S(2)}) collective-permute-start(f32[8,64,256]{2,1,0:T(8,128)S(1)} %collective-permute-done.2.refs_3_), channel_id=1, source_target_pairs={{0,192},{64,0},{128,64},{192,128},{1,193},{65,1},{129,65},{193,129... | collective-permute-start | bytes 1572872 | tf_op jit(solution)/shard_map/ppermute | solution.py:193
  49.8 2.8 %collective-permute-start.8 = (f32[8,64,256]{2,1,0:T(8,128)S(1)}, f32[8,64,256]{2,1,0:T(8,128)}, u32[]{:S(2)}, u32[]{:S(2)}) collective-permute-start(f32[8,64,256]{2,1,0:T(8,128)S(1)} %collective-permute-done.refs_1_), channel_id=1, source_target_pairs={{0,192},{64,0},{128,64},{192,128},{1,193},{65,1},{129,65},{193,129... | collective-permute-start | bytes 1572872 | tf_op jit(solution)/shard_map/ppermute | solution.py:193
  52.7 5.3 %collective-permute-done.4.refs_5_ = f32[8,64,256]{2,1,0:T(8,128)S(1)} collective-permute-done((f32[8,64,256]{2,1,0:T(8,128)S(1)}, f32[8,64,256]{2,1,0:T(8,128)S(1)}, u32[]{:S(2)}, u32[]{:S(2)}) %collective-permute-start.4) | collective-permute-done | bytes 524320 | tf_op jit(solution)/shard_map/ppermute | solution.py:193
  59.8 3.7 %split_0.1 = (bf16[512,2048]{1,0:T(8,128)(2,1)S(1)}, bf16[512,2048]{1,0:T(8,128)(2,1)}) custom-call(f32[8,64,256]{2,1,0:T(8,128)} %copy-done.5, f32[8,64,256]{2,1,0:T(8,128)} %copy-done.12, f32[8,64,256]{2,1,0:T(8,128)} %copy-done.13, f32[8,64,256]{2,1,0:T(8,128)} %copy-done.6, f32[8,64,256]{2,1,0:T(8,128)} %copy-done.11, f32[8,64,256]{2,1,0:T(8,128)} %copy-done.16, ...), custom_call_target="tpu_custom_call" | custom-call | flops 60000002048 | bytes 60000000 | tf_op jit(solution)/shard_map/split_0/pallas_call | solution.py:213
  63.5 5.7 %collective-permute-done.8.refs_1_ = f32[8,64,256]{2,1,0:T(8,128)} collective-permute-done((f32[8,64,256]{2,1,0:T(8,128)S(1)}, f32[8,64,256]{2,1,0:T(8,128)}, u32[]{:S(2)}, u32[]{:S(2)}) %collective-permute-start.8) | collective-permute-done | bytes 524320 | tf_op jit(solution)/shard_map/ppermute | solution.py:193
  69.2 3.6 %all-gather.3.cloned.1.call-done = f32[128,64,256]{2,1,0:T(8,128)} async-done(((f32[8,64,256]{2,1,0:T(8,128)}), f32[128,64,256]{2,1,0:T(8,128)}) %all-gather.3.cloned.1.call-update) | async-done | bytes 8388624 | tf_op jit(solution)/shard_map/all_gather | solution.py:195
  72.8 11.6 %product_0.1.own_0 = f32[16,64,512]{2,1,0:T(8,128)} custom-call(f32[16,8,64,256]{3,2,1,0:T(8,128)} %bitcast.10, bf16[512,2048]{1,0:T(8,128)(2,1)S(1)} %get-tuple-element.20.a_hi, bf16[512,2048]{1,0:T(8,128)(2,1)} %get-tuple-element.21.a_lo_hbm), custom_call_target="tpu_custom_call" | custom-call | flops 60000002048 | bytes 60000000 | tf_op jit(solution)/shard_map/product_0/pallas_call | solution.py:233
  84.5 5.3 %all-to-all-start.1 = ((f32[16,64,512]{2,1,0:T(8,128)}), f32[16,64,512]{2,1,0:T(8,128)S(1)}, u32[]{:S(2)}, u32[]{:S(2)}) async-start(f32[16,64,512]{2,1,0:T(8,128)} %product_0.1.own_0), calls=%async_computation.1 | async-start | bytes 4194304 | tf_op jit(solution)/shard_map/all_to_all | solution.py:254
  91.0 2.7 %collective-permute-start.10 = (f32[8,64,256]{2,1,0:T(8,128)S(1)}, f32[8,64,256]{2,1,0:T(8,128)S(1)}, u32[]{:S(2)}, u32[]{:S(2)}) collective-permute-start(f32[8,64,256]{2,1,0:T(8,128)S(1)} %copy-done.7), channel_id=1, source_target_pairs={{0,48},{16,0},{32,16},{48,32},{1,49},{17,1},{33,17},{49,33},{2,50}... | collective-permute-start | bytes 1572872 | tf_op jit(solution)/shard_map/ppermute | solution.py:193
  93.7 10.8 %collective-permute-done.11.refs_3_ = f32[8,64,256]{2,1,0:T(8,128)S(1)} collective-permute-done((f32[8,64,256]{2,1,0:T(8,128)}, f32[8,64,256]{2,1,0:T(8,128)S(1)}, u32[]{:S(2)}, u32[]{:S(2)}) %collective-permute-start.11) | collective-permute-done | bytes 524320 | tf_op jit(solution)/shard_map/ppermute | solution.py:193
  104.5 2.7 %collective-permute-start.15 = (f32[8,64,256]{2,1,0:T(8,128)S(1)}, f32[8,64,256]{2,1,0:T(8,128)S(1)}, u32[]{:S(2)}, u32[]{:S(2)}) collective-permute-start(f32[8,64,256]{2,1,0:T(8,128)S(1)} %collective-permute-done.11.refs_3_), channel_id=1, source_target_pairs={{0,48},{16,0},{32,16},{48,32},{1,49},{17,1},{33,17},{49,33},{2,50}... | collective-permute-start | bytes 1572872 | tf_op jit(solution)/shard_map/ppermute | solution.py:193
  108.7 8.7 %collective-permute-done.15.refs_7_ = f32[8,64,256]{2,1,0:T(8,128)S(1)} collective-permute-done((f32[8,64,256]{2,1,0:T(8,128)S(1)}, f32[8,64,256]{2,1,0:T(8,128)S(1)}, u32[]{:S(2)}, u32[]{:S(2)}) %collective-permute-start.15) | collective-permute-done | bytes 524320 | tf_op jit(solution)/shard_map/ppermute | solution.py:193
  119.5 2.2 %collective-permute-done.14.refs_6_ = f32[8,64,256]{2,1,0:T(8,128)S(1)} collective-permute-done((f32[8,64,256]{2,1,0:T(8,128)S(1)}, f32[8,64,256]{2,1,0:T(8,128)S(1)}, u32[]{:S(2)}, u32[]{:S(2)}) %collective-permute-start.14) | collective-permute-done | bytes 524320 | tf_op jit(solution)/shard_map/ppermute | solution.py:193
  122.4 3.6 %split_1.1 = (bf16[512,2048]{1,0:T(8,128)(2,1)S(1)}, bf16[512,2048]{1,0:T(8,128)(2,1)}) custom-call(f32[8,64,256]{2,1,0:T(8,128)} %collective-permute-done.7.refs_0_, f32[8,64,256]{2,1,0:T(8,128)} %collective-permute-done.8.refs_1_, f32[8,64,256]{2,1,0:T(8,128)} %copy-done.15, f32[8,64,256]{2,1,0:T(8,128)} %copy-done.14, f32[8,64,256]{2,1,0:T(8,128)} %copy-done.17, ...), custom_call_target="tpu_custom_call" | custom-call | flops 8000000000 | bytes 8000000 | tf_op jit(solution)/shard_map/split_1/pallas_call | solution.py:213
  126.1 11.7 %product_1.1.own_1 = f32[16,64,512]{2,1,0:T(8,128)} custom-call(f32[16,8,64,256]{3,2,1,0:T(8,128)} %bitcast.11, bf16[512,2048]{1,0:T(8,128)(2,1)S(1)} %get-tuple-element.26.a_hi, bf16[512,2048]{1,0:T(8,128)(2,1)} %get-tuple-element.27.a_lo_hbm), custom_call_target="tpu_custom_call" | custom-call | flops 8000000000 | bytes 8000000 | tf_op jit(solution)/shard_map/product_1/pallas_call | solution.py:233
  139.2 9.2 %all-to-all-start.2 = ((f32[16,64,512]{2,1,0:T(8,128)}), f32[16,64,512]{2,1,0:T(8,128)S(1)}, u32[]{:S(2)}, u32[]{:S(2)}) async-start(f32[16,64,512]{2,1,0:T(8,128)} %product_1.1.own_1), calls=%async_computation.2 | async-start | bytes 4194304 | tf_op jit(solution)/shard_map/all_to_all | solution.py:254
  149.2 3.7 %collective-permute-done.9.other_0 = f32[16,64,512]{2,1,0:T(8,128)} collective-permute-done((f32[16,64,512]{2,1,0:T(8,128)}, f32[16,64,512]{2,1,0:T(8,128)}, u32[]{:S(2)}, u32[]{:S(2)}) %collective-permute-start.9) | collective-permute-done | bytes 2097184 | tf_op jit(solution)/shard_map/ppermute | solution.py:253
  152.9 3.0 %collective-permute-done.16.other_1 = f32[16,64,512]{2,1,0:T(8,128)} collective-permute-done((f32[16,64,512]{2,1,0:T(8,128)}, f32[16,64,512]{2,1,0:T(8,128)}, u32[]{:S(2)}, u32[]{:S(2)}) %collective-permute-start.16) | collective-permute-done | bytes 2097184 | tf_op jit(solution)/shard_map/ppermute | solution.py:253
  157.5 5.8 %place.1.placed_hbm = f32[8,64,2048]{2,1,0:T(8,128)} custom-call(s32[4]{0:T(128)S(1)} %pad_add_fusion.places, s32[32]{0:T(128)S(1)} %copy-done.3, f32[16,64,512]{2,1,0:T(8,128)} %product_0.1.own_0, f32[16,64,512]{2,1,0:T(8,128)} %collective-permute-done.9.other_0, f32[16,64,512]{2,1,0:T(8,128)S(1)} %copy-done.1, f32[16,64,512]{2,1,0:T(8,128)} %product_1.1.own_1, ...), custom_call_target="tpu_custom_call" | custom-call | tf_op jit(solution)/shard_map/place/pallas_call | solution.py:268
  163.2 33.2 %all-to-all-done.2.mirror_1 = f32[16,64,512]{2,1,0:T(8,128)S(1)} async-done(((f32[16,64,512]{2,1,0:T(8,128)}), f32[16,64,512]{2,1,0:T(8,128)S(1)}, u32[]{:S(2)}, u32[]{:S(2)}) %all-to-all-start.2) | async-done | bytes 2097184 | tf_op jit(solution)/shard_map/all_to_all | solution.py:254
  196.4 5.7 %finish.1 = f32[8,64,2048]{2,1,0:T(8,128)} custom-call(s32[4]{0:T(128)S(1)} %pad_add_fusion.places, s32[32]{0:T(128)S(1)} %copy-done.3, f32[8]{0:T(128)S(1)} %copy-done.4, f32[64,1]{1,0:T(8,128)S(1)} %copy.7.e_b, f32[1,2048]{1,0:T(1,128)S(1)} %bitcast.9, f32[8,64,2048]{2,1,0:T(8,128)} %place.1.placed_hbm, f32[16,64,512]{2,1,0:T(8,128)S(1)} %all-to-all-done.2.mirror_1), custom_call_target="tpu_custom_call" | custom-call | tf_op jit(solution)/shard_map/finish/pallas_call | solution.py:277
  (69 shorter events, 18.3 us)
Async XLA Ops:
  6.5 66.3 %all-gather.3.cloned.1.call-start = ((), (), s32[]{:S(2)}) async-start(), calls=%async_computation.3 | async-start | bytes 8912896 | tf_op jit(solution)/shard_map/all_gather | solution.py:195
  33.4 24.6 %copy-start.5 = (f32[8,64,256]{2,1,0:T(8,128)}, f32[8,64,256]{2,1,0:T(8,128)S(1)}, u32[]{:S(2)}) copy-start(f32[8,64,256]{2,1,0:T(8,128)S(1)} %all_to_all.15.refs_0_) | copy-start | bytes 1572868
  33.4 10.3 %collective-permute-start.2 = (f32[8,64,256]{2,1,0:T(8,128)S(1)}, f32[8,64,256]{2,1,0:T(8,128)S(1)}, u32[]{:S(2)}, u32[]{:S(2)}) collective-permute-start(f32[8,64,256]{2,1,0:T(8,128)S(1)} %all_to_all.15.refs_0_), channel_id=1, source_target_pairs={{0,48},{16,0},{32,16},{48,32},{1,49},{17,1},{33,17},{49,33},{2,50}... | collective-permute-start | bytes 1572872 | tf_op jit(solution)/shard_map/ppermute | solution.py:193
  36.3 10.6 %collective-permute-start.3 = (f32[8,64,256]{2,1,0:T(8,128)S(1)}, f32[8,64,256]{2,1,0:T(8,128)S(1)}, u32[]{:S(2)}, u32[]{:S(2)}) collective-permute-start(f32[8,64,256]{2,1,0:T(8,128)S(1)} %all_to_all.15.refs_0_), channel_id=1, source_target_pairs={{0,16},{16,32},{32,48},{48,0},{1,17},{17,33},{33,49},{49,1},{2,18}... | collective-permute-start | bytes 1572872 | tf_op jit(solution)/shard_map/ppermute | solution.py:193
  36.3 11.9 %collective-permute-start.1 = (f32[8,64,256]{2,1,0:T(8,128)S(1)}, f32[8,64,256]{2,1,0:T(8,128)S(1)}, u32[]{:S(2)}, u32[]{:S(2)}) collective-permute-start(f32[8,64,256]{2,1,0:T(8,128)S(1)} %all_to_all.15.refs_0_), channel_id=1, source_target_pairs={{0,64},{64,128},{128,192},{192,0},{1,65},{65,129},{129,193},{193,1... | collective-permute-start | bytes 1572872 | tf_op jit(solution)/shard_map/ppermute | solution.py:193
  37.5 12.3 %collective-permute-start = (f32[8,64,256]{2,1,0:T(8,128)S(1)}, f32[8,64,256]{2,1,0:T(8,128)S(1)}, u32[]{:S(2)}, u32[]{:S(2)}) collective-permute-start(f32[8,64,256]{2,1,0:T(8,128)S(1)} %all_to_all.15.refs_0_), channel_id=1, source_target_pairs={{0,192},{64,0},{128,64},{192,128},{1,193},{65,1},{129,65},{193,129... | collective-permute-start | bytes 1572872 | tf_op jit(solution)/shard_map/ppermute | solution.py:193
  43.7 14.3 %collective-permute-start.4 = (f32[8,64,256]{2,1,0:T(8,128)S(1)}, f32[8,64,256]{2,1,0:T(8,128)S(1)}, u32[]{:S(2)}, u32[]{:S(2)}) collective-permute-start(f32[8,64,256]{2,1,0:T(8,128)S(1)} %collective-permute-done.2.refs_3_), channel_id=1, source_target_pairs={{0,192},{64,0},{128,64},{192,128},{1,193},{65,1},{129,65},{193,129... | collective-permute-start | bytes 1572872 | tf_op jit(solution)/shard_map/ppermute | solution.py:193
  46.9 11.1 %collective-permute-start.5 = (f32[8,64,256]{2,1,0:T(8,128)S(1)}, f32[8,64,256]{2,1,0:T(8,128)S(1)}, u32[]{:S(2)}, u32[]{:S(2)}) collective-permute-start(f32[8,64,256]{2,1,0:T(8,128)S(1)} %collective-permute-done.3.refs_4_), channel_id=1, source_target_pairs={{0,64},{64,128},{128,192},{192,0},{1,65},{65,129},{129,193},{193,1... | collective-permute-start | bytes 1572872 | tf_op jit(solution)/shard_map/ppermute | solution.py:193
  48.2 9.9 %collective-permute-start.6 = (f32[8,64,256]{2,1,0:T(8,128)S(1)}, f32[8,64,256]{2,1,0:T(8,128)S(1)}, u32[]{:S(2)}, u32[]{:S(2)}) collective-permute-start(f32[8,64,256]{2,1,0:T(8,128)S(1)} %collective-permute-done.1.refs_2_), channel_id=1, source_target_pairs={{0,48},{16,0},{32,16},{48,32},{1,49},{17,1},{33,17},{49,33},{2,50}... | collective-permute-start | bytes 1572872 | tf_op jit(solution)/shard_map/ppermute | solution.py:193
  49.8 13.7 %collective-permute-start.7 = (f32[8,64,256]{2,1,0:T(8,128)S(1)}, f32[8,64,256]{2,1,0:T(8,128)}, u32[]{:S(2)}, u32[]{:S(2)}) collective-permute-start(f32[8,64,256]{2,1,0:T(8,128)S(1)} %collective-permute-done.refs_1_), channel_id=1, source_target_pairs={{0,16},{16,32},{32,48},{48,0},{1,17},{17,33},{33,49},{49,1},{2,18}... | collective-permute-start | bytes 1572872 | tf_op jit(solution)/shard_map/ppermute | solution.py:193
  49.8 19.4 %collective-permute-start.8 = (f32[8,64,256]{2,1,0:T(8,128)S(1)}, f32[8,64,256]{2,1,0:T(8,128)}, u32[]{:S(2)}, u32[]{:S(2)}) collective-permute-start(f32[8,64,256]{2,1,0:T(8,128)S(1)} %collective-permute-done.refs_1_), channel_id=1, source_target_pairs={{0,192},{64,0},{128,64},{192,128},{1,193},{65,1},{129,65},{193,129... | collective-permute-start | bytes 1572872 | tf_op jit(solution)/shard_map/ppermute | solution.py:193
  84.5 24.2 %copy-start.9 = (f32[8,64,256]{2,1,0:T(8,128)S(1)}, f32[8,64,256]{2,1,0:T(8,128)}, u32[]{:S(2)}) copy-start(f32[8,64,256]{2,1,0:T(8,128)} %copy-done.8) | copy-start | bytes 1572868
  84.5 53.4 %all-to-all-start.1 = ((f32[16,64,512]{2,1,0:T(8,128)}), f32[16,64,512]{2,1,0:T(8,128)S(1)}, u32[]{:S(2)}, u32[]{:S(2)}) async-start(f32[16,64,512]{2,1,0:T(8,128)} %product_0.1.own_0), calls=%async_computation.1 | async-start | bytes 4194304 | tf_op jit(solution)/shard_map/all_to_all | solution.py:254
  89.8 14.7 %collective-permute-start.11 = (f32[8,64,256]{2,1,0:T(8,128)}, f32[8,64,256]{2,1,0:T(8,128)S(1)}, u32[]{:S(2)}, u32[]{:S(2)}) collective-permute-start(f32[8,64,256]{2,1,0:T(8,128)} %copy-done.10), channel_id=1, source_target_pairs={{0,64},{64,128},{128,192},{192,0},{1,65},{65,129},{129,193},{193,1... | collective-permute-start | bytes 1572872 | tf_op jit(solution)/shard_map/ppermute | solution.py:193
  91.0 17.6 %collective-permute-start.10 = (f32[8,64,256]{2,1,0:T(8,128)S(1)}, f32[8,64,256]{2,1,0:T(8,128)S(1)}, u32[]{:S(2)}, u32[]{:S(2)}) collective-permute-start(f32[8,64,256]{2,1,0:T(8,128)S(1)} %copy-done.7), channel_id=1, source_target_pairs={{0,48},{16,0},{32,16},{48,32},{1,49},{17,1},{33,17},{49,33},{2,50}... | collective-permute-start | bytes 1572872 | tf_op jit(solution)/shard_map/ppermute | solution.py:193
  93.7 15.0 %collective-permute-start.12 = (f32[8,64,256]{2,1,0:T(8,128)}, f32[8,64,256]{2,1,0:T(8,128)S(1)}, u32[]{:S(2)}, u32[]{:S(2)}) collective-permute-start(f32[8,64,256]{2,1,0:T(8,128)} %collective-permute-done.7.refs_0_), channel_id=1, source_target_pairs={{0,16},{16,32},{32,48},{48,0},{1,17},{17,33},{33,49},{49,1},{2,18}... | collective-permute-start | bytes 1572872 | tf_op jit(solution)/shard_map/ppermute | solution.py:193
  104.5 12.8 %collective-permute-start.15 = (f32[8,64,256]{2,1,0:T(8,128)S(1)}, f32[8,64,256]{2,1,0:T(8,128)S(1)}, u32[]{:S(2)}, u32[]{:S(2)}) collective-permute-start(f32[8,64,256]{2,1,0:T(8,128)S(1)} %collective-permute-done.11.refs_3_), channel_id=1, source_target_pairs={{0,48},{16,0},{32,16},{48,32},{1,49},{17,1},{33,17},{49,33},{2,50}... | collective-permute-start | bytes 1572872 | tf_op jit(solution)/shard_map/ppermute | solution.py:193
  107.2 12.3 %collective-permute-start.13 = (f32[8,64,256]{2,1,0:T(8,128)}, f32[8,64,256]{2,1,0:T(8,128)S(1)}, u32[]{:S(2)}, u32[]{:S(2)}) collective-permute-start(f32[8,64,256]{2,1,0:T(8,128)} %collective-permute-done.7.refs_0_), channel_id=1, source_target_pairs={{0,192},{64,0},{128,64},{192,128},{1,193},{65,1},{129,65},{193,129... | collective-permute-start | bytes 1572872 | tf_op jit(solution)/shard_map/ppermute | solution.py:193
  108.6 13.0 %collective-permute-start.14 = (f32[8,64,256]{2,1,0:T(8,128)S(1)}, f32[8,64,256]{2,1,0:T(8,128)S(1)}, u32[]{:S(2)}, u32[]{:S(2)}) collective-permute-start(f32[8,64,256]{2,1,0:T(8,128)S(1)} %copy-done.9), channel_id=1, source_target_pairs={{0,16},{16,32},{32,48},{48,0},{1,17},{17,33},{33,49},{49,1},{2,18}... | collective-permute-start | bytes 1572872 | tf_op jit(solution)/shard_map/ppermute | solution.py:193
  137.7 18.2 %copy-start.3 = (s32[32]{0:T(128)S(1)}, s32[32]{0:T(128)}, u32[]{:S(2)}) copy-start(s32[32]{0:T(128)} %panel_of.3) | copy-start | bytes 388
  139.2 57.2 %all-to-all-start.2 = ((f32[16,64,512]{2,1,0:T(8,128)}), f32[16,64,512]{2,1,0:T(8,128)S(1)}, u32[]{:S(2)}, u32[]{:S(2)}) async-start(f32[16,64,512]{2,1,0:T(8,128)} %product_1.1.own_1), calls=%async_computation.2 | async-start | bytes 4194304 | tf_op jit(solution)/shard_map/all_to_all | solution.py:254
  148.4 4.5 %collective-permute-start.9 = (f32[16,64,512]{2,1,0:T(8,128)}, f32[16,64,512]{2,1,0:T(8,128)}, u32[]{:S(2)}, u32[]{:S(2)}) collective-permute-start(f32[16,64,512]{2,1,0:T(8,128)} %product_0.1.own_0), channel_id=1, source_target_pairs={{0,8},{8,0},{1,9},{9,1},{2,10},{10,2},{3,11},{11,3},{4,12},{12,4},... | collective-permute-start | bytes 6291464 | tf_op jit(solution)/shard_map/ppermute | solution.py:253
  148.6 7.3 %collective-permute-start.16 = (f32[16,64,512]{2,1,0:T(8,128)}, f32[16,64,512]{2,1,0:T(8,128)}, u32[]{:S(2)}, u32[]{:S(2)}) collective-permute-start(f32[16,64,512]{2,1,0:T(8,128)} %product_1.1.own_1), channel_id=1, source_target_pairs={{0,8},{8,0},{1,9},{9,1},{2,10},{10,2},{3,11},{11,3},{4,12},{12,4},... | collective-permute-start | bytes 6291464 | tf_op jit(solution)/shard_map/ppermute | solution.py:253
  149.1 47.3 %copy-start.4 = (f32[8]{0:T(128)S(1)}, f32[8]{0:T(128)}, u32[]{:S(2)}) copy-start(f32[8]{0:T(128)} %e_occ.1) | copy-start | bytes 100
  (17 other events, 117.3 us)
Sparse Core Ops, SparseCore 0:
  9.2 63.5 all-gather.2

commit v6 on v4

--- a/solution.py
+++ b/solution.py
@@ -30,7 +30,7 @@
     ((2, 1), (-1, 0)),
     ((1, 2), (0, -1)),
 ]
-LAST = [((2, -1), (1, 0)), ((-1, 2), (0, -1)), ((2, 2), (0, 1))]
+LAST = [((2, -1), (1, 0)), ((-1, 2), (0, -1)), ((2, 2), (0, 2))]
 SETS = [
     [(0, 0), (1, 0), (-1, 0), (0, 1), (0, -1), (1, 1), (-1, -1), (-1, 1)],
     [(1, -1), (2, 0), (0, 2), (2, 1), (1, 2), (2, -1), (-1, 2), (2, 2)],
@@ -213,7 +213,7 @@
         places_of.append((starts[n], size))
         if n == 0:
             int_all = lax.optimization_barrier([int_all, whole])[0]
-            bring(LAST, [swapped])
+            bring(LAST, [whole])
     fixed = lambda array, place: array if place is None else pltpu.with_memory_space_constraint(array, place)
     where = [[pltpu.HBM, pltpu.HBM, pltpu.VMEM], [pltpu.HBM, pltpu.HBM, None]]
     arrays = [[fixed(*both) for both in zip(*groups)] for groups in zip(arrays, where)]

time: 209 us -> 216 us (1.033)
  waiting for transfers between devices: 93.2 us -> 101 us
    ppermute x15, waiting for transfers between devices: 41.2 us -> 49.4 us  [move(): lax.ppermute(data, name, [(n, (n - step) % SIDE) for n in range(SIDE)])]
    all_to_all x2, waiting for transfers between devices: 43.7 us -> 40.7 us  [body(): lax.all_to_all(sent, ('core', 'virt'), split_axis=0, concat_axis=0, tiled...]
    ppermute x2, waiting for transfers between devices: 4.02 us -> 6.74 us  [body(): swapped = lax.ppermute(whole, 'core', [(0, 1), (1, 0)])]
where the time goes in v6:
time: 216 us
  waiting for transfers between devices  101 us (47%)
  Pallas kernels  36.7 us (17%)
  starting transfers between devices  35.5 us (16%)
  blocking collectives  26.2 us (12%)
  between operations  13.6 us (6%)
  local copies, waits for them, and re-layouts  2.69 us (1%)
    ppermute x15, waiting for transfers between devices, move(): lax.ppermute(data, name, [(n, (n - step) % SIDE) for n in range(SIDE)])  49.4 us
    all_to_all x2, waiting for transfers between devices, body(): lax.all_to_all(sent, ('core', 'virt'), split_axis=0, concat_axis=0, tiled...  40.7 us
    all_to_all x1, blocking collectives, body(): lax.all_to_all(amps, 'virt', split_axis=0, concat_axis=0, tiled=True)  26.2 us
    pallas_call x2, Pallas kernels, body(): pl.pallas_call(functools.partial(product_kernel, (occ, panel, width)), ou...  23.3 us
    ppermute x15, starting transfers between devices, move(): lax.ppermute(data, name, [(n, (n - step) % SIDE) for n in range(SIDE)])  21.5 us
    all_to_all x2, starting transfers between devices, body(): lax.all_to_all(sent, ('core', 'virt'), split_axis=0, concat_axis=0, tiled...  13.5 us
    pallas_call x2, Pallas kernels, body(): pl.pallas_call(functools.partial(split_kernel, (panel, width, len(chips))...  7.28 us
    ppermute x2, waiting for transfers between devices, body(): swapped = lax.ppermute(whole, 'core', [(0, 1), (1, 0)])  6.74 us
  transfers between devices with their start and end apart: 20, of which 11 were waited for; matrix products, arithmetic and copies ran while one was open for 0% of the time, Pallas kernels for 9%

profile of v6, /device:TPU:1, one launch (start us, length us, event | category | flops | bytes accessed | tf_op | source)
XLA Modules:
  0.0 215.7 jit_solution(10713769749634655939)
XLA Ops:
  7.3 26.2 %all_to_all.15.refs_0_ = f32[8,64,256]{2,1,0:T(8,128)S(1)} all-to-all(f32[8,64,256]{2,1,0:T(8,128)} %param.5), channel_id=1, replica_groups=mesh['x'=4,'y'=4,'core'=2,'virt'=8] {'virt'}, dimensions={0} | all-to-all | bytes 1048576 | tf_op jit(solution)/shard_map/all_to_all | solution.py:153
  33.4 2.9 %collective-permute-start.2 = (f32[8,64,256]{2,1,0:T(8,128)S(1)}, f32[8,64,256]{2,1,0:T(8,128)S(1)}, u32[]{:S(2)}, u32[]{:S(2)}) collective-permute-start(f32[8,64,256]{2,1,0:T(8,128)S(1)} %all_to_all.15.refs_0_), channel_id=1, source_target_pairs={{0,48},{16,0},{32,16},{48,32},{1,49},{17,1},{33,17},{49,33},{2,50}... | collective-permute-start | bytes 1572872 | tf_op jit(solution)/shard_map/ppermute | solution.py:150
  39.0 4.7 %collective-permute-done.2.refs_3_ = f32[8,64,256]{2,1,0:T(8,128)S(1)} collective-permute-done((f32[8,64,256]{2,1,0:T(8,128)S(1)}, f32[8,64,256]{2,1,0:T(8,128)S(1)}, u32[]{:S(2)}, u32[]{:S(2)}) %collective-permute-start.2) | collective-permute-done | bytes 524320 | tf_op jit(solution)/shard_map/ppermute | solution.py:150
  43.7 2.5 %collective-permute-start.4 = (f32[8,64,256]{2,1,0:T(8,128)S(1)}, f32[8,64,256]{2,1,0:T(8,128)S(1)}, u32[]{:S(2)}, u32[]{:S(2)}) collective-permute-start(f32[8,64,256]{2,1,0:T(8,128)S(1)} %collective-permute-done.2.refs_3_), channel_id=1, source_target_pairs={{0,192},{64,0},{128,64},{192,128},{1,193},{65,1},{129,65},{193,129... | collective-permute-start | bytes 1572872 | tf_op jit(solution)/shard_map/ppermute | solution.py:150
  48.2 1.7 collective-permute-start.6
  49.8 2.8 %collective-permute-start.8 = (f32[8,64,256]{2,1,0:T(8,128)S(1)}, f32[8,64,256]{2,1,0:T(8,128)}, u32[]{:S(2)}, u32[]{:S(2)}) collective-permute-start(f32[8,64,256]{2,1,0:T(8,128)S(1)} %collective-permute-done.refs_1_), channel_id=1, source_target_pairs={{0,192},{64,0},{128,64},{192,128},{1,193},{65,1},{129,65},{193,129... | collective-permute-start | bytes 1572872 | tf_op jit(solution)/shard_map/ppermute | solution.py:150
  52.7 5.3 %collective-permute-done.4.refs_5_ = f32[8,64,256]{2,1,0:T(8,128)S(1)} collective-permute-done((f32[8,64,256]{2,1,0:T(8,128)S(1)}, f32[8,64,256]{2,1,0:T(8,128)S(1)}, u32[]{:S(2)}, u32[]{:S(2)}) %collective-permute-start.4) | collective-permute-done | bytes 524320 | tf_op jit(solution)/shard_map/ppermute | solution.py:150
  59.0 3.7 %split_0.1 = (bf16[512,2048]{1,0:T(8,128)(2,1)S(1)}, bf16[512,2048]{1,0:T(8,128)(2,1)}) custom-call(f32[8,64,256]{2,1,0:T(8,128)} %copy-done.3, f32[8,64,256]{2,1,0:T(8,128)} %copy-done.9, f32[8,64,256]{2,1,0:T(8,128)} %copy-done.10, f32[8,64,256]{2,1,0:T(8,128)} %copy-done.4, f32[8,64,256]{2,1,0:T(8,128)} %copy-done.8, f32[8,64,256]{2,1,0:T(8,128)} %copy-done.13, ...), custom_call_target="tpu_custom_call" | custom-call | flops 60000002048 | bytes 60000000 | tf_op jit(solution)/shard_map/split_0/pallas_call | solution.py:170
  62.7 6.6 %collective-permute-done.8.refs_1_ = f32[8,64,256]{2,1,0:T(8,128)} collective-permute-done((f32[8,64,256]{2,1,0:T(8,128)S(1)}, f32[8,64,256]{2,1,0:T(8,128)}, u32[]{:S(2)}, u32[]{:S(2)}) %collective-permute-start.8) | collective-permute-done | bytes 524320 | tf_op jit(solution)/shard_map/ppermute | solution.py:150
  69.2 3.6 %all-gather.3.cloned.1.call-done = f32[128,64,256]{2,1,0:T(8,128)} async-done(((f32[8,64,256]{2,1,0:T(8,128)}), f32[128,64,256]{2,1,0:T(8,128)}) %all-gather.3.cloned.1.call-update) | async-done | bytes 8388624 | tf_op jit(solution)/shard_map/all_gather | solution.py:152
  72.8 11.6 %product_0.1.refs_0_ = f32[16,64,512]{2,1,0:T(8,128)} custom-call(f32[16,8,64,256]{3,2,1,0:T(8,128)} %bitcast.10, bf16[512,2048]{1,0:T(8,128)(2,1)S(1)} %get-tuple-element.20.a_hi, bf16[512,2048]{1,0:T(8,128)(2,1)} %get-tuple-element.21.a_lo_hbm), custom_call_target="tpu_custom_call" | custom-call | flops 60000002048 | bytes 60000000 | tf_op jit(solution)/shard_map/product_0/pallas_call | solution.py:190
  84.5 5.3 %all-to-all-start.1 = ((f32[16,64,512]{2,1,0:T(8,128)}), f32[16,64,512]{2,1,0:T(8,128)S(1)}, u32[]{:S(2)}, u32[]{:S(2)}) async-start(f32[16,64,512]{2,1,0:T(8,128)} %product_0.1.refs_0_), calls=%async_computation.1 | async-start | bytes 4194304 | tf_op jit(solution)/shard_map/all_to_all | solution.py:211
  89.8 2.8 %collective-permute-start.10 = (f32[8,64,256]{2,1,0:T(8,128)S(1)}, f32[8,64,256]{2,1,0:T(8,128)S(1)}, u32[]{:S(2)}, u32[]{:S(2)}) collective-permute-start(f32[8,64,256]{2,1,0:T(8,128)S(1)} %copy-done.5), channel_id=1, source_target_pairs={{0,48},{16,0},{32,16},{48,32},{1,49},{17,1},{33,17},{49,33},{2,50}... | collective-permute-start | bytes 1572872 | tf_op jit(solution)/shard_map/ppermute | solution.py:150
  93.8 1.5 collective-permute-start.13
  95.2 8.5 %collective-permute-done.10.refs_2_ = f32[8,64,256]{2,1,0:T(8,128)S(1)} collective-permute-done((f32[8,64,256]{2,1,0:T(8,128)S(1)}, f32[8,64,256]{2,1,0:T(8,128)S(1)}, u32[]{:S(2)}, u32[]{:S(2)}) %collective-permute-start.10) | collective-permute-done | bytes 524320 | tf_op jit(solution)/shard_map/ppermute | solution.py:150
  103.7 2.2 %collective-permute-start.15 = (f32[8,64,256]{2,1,0:T(8,128)}, f32[8,64,256]{2,1,0:T(8,128)S(1)}, u32[]{:S(2)}, u32[]{:S(2)}) collective-permute-start(f32[8,64,256]{2,1,0:T(8,128)} %collective-permute-done.8.refs_1_), channel_id=1, source_target_pairs={{0,32},{16,48},{32,0},{48,16},{1,33},{17,49},{33,1},{49,17},{2,34}... | collective-permute-start | bytes 1572872 | tf_op jit(solution)/shard_map/ppermute | solution.py:150
  107.0 22.4 %collective-permute-done.14.refs_6_ = f32[8,64,256]{2,1,0:T(8,128)S(1)} collective-permute-done((f32[8,64,256]{2,1,0:T(8,128)S(1)}, f32[8,64,256]{2,1,0:T(8,128)S(1)}, u32[]{:S(2)}, u32[]{:S(2)}) %collective-permute-start.14) | collective-permute-done | bytes 524320 | tf_op jit(solution)/shard_map/ppermute | solution.py:150
  131.1 3.6 %split_1.1 = (bf16[512,2048]{1,0:T(8,128)(2,1)S(1)}, bf16[512,2048]{1,0:T(8,128)(2,1)}) custom-call(f32[8,64,256]{2,1,0:T(8,128)} %collective-permute-done.7.refs_0_, f32[8,64,256]{2,1,0:T(8,128)} %collective-permute-done.8.refs_1_, f32[8,64,256]{2,1,0:T(8,128)} %copy-done.11, f32[8,64,256]{2,1,0:T(8,128)} %copy-done.14, f32[8,64,256]{2,1,0:T(8,128)} %copy-done.12, ...), custom_call_target="tpu_custom_call" | custom-call | flops 8000000000 | bytes 8000000 | tf_op jit(solution)/shard_map/split_1/pallas_call | solution.py:170
  134.7 11.6 %product_1.1.refs_3_ = f32[16,64,512]{2,1,0:T(8,128)} custom-call(f32[16,8,64,256]{3,2,1,0:T(8,128)} %bitcast.11, bf16[512,2048]{1,0:T(8,128)(2,1)S(1)} %get-tuple-element.26.a_hi, bf16[512,2048]{1,0:T(8,128)(2,1)} %get-tuple-element.27.a_lo_hbm), custom_call_target="tpu_custom_call" | custom-call | flops 8000000000 | bytes 8000000 | tf_op jit(solution)/shard_map/product_1/pallas_call | solution.py:190
  146.4 8.2 %all-to-all-start.2 = ((f32[16,64,512]{2,1,0:T(8,128)}), f32[16,64,512]{2,1,0:T(8,128)}, u32[]{:S(2)}, u32[]{:S(2)}) async-start(f32[16,64,512]{2,1,0:T(8,128)} %product_1.1.refs_3_), calls=%async_computation.2 | async-start | bytes 4194304 | tf_op jit(solution)/shard_map/all_to_all | solution.py:211
  155.3 3.7 %collective-permute-done.9.refs_1_ = f32[16,64,512]{2,1,0:T(8,128)} collective-permute-done((f32[16,64,512]{2,1,0:T(8,128)}, f32[16,64,512]{2,1,0:T(8,128)}, u32[]{:S(2)}, u32[]{:S(2)}) %collective-permute-start.9) | collective-permute-done | bytes 2097184 | tf_op jit(solution)/shard_map/ppermute | solution.py:210
  159.1 3.0 %collective-permute-done.16.refs_4_ = f32[16,64,512]{2,1,0:T(8,128)} collective-permute-done((f32[16,64,512]{2,1,0:T(8,128)}, f32[16,64,512]{2,1,0:T(8,128)}, u32[]{:S(2)}, u32[]{:S(2)}) %collective-permute-start.16) | collective-permute-done | bytes 2097184 | tf_op jit(solution)/shard_map/ppermute | solution.py:210
  162.1 40.7 %all-to-all-done.2.refs_5_ = f32[16,64,512]{2,1,0:T(8,128)} async-done(((f32[16,64,512]{2,1,0:T(8,128)}), f32[16,64,512]{2,1,0:T(8,128)}, u32[]{:S(2)}, u32[]{:S(2)}) %all-to-all-start.2) | async-done | bytes 2097184 | tf_op jit(solution)/shard_map/all_to_all | solution.py:211
  202.7 6.1 %finish.1 = f32[8,64,2048]{2,1,0:T(8,128)} custom-call(s32[4]{0:T(128)S(1)} %pad_add_fusion.places, s32[32]{0:T(128)S(1)} %copy-done.1, f32[8]{0:T(128)S(1)} %copy-done.2, f32[64,1]{1,0:T(8,128)S(1)} %copy.7.e_b, f32[1,2048]{1,0:T(1,128)S(1)} %bitcast.9, f32[16,64,512]{2,1,0:T(8,128)} %product_0.1.refs_0_, f32[16,64,512]{2,1,0:T(8,128)} %collective-permute-done.9.refs_1_, ...), custom_call_target="tpu_custom_call" | custom-call | tf_op jit(solution)/shard_map/finish/pallas_call | solution.py:224
  (62 shorter events, 11.0 us)
Async XLA Ops:
  6.5 66.3 %all-gather.3.cloned.1.call-start = ((), (), s32[]{:S(2)}) async-start(), calls=%async_computation.3 | async-start | bytes 8912896 | tf_op jit(solution)/shard_map/all_gather | solution.py:152
  33.4 24.6 %copy-start.3 = (f32[8,64,256]{2,1,0:T(8,128)}, f32[8,64,256]{2,1,0:T(8,128)S(1)}, u32[]{:S(2)}) copy-start(f32[8,64,256]{2,1,0:T(8,128)S(1)} %all_to_all.15.refs_0_) | copy-start | bytes 1572868
  33.4 10.3 %collective-permute-start.2 = (f32[8,64,256]{2,1,0:T(8,128)S(1)}, f32[8,64,256]{2,1,0:T(8,128)S(1)}, u32[]{:S(2)}, u32[]{:S(2)}) collective-permute-start(f32[8,64,256]{2,1,0:T(8,128)S(1)} %all_to_all.15.refs_0_), channel_id=1, source_target_pairs={{0,48},{16,0},{32,16},{48,32},{1,49},{17,1},{33,17},{49,33},{2,50}... | collective-permute-start | bytes 1572872 | tf_op jit(solution)/shard_map/ppermute | solution.py:150
  36.3 10.6 %collective-permute-start.3 = (f32[8,64,256]{2,1,0:T(8,128)S(1)}, f32[8,64,256]{2,1,0:T(8,128)S(1)}, u32[]{:S(2)}, u32[]{:S(2)}) collective-permute-start(f32[8,64,256]{2,1,0:T(8,128)S(1)} %all_to_all.15.refs_0_), channel_id=1, source_target_pairs={{0,16},{16,32},{32,48},{48,0},{1,17},{17,33},{33,49},{49,1},{2,18}... | collective-permute-start | bytes 1572872 | tf_op jit(solution)/shard_map/ppermute | solution.py:150
  36.3 11.9 %collective-permute-start.1 = (f32[8,64,256]{2,1,0:T(8,128)S(1)}, f32[8,64,256]{2,1,0:T(8,128)S(1)}, u32[]{:S(2)}, u32[]{:S(2)}) collective-permute-start(f32[8,64,256]{2,1,0:T(8,128)S(1)} %all_to_all.15.refs_0_), channel_id=1, source_target_pairs={{0,64},{64,128},{128,192},{192,0},{1,65},{65,129},{129,193},{193,1... | collective-permute-start | bytes 1572872 | tf_op jit(solution)/shard_map/ppermute | solution.py:150
  37.5 12.3 %collective-permute-start = (f32[8,64,256]{2,1,0:T(8,128)S(1)}, f32[8,64,256]{2,1,0:T(8,128)S(1)}, u32[]{:S(2)}, u32[]{:S(2)}) collective-permute-start(f32[8,64,256]{2,1,0:T(8,128)S(1)} %all_to_all.15.refs_0_), channel_id=1, source_target_pairs={{0,192},{64,0},{128,64},{192,128},{1,193},{65,1},{129,65},{193,129... | collective-permute-start | bytes 1572872 | tf_op jit(solution)/shard_map/ppermute | solution.py:150
  43.7 14.3 %collective-permute-start.4 = (f32[8,64,256]{2,1,0:T(8,128)S(1)}, f32[8,64,256]{2,1,0:T(8,128)S(1)}, u32[]{:S(2)}, u32[]{:S(2)}) collective-permute-start(f32[8,64,256]{2,1,0:T(8,128)S(1)} %collective-permute-done.2.refs_3_), channel_id=1, source_target_pairs={{0,192},{64,0},{128,64},{192,128},{1,193},{65,1},{129,65},{193,129... | collective-permute-start | bytes 1572872 | tf_op jit(solution)/shard_map/ppermute | solution.py:150
  46.9 11.1 %collective-permute-start.5 = (f32[8,64,256]{2,1,0:T(8,128)S(1)}, f32[8,64,256]{2,1,0:T(8,128)S(1)}, u32[]{:S(2)}, u32[]{:S(2)}) collective-permute-start(f32[8,64,256]{2,1,0:T(8,128)S(1)} %collective-permute-done.3.refs_4_), channel_id=1, source_target_pairs={{0,64},{64,128},{128,192},{192,0},{1,65},{65,129},{129,193},{193,1... | collective-permute-start | bytes 1572872 | tf_op jit(solution)/shard_map/ppermute | solution.py:150
  48.2 9.9 %collective-permute-start.6 = (f32[8,64,256]{2,1,0:T(8,128)S(1)}, f32[8,64,256]{2,1,0:T(8,128)}, u32[]{:S(2)}, u32[]{:S(2)}) collective-permute-start(f32[8,64,256]{2,1,0:T(8,128)S(1)} %collective-permute-done.1.refs_2_), channel_id=1, source_target_pairs={{0,48},{16,0},{32,16},{48,32},{1,49},{17,1},{33,17},{49,33},{2,50}... | collective-permute-start | bytes 1572872 | tf_op jit(solution)/shard_map/ppermute | solution.py:150
  49.8 12.8 %collective-permute-start.7 = (f32[8,64,256]{2,1,0:T(8,128)S(1)}, f32[8,64,256]{2,1,0:T(8,128)}, u32[]{:S(2)}, u32[]{:S(2)}) collective-permute-start(f32[8,64,256]{2,1,0:T(8,128)S(1)} %collective-permute-done.refs_1_), channel_id=1, source_target_pairs={{0,16},{16,32},{32,48},{48,0},{1,17},{17,33},{33,49},{49,1},{2,18}... | collective-permute-start | bytes 1572872 | tf_op jit(solution)/shard_map/ppermute | solution.py:150
  49.8 19.4 %collective-permute-start.8 = (f32[8,64,256]{2,1,0:T(8,128)S(1)}, f32[8,64,256]{2,1,0:T(8,128)}, u32[]{:S(2)}, u32[]{:S(2)}) collective-permute-start(f32[8,64,256]{2,1,0:T(8,128)S(1)} %collective-permute-done.refs_1_), channel_id=1, source_target_pairs={{0,192},{64,0},{128,64},{192,128},{1,193},{65,1},{129,65},{193,129... | collective-permute-start | bytes 1572872 | tf_op jit(solution)/shard_map/ppermute | solution.py:150
  84.5 61.9 %all-to-all-start.1 = ((f32[16,64,512]{2,1,0:T(8,128)}), f32[16,64,512]{2,1,0:T(8,128)S(1)}, u32[]{:S(2)}, u32[]{:S(2)}) async-start(f32[16,64,512]{2,1,0:T(8,128)} %product_0.1.refs_0_), calls=%async_computation.1 | async-start | bytes 4194304 | tf_op jit(solution)/shard_map/all_to_all | solution.py:211
  89.8 13.9 %collective-permute-start.10 = (f32[8,64,256]{2,1,0:T(8,128)S(1)}, f32[8,64,256]{2,1,0:T(8,128)S(1)}, u32[]{:S(2)}, u32[]{:S(2)}) collective-permute-start(f32[8,64,256]{2,1,0:T(8,128)S(1)} %copy-done.5), channel_id=1, source_target_pairs={{0,48},{16,0},{32,16},{48,32},{1,49},{17,1},{33,17},{49,33},{2,50}... | collective-permute-start | bytes 1572872 | tf_op jit(solution)/shard_map/ppermute | solution.py:150
  92.6 14.5 %collective-permute-start.12 = (f32[8,64,256]{2,1,0:T(8,128)}, f32[8,64,256]{2,1,0:T(8,128)S(1)}, u32[]{:S(2)}, u32[]{:S(2)}) collective-permute-start(f32[8,64,256]{2,1,0:T(8,128)} %collective-permute-done.7.refs_0_), channel_id=1, source_target_pairs={{0,16},{16,32},{32,48},{48,0},{1,17},{17,33},{33,49},{49,1},{2,18}... | collective-permute-start | bytes 1572872 | tf_op jit(solution)/shard_map/ppermute | solution.py:150
  92.6 14.5 %collective-permute-start.11 = (f32[8,64,256]{2,1,0:T(8,128)}, f32[8,64,256]{2,1,0:T(8,128)S(1)}, u32[]{:S(2)}, u32[]{:S(2)}) collective-permute-start(f32[8,64,256]{2,1,0:T(8,128)} %collective-permute-done.6.refs_7_), channel_id=1, source_target_pairs={{0,64},{64,128},{128,192},{192,0},{1,65},{65,129},{129,193},{193,1... | collective-permute-start | bytes 1572872 | tf_op jit(solution)/shard_map/ppermute | solution.py:150
  93.8 13.3 %collective-permute-start.13 = (f32[8,64,256]{2,1,0:T(8,128)}, f32[8,64,256]{2,1,0:T(8,128)S(1)}, u32[]{:S(2)}, u32[]{:S(2)}) collective-permute-start(f32[8,64,256]{2,1,0:T(8,128)} %collective-permute-done.7.refs_0_), channel_id=1, source_target_pairs={{0,192},{64,0},{128,64},{192,128},{1,193},{65,1},{129,65},{193,129... | collective-permute-start | bytes 1572872 | tf_op jit(solution)/shard_map/ppermute | solution.py:150
  95.2 34.2 %collective-permute-start.14 = (f32[8,64,256]{2,1,0:T(8,128)S(1)}, f32[8,64,256]{2,1,0:T(8,128)S(1)}, u32[]{:S(2)}, u32[]{:S(2)}) collective-permute-start(f32[8,64,256]{2,1,0:T(8,128)S(1)} %copy-done.7), channel_id=1, source_target_pairs={{0,16},{16,32},{32,48},{48,0},{1,17},{17,33},{33,49},{49,1},{2,18}... | collective-permute-start | bytes 1572872 | tf_op jit(solution)/shard_map/ppermute | solution.py:150
  103.7 25.8 %copy-start.11 = (f32[8,64,256]{2,1,0:T(8,128)}, f32[8,64,256]{2,1,0:T(8,128)S(1)}, u32[]{:S(2)}) copy-start(f32[8,64,256]{2,1,0:T(8,128)S(1)} %collective-permute-done.10.refs_2_) | copy-start | bytes 1572868
  103.7 25.8 %collective-permute-start.15 = (f32[8,64,256]{2,1,0:T(8,128)}, f32[8,64,256]{2,1,0:T(8,128)S(1)}, u32[]{:S(2)}, u32[]{:S(2)}) collective-permute-start(f32[8,64,256]{2,1,0:T(8,128)} %collective-permute-done.8.refs_1_), channel_id=1, source_target_pairs={{0,32},{16,48},{32,0},{48,16},{1,33},{17,49},{33,1},{49,17},{2,34}... | collective-permute-start | bytes 1572872 | tf_op jit(solution)/shard_map/ppermute | solution.py:150
  146.3 56.4 %copy-start.1 = (s32[32]{0:T(128)S(1)}, s32[32]{0:T(128)}, u32[]{:S(2)}) copy-start(s32[32]{0:T(128)} %panel_of.1) | copy-start | bytes 388
  146.4 56.4 %copy-start.2 = (f32[8]{0:T(128)S(1)}, f32[8]{0:T(128)}, u32[]{:S(2)}) copy-start(f32[8]{0:T(128)} %e_occ.1) | copy-start | bytes 100
  146.4 56.3 %all-to-all-start.2 = ((f32[16,64,512]{2,1,0:T(8,128)}), f32[16,64,512]{2,1,0:T(8,128)}, u32[]{:S(2)}, u32[]{:S(2)}) async-start(f32[16,64,512]{2,1,0:T(8,128)} %product_1.1.refs_3_), calls=%async_computation.2 | async-start | bytes 4194304 | tf_op jit(solution)/shard_map/all_to_all | solution.py:211
  154.6 4.5 %collective-permute-start.9 = (f32[16,64,512]{2,1,0:T(8,128)}, f32[16,64,512]{2,1,0:T(8,128)}, u32[]{:S(2)}, u32[]{:S(2)}) collective-permute-start(f32[16,64,512]{2,1,0:T(8,128)} %product_0.1.refs_0_), channel_id=1, source_target_pairs={{0,8},{8,0},{1,9},{9,1},{2,10},{10,2},{3,11},{11,3},{4,12},{12,4},... | collective-permute-start | bytes 6291464 | tf_op jit(solution)/shard_map/ppermute | solution.py:210
  154.8 7.3 %collective-permute-start.16 = (f32[16,64,512]{2,1,0:T(8,128)}, f32[16,64,512]{2,1,0:T(8,128)}, u32[]{:S(2)}, u32[]{:S(2)}) collective-permute-start(f32[16,64,512]{2,1,0:T(8,128)} %product_1.1.refs_3_), channel_id=1, source_target_pairs={{0,8},{8,0},{1,9},{9,1},{2,10},{10,2},{3,11},{11,3},{4,12},{12,4},... | collective-permute-start | bytes 6291464 | tf_op jit(solution)/shard_map/ppermute | solution.py:210
  (14 other events, 139.3 us)
Sparse Core Ops, SparseCore 0:
  9.2 63.5 all-gather.2

commit v7 on v6

--- a/solution.py
+++ b/solution.py
@@ -29,8 +29,9 @@
     ((0, 2), (0, 1)),
     ((2, 1), (-1, 0)),
     ((1, 2), (0, -1)),
+    ((2, -1), (1, 0)),
 ]
-LAST = [((2, -1), (1, 0)), ((-1, 2), (0, -1)), ((2, 2), (0, 2))]
+LAST = [((-1, 2), (0, -1)), ((2, 2), (0, 1))]
 SETS = [
     [(0, 0), (1, 0), (-1, 0), (0, 1), (0, -1), (1, 1), (-1, -1), (-1, 1)],
     [(1, -1), (2, 0), (0, 2), (2, 1), (1, 2), (2, -1), (-1, 2), (2, 2)],

time: 216 us -> 207 us (0.958)
  waiting for transfers between devices: 101 us -> 92.9 us
    ppermute x15, waiting for transfers between devices: 49.4 us -> 39.8 us  [move(): lax.ppermute(data, name, [(n, (n - step) % SIDE) for n in range(SIDE)])]
  transfers between devices with their start and end apart: 20 -> 20, of which waited for: 11 -> 13; matrix products, arithmetic and copies ran while one was open for 0% -> 0% of each run, Pallas kernels for 9% -> 9%
where the time goes in v7:
time: 207 us
  waiting for transfers between devices  92.9 us (45%)
  Pallas kernels  36.7 us (18%)
  starting transfers between devices  35.5 us (17%)
  blocking collectives  26.2 us (13%)
  between operations  13.6 us (7%)
    all_to_all x2, waiting for transfers between devices, body(): lax.all_to_all(sent, ('core', 'virt'), split_axis=0, concat_axis=0, tiled...  42 us
    ppermute x15, waiting for transfers between devices, move(): lax.ppermute(data, name, [(n, (n - step) % SIDE) for n in range(SIDE)])  39.8 us
    all_to_all x1, blocking collectives, body(): lax.all_to_all(amps, 'virt', split_axis=0, concat_axis=0, tiled=True)  26.2 us
    pallas_call x2, Pallas kernels, body(): pl.pallas_call(functools.partial(product_kernel, (occ, panel, width)), ou...  23.3 us
    ppermute x15, starting transfers between devices, move(): lax.ppermute(data, name, [(n, (n - step) % SIDE) for n in range(SIDE)])  21.9 us
    all_to_all x2, starting transfers between devices, body(): lax.all_to_all(sent, ('core', 'virt'), split_axis=0, concat_axis=0, tiled...  13 us
    pallas_call x2, Pallas kernels, body(): pl.pallas_call(functools.partial(split_kernel, (panel, width, len(chips))...  7.28 us
    ppermute x2, waiting for transfers between devices, body(): swapped = lax.ppermute(whole, 'core', [(0, 1), (1, 0)])  6.74 us
  transfers between devices with their start and end apart: 20, of which 13 were waited for; matrix products, arithmetic and copies ran while one was open for 0% of the time, Pallas kernels for 9%

profile of v7, /device:TPU:1, one launch (start us, length us, event | category | flops | bytes accessed | tf_op | source)
XLA Modules:
  0.0 206.8 jit_solution(4110508351344193747)
XLA Ops:
  7.3 26.2 %all_to_all.15.refs_0_ = f32[8,64,256]{2,1,0:T(8,128)S(1)} all-to-all(f32[8,64,256]{2,1,0:T(8,128)} %param.5), channel_id=1, replica_groups=mesh['x'=4,'y'=4,'core'=2,'virt'=8] {'virt'}, dimensions={0} | all-to-all | bytes 1048576 | tf_op jit(solution)/shard_map/all_to_all | solution.py:154
  33.4 2.9 %collective-permute-start.2 = (f32[8,64,256]{2,1,0:T(8,128)S(1)}, f32[8,64,256]{2,1,0:T(8,128)S(1)}, u32[]{:S(2)}, u32[]{:S(2)}) collective-permute-start(f32[8,64,256]{2,1,0:T(8,128)S(1)} %all_to_all.15.refs_0_), channel_id=1, source_target_pairs={{0,48},{16,0},{32,16},{48,32},{1,49},{17,1},{33,17},{49,33},{2,50}... | collective-permute-start | bytes 1572872 | tf_op jit(solution)/shard_map/ppermute | solution.py:151
  39.0 4.7 %collective-permute-done.2.refs_3_ = f32[8,64,256]{2,1,0:T(8,128)S(1)} collective-permute-done((f32[8,64,256]{2,1,0:T(8,128)S(1)}, f32[8,64,256]{2,1,0:T(8,128)S(1)}, u32[]{:S(2)}, u32[]{:S(2)}) %collective-permute-start.2) | collective-permute-done | bytes 524320 | tf_op jit(solution)/shard_map/ppermute | solution.py:151
  43.7 2.5 %collective-permute-start.4 = (f32[8,64,256]{2,1,0:T(8,128)S(1)}, f32[8,64,256]{2,1,0:T(8,128)S(1)}, u32[]{:S(2)}, u32[]{:S(2)}) collective-permute-start(f32[8,64,256]{2,1,0:T(8,128)S(1)} %collective-permute-done.2.refs_3_), channel_id=1, source_target_pairs={{0,192},{64,0},{128,64},{192,128},{1,193},{65,1},{129,65},{193,129... | collective-permute-start | bytes 1572872 | tf_op jit(solution)/shard_map/ppermute | solution.py:151
  48.2 1.7 collective-permute-start.6
  49.8 2.8 %collective-permute-start.8 = (f32[8,64,256]{2,1,0:T(8,128)S(1)}, f32[8,64,256]{2,1,0:T(8,128)}, u32[]{:S(2)}, u32[]{:S(2)}) collective-permute-start(f32[8,64,256]{2,1,0:T(8,128)S(1)} %collective-permute-done.refs_1_), channel_id=1, source_target_pairs={{0,192},{64,0},{128,64},{192,128},{1,193},{65,1},{129,65},{193,129... | collective-permute-start | bytes 1572872 | tf_op jit(solution)/shard_map/ppermute | solution.py:151
  52.7 5.3 %collective-permute-done.4.refs_5_ = f32[8,64,256]{2,1,0:T(8,128)S(1)} collective-permute-done((f32[8,64,256]{2,1,0:T(8,128)S(1)}, f32[8,64,256]{2,1,0:T(8,128)S(1)}, u32[]{:S(2)}, u32[]{:S(2)}) %collective-permute-start.4) | collective-permute-done | bytes 524320 | tf_op jit(solution)/shard_map/ppermute | solution.py:151
  59.0 3.7 %split_0.1 = (bf16[512,2048]{1,0:T(8,128)(2,1)S(1)}, bf16[512,2048]{1,0:T(8,128)(2,1)}) custom-call(f32[8,64,256]{2,1,0:T(8,128)} %copy-done.3, f32[8,64,256]{2,1,0:T(8,128)} %copy-done.9, f32[8,64,256]{2,1,0:T(8,128)} %copy-done.10, f32[8,64,256]{2,1,0:T(8,128)} %copy-done.4, f32[8,64,256]{2,1,0:T(8,128)} %copy-done.8, f32[8,64,256]{2,1,0:T(8,128)} %copy-done.13, ...), custom_call_target="tpu_custom_call" | custom-call | flops 60000002048 | bytes 60000000 | tf_op jit(solution)/shard_map/split_0/pallas_call | solution.py:171
  62.7 6.6 %collective-permute-done.8.refs_1_ = f32[8,64,256]{2,1,0:T(8,128)} collective-permute-done((f32[8,64,256]{2,1,0:T(8,128)S(1)}, f32[8,64,256]{2,1,0:T(8,128)}, u32[]{:S(2)}, u32[]{:S(2)}) %collective-permute-start.8) | collective-permute-done | bytes 524320 | tf_op jit(solution)/shard_map/ppermute | solution.py:151
  69.2 3.6 %all-gather.3.cloned.1.call-done = f32[128,64,256]{2,1,0:T(8,128)} async-done(((f32[8,64,256]{2,1,0:T(8,128)}), f32[128,64,256]{2,1,0:T(8,128)}) %all-gather.3.cloned.1.call-update) | async-done | bytes 8388624 | tf_op jit(solution)/shard_map/all_gather | solution.py:153
  72.8 11.6 %product_0.1.refs_0_ = f32[16,64,512]{2,1,0:T(8,128)} custom-call(f32[16,8,64,256]{3,2,1,0:T(8,128)} %bitcast.10, bf16[512,2048]{1,0:T(8,128)(2,1)S(1)} %get-tuple-element.19.a_hi, bf16[512,2048]{1,0:T(8,128)(2,1)} %get-tuple-element.20.a_lo_hbm), custom_call_target="tpu_custom_call" | custom-call | flops 60000002048 | bytes 60000000 | tf_op jit(solution)/shard_map/product_0/pallas_call | solution.py:191
  84.5 5.3 %all-to-all-start.1 = ((f32[16,64,512]{2,1,0:T(8,128)}), f32[16,64,512]{2,1,0:T(8,128)S(1)}, u32[]{:S(2)}, u32[]{:S(2)}) async-start(f32[16,64,512]{2,1,0:T(8,128)} %product_0.1.refs_0_), calls=%async_computation.1 | async-start | bytes 4194304 | tf_op jit(solution)/shard_map/all_to_all | solution.py:212
  91.0 2.7 %collective-permute-start.10 = (f32[8,64,256]{2,1,0:T(8,128)S(1)}, f32[8,64,256]{2,1,0:T(8,128)S(1)}, u32[]{:S(2)}, u32[]{:S(2)}) collective-permute-start(f32[8,64,256]{2,1,0:T(8,128)S(1)} %copy-done.5), channel_id=1, source_target_pairs={{0,48},{16,0},{32,16},{48,32},{1,49},{17,1},{33,17},{49,33},{2,50}... | collective-permute-start | bytes 1572872 | tf_op jit(solution)/shard_map/ppermute | solution.py:151
  95.2 9.3 %collective-permute-done.11.refs_3_ = f32[8,64,256]{2,1,0:T(8,128)S(1)} collective-permute-done((f32[8,64,256]{2,1,0:T(8,128)}, f32[8,64,256]{2,1,0:T(8,128)S(1)}, u32[]{:S(2)}, u32[]{:S(2)}) %collective-permute-start.11) | collective-permute-done | bytes 524320 | tf_op jit(solution)/shard_map/ppermute | solution.py:151
  104.5 2.7 %collective-permute-start.15 = (f32[8,64,256]{2,1,0:T(8,128)S(1)}, f32[8,64,256]{2,1,0:T(8,128)S(1)}, u32[]{:S(2)}, u32[]{:S(2)}) collective-permute-start(f32[8,64,256]{2,1,0:T(8,128)S(1)} %collective-permute-done.11.refs_3_), channel_id=1, source_target_pairs={{0,48},{16,0},{32,16},{48,32},{1,49},{17,1},{33,17},{49,33},{2,50}... | collective-permute-start | bytes 1572872 | tf_op jit(solution)/shard_map/ppermute | solution.py:151
  107.8 9.6 %collective-permute-done.15.refs_7_ = f32[8,64,256]{2,1,0:T(8,128)S(1)} collective-permute-done((f32[8,64,256]{2,1,0:T(8,128)S(1)}, f32[8,64,256]{2,1,0:T(8,128)S(1)}, u32[]{:S(2)}, u32[]{:S(2)}) %collective-permute-start.15) | collective-permute-done | bytes 524320 | tf_op jit(solution)/shard_map/ppermute | solution.py:151
  117.3 3.1 %collective-permute-done.14.refs_6_ = f32[8,64,256]{2,1,0:T(8,128)S(1)} collective-permute-done((f32[8,64,256]{2,1,0:T(8,128)S(1)}, f32[8,64,256]{2,1,0:T(8,128)S(1)}, u32[]{:S(2)}, u32[]{:S(2)}) %collective-permute-start.14) | collective-permute-done | bytes 524320 | tf_op jit(solution)/shard_map/ppermute | solution.py:151
  121.3 3.6 %split_1.1 = (bf16[512,2048]{1,0:T(8,128)(2,1)S(1)}, bf16[512,2048]{1,0:T(8,128)(2,1)}) custom-call(f32[8,64,256]{2,1,0:T(8,128)} %collective-permute-done.7.refs_0_, f32[8,64,256]{2,1,0:T(8,128)} %collective-permute-done.8.refs_1_, f32[8,64,256]{2,1,0:T(8,128)} %copy-done.12, f32[8,64,256]{2,1,0:T(8,128)} %copy-done.11, f32[8,64,256]{2,1,0:T(8,128)} %copy-done.14, ...), custom_call_target="tpu_custom_call" | custom-call | flops 8000000000 | bytes 8000000 | tf_op jit(solution)/shard_map/split_1/pallas_call | solution.py:171
  124.9 11.7 %product_1.1.refs_3_ = f32[16,64,512]{2,1,0:T(8,128)} custom-call(f32[16,8,64,256]{3,2,1,0:T(8,128)} %bitcast.11, bf16[512,2048]{1,0:T(8,128)(2,1)S(1)} %get-tuple-element.24.a_hi, bf16[512,2048]{1,0:T(8,128)(2,1)} %get-tuple-element.25.a_lo_hbm), custom_call_target="tpu_custom_call" | custom-call | flops 8000000000 | bytes 8000000 | tf_op jit(solution)/shard_map/product_1/pallas_call | solution.py:191
  137.9 7.7 %all-to-all-start.2 = ((f32[16,64,512]{2,1,0:T(8,128)}), f32[16,64,512]{2,1,0:T(8,128)}, u32[]{:S(2)}, u32[]{:S(2)}) async-start(f32[16,64,512]{2,1,0:T(8,128)} %product_1.1.refs_3_), calls=%async_computation.2 | async-start | bytes 4194304 | tf_op jit(solution)/shard_map/all_to_all | solution.py:212
  146.4 3.7 %collective-permute-done.9.refs_1_ = f32[16,64,512]{2,1,0:T(8,128)} collective-permute-done((f32[16,64,512]{2,1,0:T(8,128)}, f32[16,64,512]{2,1,0:T(8,128)}, u32[]{:S(2)}, u32[]{:S(2)}) %collective-permute-start.9) | collective-permute-done | bytes 2097184 | tf_op jit(solution)/shard_map/ppermute | solution.py:211
  150.1 3.0 %collective-permute-done.16.refs_4_ = f32[16,64,512]{2,1,0:T(8,128)} collective-permute-done((f32[16,64,512]{2,1,0:T(8,128)}, f32[16,64,512]{2,1,0:T(8,128)}, u32[]{:S(2)}, u32[]{:S(2)}) %collective-permute-start.16) | collective-permute-done | bytes 2097184 | tf_op jit(solution)/shard_map/ppermute | solution.py:211
  153.1 40.7 %all-to-all-done.2.refs_5_ = f32[16,64,512]{2,1,0:T(8,128)} async-done(((f32[16,64,512]{2,1,0:T(8,128)}), f32[16,64,512]{2,1,0:T(8,128)}, u32[]{:S(2)}, u32[]{:S(2)}) %all-to-all-start.2) | async-done | bytes 2097184 | tf_op jit(solution)/shard_map/all_to_all | solution.py:212
  193.8 6.1 %finish.1 = f32[8,64,2048]{2,1,0:T(8,128)} custom-call(s32[4]{0:T(128)S(1)} %pad_add_fusion.places, s32[32]{0:T(128)S(1)} %copy-done.1, f32[8]{0:T(128)S(1)} %copy-done.2, f32[64,1]{1,0:T(8,128)S(1)} %copy.7.e_b, f32[1,2048]{1,0:T(1,128)S(1)} %bitcast.9, f32[16,64,512]{2,1,0:T(8,128)} %product_0.1.refs_0_, f32[16,64,512]{2,1,0:T(8,128)} %collective-permute-done.9.refs_1_, ...), custom_call_target="tpu_custom_call" | custom-call | tf_op jit(solution)/shard_map/finish/pallas_call | solution.py:225
  (62 shorter events, 12.5 us)
Async XLA Ops:
  6.5 66.3 %all-gather.3.cloned.1.call-start = ((), (), s32[]{:S(2)}) async-start(), calls=%async_computation.3 | async-start | bytes 8912896 | tf_op jit(solution)/shard_map/all_gather | solution.py:153
  33.4 24.6 %copy-start.3 = (f32[8,64,256]{2,1,0:T(8,128)}, f32[8,64,256]{2,1,0:T(8,128)S(1)}, u32[]{:S(2)}) copy-start(f32[8,64,256]{2,1,0:T(8,128)S(1)} %all_to_all.15.refs_0_) | copy-start | bytes 1572868
  33.4 10.3 %collective-permute-start.2 = (f32[8,64,256]{2,1,0:T(8,128)S(1)}, f32[8,64,256]{2,1,0:T(8,128)S(1)}, u32[]{:S(2)}, u32[]{:S(2)}) collective-permute-start(f32[8,64,256]{2,1,0:T(8,128)S(1)} %all_to_all.15.refs_0_), channel_id=1, source_target_pairs={{0,48},{16,0},{32,16},{48,32},{1,49},{17,1},{33,17},{49,33},{2,50}... | collective-permute-start | bytes 1572872 | tf_op jit(solution)/shard_map/ppermute | solution.py:151
  36.3 10.6 %collective-permute-start.3 = (f32[8,64,256]{2,1,0:T(8,128)S(1)}, f32[8,64,256]{2,1,0:T(8,128)S(1)}, u32[]{:S(2)}, u32[]{:S(2)}) collective-permute-start(f32[8,64,256]{2,1,0:T(8,128)S(1)} %all_to_all.15.refs_0_), channel_id=1, source_target_pairs={{0,16},{16,32},{32,48},{48,0},{1,17},{17,33},{33,49},{49,1},{2,18}... | collective-permute-start | bytes 1572872 | tf_op jit(solution)/shard_map/ppermute | solution.py:151
  36.3 11.9 %collective-permute-start.1 = (f32[8,64,256]{2,1,0:T(8,128)S(1)}, f32[8,64,256]{2,1,0:T(8,128)S(1)}, u32[]{:S(2)}, u32[]{:S(2)}) collective-permute-start(f32[8,64,256]{2,1,0:T(8,128)S(1)} %all_to_all.15.refs_0_), channel_id=1, source_target_pairs={{0,64},{64,128},{128,192},{192,0},{1,65},{65,129},{129,193},{193,1... | collective-permute-start | bytes 1572872 | tf_op jit(solution)/shard_map/ppermute | solution.py:151
  37.5 12.3 %collective-permute-start = (f32[8,64,256]{2,1,0:T(8,128)S(1)}, f32[8,64,256]{2,1,0:T(8,128)S(1)}, u32[]{:S(2)}, u32[]{:S(2)}) collective-permute-start(f32[8,64,256]{2,1,0:T(8,128)S(1)} %all_to_all.15.refs_0_), channel_id=1, source_target_pairs={{0,192},{64,0},{128,64},{192,128},{1,193},{65,1},{129,65},{193,129... | collective-permute-start | bytes 1572872 | tf_op jit(solution)/shard_map/ppermute | solution.py:151
  43.7 14.3 %collective-permute-start.4 = (f32[8,64,256]{2,1,0:T(8,128)S(1)}, f32[8,64,256]{2,1,0:T(8,128)S(1)}, u32[]{:S(2)}, u32[]{:S(2)}) collective-permute-start(f32[8,64,256]{2,1,0:T(8,128)S(1)} %collective-permute-done.2.refs_3_), channel_id=1, source_target_pairs={{0,192},{64,0},{128,64},{192,128},{1,193},{65,1},{129,65},{193,129... | collective-permute-start | bytes 1572872 | tf_op jit(solution)/shard_map/ppermute | solution.py:151
  46.9 11.1 %collective-permute-start.5 = (f32[8,64,256]{2,1,0:T(8,128)S(1)}, f32[8,64,256]{2,1,0:T(8,128)S(1)}, u32[]{:S(2)}, u32[]{:S(2)}) collective-permute-start(f32[8,64,256]{2,1,0:T(8,128)S(1)} %collective-permute-done.3.refs_4_), channel_id=1, source_target_pairs={{0,64},{64,128},{128,192},{192,0},{1,65},{65,129},{129,193},{193,1... | collective-permute-start | bytes 1572872 | tf_op jit(solution)/shard_map/ppermute | solution.py:151
  48.2 9.9 %collective-permute-start.6 = (f32[8,64,256]{2,1,0:T(8,128)S(1)}, f32[8,64,256]{2,1,0:T(8,128)}, u32[]{:S(2)}, u32[]{:S(2)}) collective-permute-start(f32[8,64,256]{2,1,0:T(8,128)S(1)} %collective-permute-done.1.refs_2_), channel_id=1, source_target_pairs={{0,48},{16,0},{32,16},{48,32},{1,49},{17,1},{33,17},{49,33},{2,50}... | collective-permute-start | bytes 1572872 | tf_op jit(solution)/shard_map/ppermute | solution.py:151
  49.8 12.8 %collective-permute-start.7 = (f32[8,64,256]{2,1,0:T(8,128)S(1)}, f32[8,64,256]{2,1,0:T(8,128)}, u32[]{:S(2)}, u32[]{:S(2)}) collective-permute-start(f32[8,64,256]{2,1,0:T(8,128)S(1)} %collective-permute-done.refs_1_), channel_id=1, source_target_pairs={{0,16},{16,32},{32,48},{48,0},{1,17},{17,33},{33,49},{49,1},{2,18}... | collective-permute-start | bytes 1572872 | tf_op jit(solution)/shard_map/ppermute | solution.py:151
  49.8 19.4 %collective-permute-start.8 = (f32[8,64,256]{2,1,0:T(8,128)S(1)}, f32[8,64,256]{2,1,0:T(8,128)}, u32[]{:S(2)}, u32[]{:S(2)}) collective-permute-start(f32[8,64,256]{2,1,0:T(8,128)S(1)} %collective-permute-done.refs_1_), channel_id=1, source_target_pairs={{0,192},{64,0},{128,64},{192,128},{1,193},{65,1},{129,65},{193,129... | collective-permute-start | bytes 1572872 | tf_op jit(solution)/shard_map/ppermute | solution.py:151
  84.5 22.7 %copy-start.7 = (f32[8,64,256]{2,1,0:T(8,128)S(1)}, f32[8,64,256]{2,1,0:T(8,128)}, u32[]{:S(2)}) copy-start(f32[8,64,256]{2,1,0:T(8,128)} %copy-done.6) | copy-start | bytes 1572868
  84.5 53.4 %all-to-all-start.1 = ((f32[16,64,512]{2,1,0:T(8,128)}), f32[16,64,512]{2,1,0:T(8,128)S(1)}, u32[]{:S(2)}, u32[]{:S(2)}) async-start(f32[16,64,512]{2,1,0:T(8,128)} %product_0.1.refs_0_), calls=%async_computation.1 | async-start | bytes 4194304 | tf_op jit(solution)/shard_map/all_to_all | solution.py:212
  89.8 14.7 %collective-permute-start.11 = (f32[8,64,256]{2,1,0:T(8,128)}, f32[8,64,256]{2,1,0:T(8,128)S(1)}, u32[]{:S(2)}, u32[]{:S(2)}) collective-permute-start(f32[8,64,256]{2,1,0:T(8,128)} %collective-permute-done.6.refs_7_), channel_id=1, source_target_pairs={{0,64},{64,128},{128,192},{192,0},{1,65},{65,129},{129,193},{193,1... | collective-permute-start | bytes 1572872 | tf_op jit(solution)/shard_map/ppermute | solution.py:151
  91.0 16.2 %collective-permute-start.10 = (f32[8,64,256]{2,1,0:T(8,128)S(1)}, f32[8,64,256]{2,1,0:T(8,128)S(1)}, u32[]{:S(2)}, u32[]{:S(2)}) collective-permute-start(f32[8,64,256]{2,1,0:T(8,128)S(1)} %copy-done.5), channel_id=1, source_target_pairs={{0,48},{16,0},{32,16},{48,32},{1,49},{17,1},{33,17},{49,33},{2,50}... | collective-permute-start | bytes 1572872 | tf_op jit(solution)/shard_map/ppermute | solution.py:151
  93.7 14.1 %collective-permute-start.12 = (f32[8,64,256]{2,1,0:T(8,128)}, f32[8,64,256]{2,1,0:T(8,128)S(1)}, u32[]{:S(2)}, u32[]{:S(2)}) collective-permute-start(f32[8,64,256]{2,1,0:T(8,128)} %collective-permute-done.7.refs_0_), channel_id=1, source_target_pairs={{0,16},{16,32},{32,48},{48,0},{1,17},{17,33},{33,49},{49,1},{2,18}... | collective-permute-start | bytes 1572872 | tf_op jit(solution)/shard_map/ppermute | solution.py:151
  93.7 14.1 %collective-permute-start.13 = (f32[8,64,256]{2,1,0:T(8,128)}, f32[8,64,256]{2,1,0:T(8,128)S(1)}, u32[]{:S(2)}, u32[]{:S(2)}) collective-permute-start(f32[8,64,256]{2,1,0:T(8,128)} %collective-permute-done.7.refs_0_), channel_id=1, source_target_pairs={{0,192},{64,0},{128,64},{192,128},{1,193},{65,1},{129,65},{193,129... | collective-permute-start | bytes 1572872 | tf_op jit(solution)/shard_map/ppermute | solution.py:151
  104.5 12.8 %collective-permute-start.15 = (f32[8,64,256]{2,1,0:T(8,128)S(1)}, f32[8,64,256]{2,1,0:T(8,128)S(1)}, u32[]{:S(2)}, u32[]{:S(2)}) collective-permute-start(f32[8,64,256]{2,1,0:T(8,128)S(1)} %collective-permute-done.11.refs_3_), channel_id=1, source_target_pairs={{0,48},{16,0},{32,16},{48,32},{1,49},{17,1},{33,17},{49,33},{2,50}... | collective-permute-start | bytes 1572872 | tf_op jit(solution)/shard_map/ppermute | solution.py:151
  107.2 13.3 %collective-permute-start.14 = (f32[8,64,256]{2,1,0:T(8,128)S(1)}, f32[8,64,256]{2,1,0:T(8,128)S(1)}, u32[]{:S(2)}, u32[]{:S(2)}) collective-permute-start(f32[8,64,256]{2,1,0:T(8,128)S(1)} %copy-done.7), channel_id=1, source_target_pairs={{0,16},{16,32},{32,48},{48,0},{1,17},{17,33},{33,49},{49,1},{2,18}... | collective-permute-start | bytes 1572872 | tf_op jit(solution)/shard_map/ppermute | solution.py:151
  136.6 57.2 %copy-start.1 = (s32[32]{0:T(128)S(1)}, s32[32]{0:T(128)}, u32[]{:S(2)}) copy-start(s32[32]{0:T(128)} %panel_of.1) | copy-start | bytes 388
  136.6 57.2 %copy-start.2 = (f32[8]{0:T(128)S(1)}, f32[8]{0:T(128)}, u32[]{:S(2)}) copy-start(f32[8]{0:T(128)} %e_occ.1) | copy-start | bytes 100
  137.9 55.9 %all-to-all-start.2 = ((f32[16,64,512]{2,1,0:T(8,128)}), f32[16,64,512]{2,1,0:T(8,128)}, u32[]{:S(2)}, u32[]{:S(2)}) async-start(f32[16,64,512]{2,1,0:T(8,128)} %product_1.1.refs_3_), calls=%async_computation.2 | async-start | bytes 4194304 | tf_op jit(solution)/shard_map/all_to_all | solution.py:212
  145.6 4.5 %collective-permute-start.9 = (f32[16,64,512]{2,1,0:T(8,128)}, f32[16,64,512]{2,1,0:T(8,128)}, u32[]{:S(2)}, u32[]{:S(2)}) collective-permute-start(f32[16,64,512]{2,1,0:T(8,128)} %product_0.1.refs_0_), channel_id=1, source_target_pairs={{0,8},{8,0},{1,9},{9,1},{2,10},{10,2},{3,11},{11,3},{4,12},{12,4},... | collective-permute-start | bytes 6291464 | tf_op jit(solution)/shard_map/ppermute | solution.py:211
  145.9 7.3 %collective-permute-start.16 = (f32[16,64,512]{2,1,0:T(8,128)}, f32[16,64,512]{2,1,0:T(8,128)}, u32[]{:S(2)}, u32[]{:S(2)}) collective-permute-start(f32[16,64,512]{2,1,0:T(8,128)} %product_1.1.refs_3_), channel_id=1, source_target_pairs={{0,8},{8,0},{1,9},{9,1},{2,10},{10,2},{3,11},{11,3},{4,12},{12,4},... | collective-permute-start | bytes 6291464 | tf_op jit(solution)/shard_map/ppermute | solution.py:211
  (14 other events, 120.2 us)
Sparse Core Ops, SparseCore 0:
  9.2 63.5 all-gather.2
